TPU v7x, 32 devices: a whole 2x2x4 slice. The times are simulated.
32 devices in a mesh: feat: 4 (over x, core), batch: 8 (over z, y).
Axes of the slice: x: 2, y: 2, z: 4, core: 2. Of those that a mesh axis runs over, the one named last changes fastest.
Arguments:
- node_feats: bfloat16 [32768, 1024], P('batch', 'feat'), may hold values from -96 to 96
- seed_ids: int32 [2048], P('batch'), may hold values from 0 to 4095
- first_hop: int32 [2048, 10], P('batch'), may hold values from 0 to 4095
- second_hop: int32 [2048, 10, 15], P('batch'), may hold values from 0 to 4095
- lower_self: bfloat16 [1024, 256], P('feat'), may hold values from -0.1875 to 0.1875
- lower_neighbour: bfloat16 [1024, 256], P('feat'), may hold values from -0.1875 to 0.1875
- norm_gain: float32 [256], replicated, may hold values from 0.1 to 1.9
- norm_shift: float32 [256], replicated, may hold values from -3 to 3
- upper_self: bfloat16 [256, 256], replicated, may hold values from -0.375 to 0.375
- upper_neighbour: bfloat16 [256, 256], replicated, may hold values from -0.375 to 0.375
- embed_grad: bfloat16 [2048, 256], P(('batch', 'feat')), may hold values from -0.125 to 0.125
Outputs:
- embedding: bfloat16 [2048, 256], P(('batch', 'feat'))
- grad_lower_self: float32 [1024, 256], P('feat')
- grad_lower_neighbour: float32 [1024, 256], P('feat')
- grad_upper_self: float32 [256, 256], replicated
- grad_upper_neighbour: float32 [256, 256], replicated
- grad_gain: float32 [256], replicated
- grad_shift: float32 [256], replicated
All inputs are finite; a program needn't handle non-finite values.
Results may differ from a plain program's by a relative error of at most 0.007.
Values may be sent and summed in bfloat16 or wider, within the bound.
No kernel may reach another device: no remote copies, remote signals or barrier semaphores. Data moves between devices by JAX's collectives and lax.ppermute only.
A program may use at most 64 MiB of HBM per device.

v0:
```python
import math

import jax
import jax.numpy as jnp
from jax import lax
from jax.sharding import PartitionSpec as P


def cross_rows(left, right):
    return lax.dot_general(
        left, right, (((0,), (0,)), ((), ())), preferred_element_type=jnp.float32
    )


def collect_rows(node_feats, seed_ids, first_hop, second_hop):
    table_rows = node_feats.shape[0]
    width = node_feats.shape[1]
    seed_total = seed_ids.shape[0]
    fan_one = first_hop.shape[1]
    fan_two = second_hop.shape[2]
    block = math.gcd(seed_total, 32)
    steps_count = seed_total // block
    positions = jnp.arange(table_rows, dtype=jnp.int32)

    def one_block(items):
        seeds_part, near_part, far_part = items
        self_ids = jnp.concatenate([seeds_part[:, None], near_part], axis=1)
        picker = (self_ids[:, :, None] == positions).astype(jnp.bfloat16).reshape(-1, table_rows)
        self_block = jnp.dot(picker, node_feats, preferred_element_type=jnp.float32).astype(
            jnp.bfloat16
        )
        near_counts = jnp.sum(
            (near_part[:, :, None] == positions).astype(jnp.float32), axis=1
        ).astype(jnp.bfloat16)
        far_counts = jnp.sum(
            (far_part[:, :, :, None] == positions).astype(jnp.float32), axis=2
        ).astype(jnp.bfloat16)
        near_mean = (
            jnp.dot(near_counts, node_feats, preferred_element_type=jnp.float32) / fan_one
        ).astype(jnp.bfloat16)
        far_mean = (
            jnp.dot(
                far_counts.reshape(-1, table_rows), node_feats, preferred_element_type=jnp.float32
            )
            / fan_two
        ).astype(jnp.bfloat16)
        neigh_block = jnp.concatenate(
            [near_mean[:, None, :], far_mean.reshape(block, fan_one, width)], axis=1
        ).reshape(-1, width)
        return (self_block, neigh_block)

    self_x, neigh_x = lax.map(
        one_block,
        (
            seed_ids.reshape(steps_count, block),
            first_hop.reshape(steps_count, block, fan_one),
            second_hop.reshape(steps_count, block, fan_one, fan_two),
        ),
    )
    return (self_x.reshape(-1, width), neigh_x.reshape(-1, width))


def on_device(
    node_feats,
    seed_ids,
    first_hop,
    second_hop,
    lower_self,
    lower_neighbour,
    norm_gain,
    norm_shift,
    upper_self,
    upper_neighbour,
    embed_grad,
):
    fan_one = first_hop.shape[1]
    slots = fan_one + 1
    hidden_width = lower_self.shape[1]
    seed_count = embed_grad.shape[0]
    own_count = seed_count * slots
    row_total = own_count * lax.axis_size("feat") * lax.axis_size("batch")
    self_x, neigh_x = collect_rows(node_feats, seed_ids, first_hop, second_hop)
    self_block = self_x
    neigh_block = neigh_x
    pre_act = lax.psum_scatter(
        jnp.dot(self_block, lower_self, preferred_element_type=jnp.float32)
        + jnp.dot(neigh_block, lower_neighbour, preferred_element_type=jnp.float32),
        "feat",
        scatter_dimension=0,
        tiled=True,
    )
    row_mean = lax.psum(jnp.sum(pre_act, axis=0), ("feat", "batch")) / row_total
    centred = pre_act - row_mean
    spread = lax.psum(jnp.sum(centred * centred, axis=0), ("feat", "batch")) / row_total
    inv_std = lax.rsqrt(spread + 1e-05)
    normed = centred * inv_std
    shifted = norm_gain * normed + norm_shift
    hidden = jax.nn.silu(shifted).astype(jnp.bfloat16)
    hidden_slots = hidden.reshape(seed_count, slots, hidden_width)
    own_rows = hidden_slots[:, 0, :]
    hidden_mean = (jnp.sum(hidden_slots[:, 1:, :], axis=1, dtype=jnp.float32) / fan_one).astype(
        jnp.bfloat16
    )
    embedding = (
        jnp.dot(own_rows, upper_self, preferred_element_type=jnp.float32)
        + jnp.dot(hidden_mean, upper_neighbour, preferred_element_type=jnp.float32)
    ).astype(jnp.bfloat16)
    upper_self_part = cross_rows(own_rows, embed_grad)
    upper_neigh_part = cross_rows(hidden_mean, embed_grad)
    d_self = lax.dot_general(
        embed_grad, upper_self, (((1,), (1,)), ((), ())), preferred_element_type=jnp.float32
    )
    d_mean = (
        lax.dot_general(
            embed_grad,
            upper_neighbour,
            (((1,), (1,)), ((), ())),
            preferred_element_type=jnp.float32,
        )
        / fan_one
    )
    grad_hidden = jnp.concatenate(
        [
            d_self[:, None, :],
            jnp.broadcast_to(d_mean[:, None, :], (seed_count, fan_one, hidden_width)),
        ],
        axis=1,
    ).reshape(-1, hidden_width)
    sigmoid_v = jax.nn.sigmoid(shifted)
    grad_shifted = grad_hidden * sigmoid_v * (1.0 + shifted * (1.0 - sigmoid_v))
    gain_part = jnp.sum(grad_shifted * normed, axis=0)
    shift_part = jnp.sum(grad_shifted, axis=0)
    grad_gain, grad_shift = lax.psum((gain_part, shift_part), ("feat", "batch"))
    grad_pre = (
        norm_gain
        * inv_std
        * (grad_shifted - grad_shift / row_total - normed * grad_gain / row_total)
    ).astype(jnp.bfloat16)
    block_rows = lax.all_gather(grad_pre, "feat", axis=0, tiled=True)
    self_block = self_x
    neigh_block = neigh_x
    lower_self_part = cross_rows(self_block, block_rows)
    lower_neigh_part = cross_rows(neigh_block, block_rows)
    grad_lower_self, grad_lower_neighbour, batch_upper_self, batch_upper_neigh = lax.psum(
        (lower_self_part, lower_neigh_part, upper_self_part, upper_neigh_part), "batch"
    )
    grad_upper_self, grad_upper_neighbour = lax.psum((batch_upper_self, batch_upper_neigh), "feat")
    return (
        embedding,
        grad_lower_self,
        grad_lower_neighbour,
        grad_upper_self,
        grad_upper_neighbour,
        grad_gain,
        grad_shift,
    )


def solution(mesh):
    return jax.shard_map(
        on_device,
        mesh=mesh,
        in_specs=(
            P("batch", "feat"),
            P("batch"),
            P("batch", None),
            P("batch", None, None),
            P("feat", None),
            P("feat", None),
            P(),
            P(),
            P(),
            P(),
            P(("batch", "feat"), None),
        ),
        out_specs=(
            P(("batch", "feat"), None),
            P("feat", None),
            P("feat", None),
            P(),
            P(),
            P(),
            P(),
        ),
        check_vma=False,
    )
```

profile of v0, /device:TPU:0, one launch (start us, length us, event | category | flops | bytes accessed | tf_op | source)
XLA Modules:
  0.0 564.8 jit_solution(11872161725431714999)
XLA Ops:
  8.0 1.4 reshape.63
  10.5 234.1 %while.14 = (s32[]{:T(128)}, bf16[8,352,256]{2,1,0:T(8,128)(2,1)}, bf16[8,352,256]{2,1,0:T(8,128)(2,1)}, s32[8,32]{1,0:T(8,128)S(1)}, s32[8,32,10]{1,0,2:T(8,128...) while((s32[]{:T(128)}, bf16[8,352,256]{2,1,0:T(8,128)(2,1)}, ...), condition=%wide.region_3.4_spmd.clone.clone, body=%wide.region_0.3_spmd.clone.clone.sunk | while | flops 1539940736 | bytes 24459248 | solution.py:52
  11.5 3.4 fusion.63
  15.0 11.7 %convert_reduce_fusion.5 = bf16[32,10,4096]{2,0,1:T(8,128)(2,1)S(1)} fusion(s32[32,10,15]{0,2,1:T(8,128)S(1)} %bitcast.68), kind=kLoop, calls=%fused_computation.2.clone.1 | loop fusion | flops 57671680 | bytes 2640640 | tf_op jit(solution)/shard_map/while/body/eval_jaxpr/reduce_sum | solution.py:35
  26.7 3.5 copy.62
  30.2 3.3 convert_element_type.93
  33.5 2.4 fusion.64
  36.8 2.1 fusion.65
  40.8 3.4 fusion.63
  44.2 11.7 %convert_reduce_fusion.5 = bf16[32,10,4096]{2,0,1:T(8,128)(2,1)S(1)} fusion(s32[32,10,15]{0,2,1:T(8,128)S(1)} %bitcast.68), kind=kLoop, calls=%fused_computation.2.clone.1 | loop fusion | flops 57671680 | bytes 2640640 | tf_op jit(solution)/shard_map/while/body/eval_jaxpr/reduce_sum | solution.py:35
  56.0 3.5 copy.62
  59.5 3.3 convert_element_type.93
  62.8 2.4 fusion.64
  66.0 2.1 fusion.65
  70.1 3.4 fusion.63
  73.5 11.7 %convert_reduce_fusion.5 = bf16[32,10,4096]{2,0,1:T(8,128)(2,1)S(1)} fusion(s32[32,10,15]{0,2,1:T(8,128)S(1)} %bitcast.68), kind=kLoop, calls=%fused_computation.2.clone.1 | loop fusion | flops 57671680 | bytes 2640640 | tf_op jit(solution)/shard_map/while/body/eval_jaxpr/reduce_sum | solution.py:35
  85.2 3.5 copy.62
  88.7 3.3 convert_element_type.93
  92.1 2.4 fusion.64
  95.3 2.1 fusion.65
  99.3 3.4 fusion.63
  102.8 11.7 %convert_reduce_fusion.5 = bf16[32,10,4096]{2,0,1:T(8,128)(2,1)S(1)} fusion(s32[32,10,15]{0,2,1:T(8,128)S(1)} %bitcast.68), kind=kLoop, calls=%fused_computation.2.clone.1 | loop fusion | flops 57671680 | bytes 2640640 | tf_op jit(solution)/shard_map/while/body/eval_jaxpr/reduce_sum | solution.py:35
  114.5 3.5 copy.62
  118.0 3.3 convert_element_type.93
  121.3 2.4 fusion.64
  124.6 2.1 fusion.65
  128.6 3.4 fusion.63
  132.0 11.7 %convert_reduce_fusion.5 = bf16[32,10,4096]{2,0,1:T(8,128)(2,1)S(1)} fusion(s32[32,10,15]{0,2,1:T(8,128)S(1)} %bitcast.68), kind=kLoop, calls=%fused_computation.2.clone.1 | loop fusion | flops 57671680 | bytes 2640640 | tf_op jit(solution)/shard_map/while/body/eval_jaxpr/reduce_sum | solution.py:35
  143.8 3.5 copy.62
  147.3 3.3 convert_element_type.93
  150.6 2.4 fusion.64
  153.8 2.1 fusion.65
  157.9 3.4 fusion.63
  161.3 11.7 %convert_reduce_fusion.5 = bf16[32,10,4096]{2,0,1:T(8,128)(2,1)S(1)} fusion(s32[32,10,15]{0,2,1:T(8,128)S(1)} %bitcast.68), kind=kLoop, calls=%fused_computation.2.clone.1 | loop fusion | flops 57671680 | bytes 2640640 | tf_op jit(solution)/shard_map/while/body/eval_jaxpr/reduce_sum | solution.py:35
  173.0 3.5 copy.62
  176.5 3.3 convert_element_type.93
  179.9 2.4 fusion.64
  183.1 2.1 fusion.65
  187.1 3.4 fusion.63
  190.6 11.7 %convert_reduce_fusion.5 = bf16[32,10,4096]{2,0,1:T(8,128)(2,1)S(1)} fusion(s32[32,10,15]{0,2,1:T(8,128)S(1)} %bitcast.68), kind=kLoop, calls=%fused_computation.2.clone.1 | loop fusion | flops 57671680 | bytes 2640640 | tf_op jit(solution)/shard_map/while/body/eval_jaxpr/reduce_sum | solution.py:35
  202.3 3.5 copy.62
  205.8 3.3 convert_element_type.93
  209.1 2.4 fusion.64
  212.4 2.1 fusion.65
  216.4 3.4 fusion.63
  219.8 11.7 %convert_reduce_fusion.5 = bf16[32,10,4096]{2,0,1:T(8,128)(2,1)S(1)} fusion(s32[32,10,15]{0,2,1:T(8,128)S(1)} %bitcast.68), kind=kLoop, calls=%fused_computation.2.clone.1 | loop fusion | flops 57671680 | bytes 2640640 | tf_op jit(solution)/shard_map/while/body/eval_jaxpr/reduce_sum | solution.py:35
  231.6 3.5 copy.62
  235.1 3.3 convert_element_type.93
  238.4 2.4 fusion.64
  241.6 2.1 fusion.65
  244.7 2.0 fusion.24
  246.7 2.1 convolution_add_fusion
  251.4 36.6 %reduce-scatter.2.cloned.1.call-done = f32[704,256]{1,0:T(8,128)} async-done(((f32[2816,256]{1,0:T(8,128)}), f32[704,256]{1,0:T(8,128)}) %reduce-scatter.2.cloned.1.call-update) | async-done | bytes 720912 | tf_op jit(solution)/shard_map/reduce_scatter | solution.py:85
  289.3 39.3 %psum.70 = f32[256]{0:T(256)S(1)} all-reduce(f32[256]{0:T(256)S(1)} %reduce_sum.63), channel_id=1, replica_groups=mesh['feat'=4,'batch'=8] {'feat','batch'}, use_global_device_ids=true, to_apply=%region_6.7 | all-reduce | flops 256 | bytes 2048 | tf_op jit(solution)/shard_map/psum | solution.py:92
  329.9 41.0 %psum.71 = f32[256]{0:T(256)S(1)} all-reduce(f32[256]{0:T(256)S(1)} %multiply_reduce_fusion.1), channel_id=1, replica_groups=mesh['feat'=4,'batch'=8] {'feat','batch'}, use_global_device_ids=true, to_apply=%region_8.9 | all-reduce | flops 256 | bytes 2048 | tf_op jit(solution)/shard_map/psum | solution.py:94
  371.5 2.0 fusion.23
  373.5 39.1 %all-reduce = (f32[256]{0:T(256)S(1)}, f32[256]{0:T(256)S(1)}) all-reduce(f32[256]{0:T(256)S(1)} %get-tuple-element.110, f32[256]{0:T(256)S(1)} %get-tuple-element.109), channel_id=1, replica_groups=mesh['feat'=4,'batch'=8] {'feat','batch'}, use_global_device_ids=true, to_apply=%region_13.14 | all-reduce | flops 512 | bytes 4096 | tf_op jit(solution)/shard_map/psum | solution.py:133
  412.6 2.0 multiply_convert_fusion
  417.1 17.4 %all-gather.2.cloned.1.call-done = bf16[2816,256]{1,0:T(8,128)(2,1)} async-done(((bf16[704,256]{1,0:T(8,128)(2,1)}), bf16[2816,256]{1,0:T(8,128)(2,1)}) %all-gather.2.cloned.1.call-update) | async-done | bytes 1441808 | tf_op jit(solution)/shard_map/all_gather | solution.py:139
  434.4 3.2 fusion.25
  439.0 79.4 %all-reduce.6.cloned.1.call-done = (f32[256,256]{1,0:T(8,128)}, f32[256,256]{1,0:T(8,128)}, f32[256,256]{1,0:T(8,128)}, f32[256,256]{1,0:T(8,128)}) async-done(((f32[256,256]{1,0:T(8,128)}, f32[256,256]{1,0:T(8,128)}, f32[256,256]{1,0:T(8,128)}, f32[256,256]{1,0:T(8,128)}), (f32[256,256]{1,0:T(8,128)}, f32[256,256]{1,0:T(8,128)}, f32[256,256]{1,0:T(8,128)}, ...) | async-done | bytes 1048592 | tf_op jit(solution)/shard_map/psum | solution.py:144
  519.4 34.1 %all-reduce.8.cloned.1.call-done = (f32[256,256]{1,0:T(8,128)}, f32[256,256]{1,0:T(8,128)}) async-done(((f32[256,256]{1,0:T(8,128)}, f32[256,256]{1,0:T(8,128)}), (f32[256,256]{1,0:T(8,128)}, f32[256,256]{1,0:T(8,128)})) %all-reduce.8.cloned.1.call-update) | async-done | bytes 524304 | tf_op jit(solution)/shard_map/psum | solution.py:147
  553.4 1.7 copy.83
  555.9 1.7 copy.85
  (175 shorter events, 35.7 us)
Async XLA Ops:
  7.2 237.5 %copy-start = (bf16[256,256]{1,0:T(8,128)(2,1)S(1)}, bf16[256,256]{1,0:T(8,128)(2,1)}, u32[]{:S(2)}) copy-start(bf16[256,256]{1,0:T(8,128)(2,1)} %param.17) | copy-start | bytes 393220
  7.2 280.9 %reduce-scatter.2.cloned.1.call-start = ((), (), s32[]{:S(2)}) async-start(), calls=%async_computation.1 | async-start | bytes 3604480 | tf_op jit(solution)/shard_map/reduce_scatter | solution.py:85
  244.6 2.0 copy-start.2
  244.6 2.0 copy-start.11
  248.8 0.9 copy-start.5
  248.8 0.9 copy-start.8
  248.8 1.2 copy-start.6
  248.8 185.6 %all-gather.2.cloned.1.call-start = ((), (), s32[]{:S(2)}) async-start(), calls=%async_computation.2 | async-start | bytes 1802240 | tf_op jit(solution)/shard_map/all_gather | solution.py:139
  250.4 120.5 %copy-start.12 = (f32[256]{0:T(256)S(1)}, f32[256]{0:T(256)}, u32[]{:S(2)}) copy-start(f32[256]{0:T(256)} %param.19) | copy-start | bytes 3076
  251.4 120.1 %copy-start.4 = (f32[704,256]{1,0:T(8,128)S(1)}, f32[704,256]{1,0:T(8,128)}, u32[]{:S(2)}) copy-start(f32[704,256]{1,0:T(8,128)} %reshape.68) | copy-start | bytes 2162692
  288.0 83.5 %copy-start.1 = (f32[704,256]{1,0:T(8,128)S(1)}, f32[704,256]{1,0:T(8,128)}, u32[]{:S(2)}) copy-start(f32[704,256]{1,0:T(8,128)} %reduce-scatter.2.cloned.1.call-done) | copy-start | bytes 2162692
  412.6 2.3 copy-start.13
  412.6 2.3 copy-start.14
  414.6 103.8 %all-reduce.6.cloned.1.call-start = ((), (), s32[]{:S(2)}) async-start(), calls=%async_computation.3 | async-start | bytes 2097152 | tf_op jit(solution)/shard_map/psum | solution.py:144
  434.4 3.2 copy-start.3
  438.9 79.7 %copy-start.7 = (bf16[256,256]{1,0:T(8,128)(2,1)S(1)}, bf16[256,256]{1,0:T(8,128)(2,1)}, u32[]{:S(2)}) copy-start(bf16[256,256]{1,0:T(8,128)(2,1)} %param.22) | copy-start | bytes 393220
  438.9 114.5 %all-reduce.8.cloned.1.call-start = ((), (), s32[]{:S(2)}) async-start(), calls=%async_computation.4 | async-start | bytes 1048576 | tf_op jit(solution)/shard_map/psum | solution.py:147
  518.4 36.7 %copy-start.9 = (f32[256,256]{1,0:T(8,128)S(1)}, f32[256,256]{1,0:T(8,128)}, u32[]{:S(2)}) copy-start(f32[256,256]{1,0:T(8,128)} %get-tuple-element.206) | copy-start | bytes 786436
  553.4 4.1 copy-start.10
Sparse Core Ops, SparseCore 0:
  249.0 39.0 reduce-scatter.1
  414.7 19.6 all-gather.1
  439.4 78.9 all-reduce.5
  520.7 32.6 all-reduce.7
where the time goes:
time: 567 us; the launch traced here: 565 us
  waiting for transfers between devices  168 us (30%)
  blocking collectives  119 us (21%)
  other arithmetic  108 us (19%)
  local copies, waits for them, and re-layouts  80.2 us (14%)
  matrix products  74.6 us (13%)
  between operations  13.9 us (2%)
    reduce_sum x8, other arithmetic, one_block(): jnp.sum((far_part[:, :, :, None] == positions).astype(jnp.float32), axis=2)  93.7 us
    psum x1, waiting for transfers between devices, on_device(): lax.psum((lower_self_part, lower_neigh_part, upper_self_part, upper_neigh...  79.4 us
    convert_element_type x16, local copies, waits for them, and re-layouts, one_block(): far_counts = jnp.sum((far_part[:, :, :, None] == positions).astype(jnp.fl...  54.6 us
    psum x1, blocking collectives, on_device(): lax.psum(jnp.sum(centred * centred, axis=0), ('feat', 'batch')) / row_total  41 us
    psum x1, blocking collectives, on_device(): row_mean = lax.psum(jnp.sum(pre_act, axis=0), ('feat', 'batch')) / row_total  39.3 us
    psum x1, blocking collectives, on_device(): grad_gain, grad_shift = lax.psum((gain_part, shift_part), ('feat', 'batch'))  39.1 us
    reduce_scatter x1, waiting for transfers between devices, on_device(): lax.psum_scatter(jnp.dot(self_block, lower_self, preferred_element_type=j...  36.6 us
    psum x1, waiting for transfers between devices, on_device(): lax.psum((batch_upper_self, batch_upper_neigh), 'feat')  34.1 us
  transfers between devices with their start and end apart: 4, of which 4 were waited for; matrix products, arithmetic and copies ran while one was open for 1% of the time, Pallas kernels for 0%

commit v1 on v0

v1 whole, which is shorter than its diff:
```python
import functools

import jax
import jax.numpy as jnp
from jax import lax
from jax.experimental import pallas as pl
from jax.experimental.pallas import tpu as pltpu
from jax.sharding import PartitionSpec as P

BF = jnp.bfloat16
F32 = jnp.float32
LANES = 128
LOW = 256
SLOT = 16
GROUP = LOW // SLOT
MIB = 2**20


def dot(left, right, dims=((1,), (0,)), precision=None):
    return lax.dot_general(
        left, right, (dims, ((), ())), preferred_element_type=F32, precision=precision
    )


def params(mib):
    return pltpu.CompilerParams(vmem_limit_bytes=mib * MIB)


def whole(shape):
    return pl.BlockSpec(shape, lambda *_: (0,) * len(shape))


def halves(value):
    high = value.astype(BF)
    return high, (value - high.astype(F32)).astype(BF)


def count_kernel(high_ref, low_ref, count_ref):
    index = lax.broadcasted_iota(jnp.int32, (LOW, LOW), 0).astype(BF)
    one = jnp.ones((LOW, LOW), BF)
    zero = jnp.zeros((LOW, LOW), BF)
    for g in range(high_ref.shape[1]):
        left = jnp.where(index == high_ref[0, g : g + 1, :].astype(BF), one, zero)
        right = jnp.where(index == low_ref[0, g : g + 1, :].astype(BF), one, zero)
        counts = dot(left, right, ((1,), (1,))).astype(BF)
        for h in range(LOW // GROUP):
            count_ref[g * GROUP : (g + 1) * GROUP, h * LOW : (h + 1) * LOW] = counts[
                h * GROUP : (h + 1) * GROUP, :
            ]


def count_rows(high, low, table_rows):
    steps, groups, _ = high.shape
    rows = groups * GROUP
    spec = pl.BlockSpec((1, groups, LOW), lambda i: (i, 0, 0))
    return pl.pallas_call(
        count_kernel,
        grid=(steps,),
        in_specs=[spec, spec],
        out_specs=pl.BlockSpec((rows, table_rows), lambda i: (i, 0)),
        out_shape=jax.ShapeDtypeStruct((steps * rows, table_rows), BF),
        compiler_params=params(24),
        cost_estimate=pl.CostEstimate(
            flops=2 * steps * groups * LOW**3,
            bytes_accessed=2 * steps * rows * table_rows,
            transcendentals=0,
        ),
        name="count_rows",
    )(high, low)


def pick_kernel(
    first_block,
    per_slot,
    fans,
    ids_ref,
    count_ref,
    own_ref,
    peer_ref,
    self_own_ref,
    self_peer_ref,
    neigh_own_ref,
    neigh_peer_ref,
    across_ref,
    pre_ref,
    hot,
):
    blocks = ids_ref.shape[1]
    table_rows, width = own_ref.shape
    lanes = lax.broadcasted_iota(jnp.int32, (LANES, LANES), 1)
    for b in range(blocks):
        ids = jnp.broadcast_to(ids_ref[0, b : b + 1, :], (LANES, LANES)).T
        low = jnp.bitwise_and(ids, LOW - 1)
        high = lax.shift_right_logical(ids, 8).astype(BF)
        for part in range(LOW // LANES):
            base = jnp.where(lanes + LANES * part == low, 1.0, 0.0).astype(BF)
            for h in range(table_rows // LOW):
                start = h * LOW + part * LANES
                hot[b * LANES : (b + 1) * LANES, start : start + LANES] = jnp.where(
                    high == BF(h), base, jnp.zeros_like(base)
                )
    slot = (first_block + pl.program_id(0) * blocks) // per_slot
    fan = jnp.where(slot == 0, fans[0], fans[1]).astype(F32)
    total = None
    for i, (table, weight_self, weight_neigh) in enumerate(
        ((own_ref, self_own_ref, neigh_own_ref), (peer_ref, self_peer_ref, neigh_peer_ref))
    ):
        self_x = dot(hot[...], table[...]).astype(BF)
        neigh_x = (dot(count_ref[...], table[...]) / fan).astype(BF)
        across_ref[2 * i * width : (2 * i + 1) * width, :] = self_x.T
        across_ref[(2 * i + 1) * width : (2 * i + 2) * width, :] = neigh_x.T
        part = dot(self_x, weight_self[...]) + dot(neigh_x, weight_neigh[...])
        total = part if total is None else total + part
    pre_ref[...] = total.astype(BF)


def pick_rows(first_block, count, ids, counts, own, peer, weights, per_slot, fans):
    blocks = 1
    table_rows, width = own.shape
    rows = blocks * LANES
    steps = count // blocks
    skip = first_block // blocks
    hidden_width = weights[0].shape[1]
    total = count * LANES
    return pl.pallas_call(
        functools.partial(pick_kernel, first_block, per_slot, fans),
        grid=(steps,),
        in_specs=[
            pl.BlockSpec((1, blocks, LANES), lambda i: (i + skip, 0, 0)),
            pl.BlockSpec((rows, table_rows), lambda i: (i + skip, 0)),
            whole(own.shape),
            whole(peer.shape),
        ]
        + [whole(weights[0].shape)] * 4,
        out_specs=[
            pl.BlockSpec((4 * width, rows), lambda i: (0, i)),
            pl.BlockSpec((rows, hidden_width), lambda i: (i, 0)),
        ],
        out_shape=[
            jax.ShapeDtypeStruct((4 * width, total), BF),
            jax.ShapeDtypeStruct((total, hidden_width), BF),
        ],
        scratch_shapes=[pltpu.VMEM((rows, table_rows), BF)],
        compiler_params=params(32),
        cost_estimate=pl.CostEstimate(
            flops=8 * total * table_rows * width,
            bytes_accessed=2 * total * table_rows + 4 * table_rows * width,
            transcendentals=0,
        ),
        name="pick_rows",
    )(ids, counts, own, peer, *weights)


def stats_kernel(chunks, *refs):
    pairs, acrosses = refs[: 2 * chunks], refs[2 * chunks : 3 * chunks]
    keep_ref, send_ref = refs[3 * chunks :]
    width = acrosses[0].shape[0] // 4
    rows = sum(pairs[2 * i].shape[0] for i in range(chunks))
    values = [
        pairs[2 * i][...].astype(F32) + pairs[2 * i + 1][...].astype(F32) for i in range(chunks)
    ]
    mean = sum(jnp.sum(v, axis=0, keepdims=True) for v in values) / rows
    square = sum(jnp.sum((v - mean) * (v - mean), axis=0, keepdims=True) for v in values)
    column = sum(
        dot(jnp.ones((8, a.shape[1]), BF), a[...], ((1,), (1,))) for a in acrosses
    )
    pad = jnp.zeros((4, mean.shape[1]), F32)
    lanes = mean.shape[1] - width
    for ref, first in ((keep_ref, 0), (send_ref, 2)):
        parts = [column[:1, (first + j) * width : (first + j + 1) * width] for j in range(2)]
        if lanes:
            parts = [jnp.concatenate([p, jnp.zeros((1, lanes), F32)], axis=1) for p in parts]
        ref[...] = jnp.concatenate([mean, square, *parts, pad], axis=0)


def middle_kernel(
    chunks,
    slots,
    row_total,
    batches,
    place_ref,
    *refs,
):
    pairs, acrosses = refs[: 2 * chunks], refs[2 * chunks : 3 * chunks]
    (
        stats_ref,
        gain_ref,
        shift_ref,
        upper_self_ref,
        upper_neigh_ref,
        grad_ref,
        embed_ref,
        keep_ref,
        send_ref,
        sums_ref,
        both,
        embed_all,
    ) = refs[3 * chunks :]
    seeds, hidden_width = grad_ref.shape
    width = acrosses[0].shape[0] // 4
    fan_one = slots - 1
    mean = stats_ref[0:1, :]
    inv_std = lax.rsqrt(stats_ref[1:2, :] / row_total + 1e-05)
    gain, shift = gain_ref[...], shift_ref[...]
    grad = grad_ref[...]
    d_self = dot(grad, upper_self_ref[...], ((1,), (1,)))
    d_mean = dot(grad, upper_neigh_ref[...], ((1,), (1,))) / fan_one
    gain_sum = shift_sum = hidden_sum = own_rows = None
    slot = 0
    for i in range(chunks):
        for k in range(pairs[2 * i].shape[0] // seeds):
            span = slice(k * seeds, (k + 1) * seeds)
            pre_act = pairs[2 * i][span, :].astype(F32) + pairs[2 * i + 1][span, :].astype(F32)
            normed = (pre_act - mean) * inv_std
            shifted = gain * normed + shift
            sigmoid_v = 1.0 / (1.0 + jnp.exp(-shifted))
            hidden = (shifted * sigmoid_v).astype(BF)
            if slot == 0:
                own_rows = hidden
            else:
                hidden_sum = hidden.astype(F32) + (0.0 if hidden_sum is None else hidden_sum)
            grad_hidden = d_self if slot == 0 else d_mean
            grad_shifted = grad_hidden * sigmoid_v * (1.0 + shifted * (1.0 - sigmoid_v))
            gain_part = grad_shifted * normed
            gain_sum = gain_part if gain_sum is None else gain_sum + gain_part
            shift_sum = grad_shifted if shift_sum is None else shift_sum + grad_shifted
            both[slot * seeds : (slot + 1) * seeds, :hidden_width] = grad_shifted.astype(BF)
            both[slot * seeds : (slot + 1) * seeds, hidden_width:] = normed.astype(BF)
            slot += 1
    hidden_mean = (hidden_sum / fan_one).astype(BF)
    embed_all[...] = dot(own_rows, upper_self_ref[...]) + dot(hidden_mean, upper_neigh_ref[...])
    own_seeds = embed_ref.shape[0]
    start = pl.multiple_of(place_ref[0] * own_seeds, own_seeds)
    embed_ref[...] = embed_all[pl.ds(start, own_seeds), :].astype(BF)
    upper_self_part = dot(own_rows, grad, ((0,), (0,)))
    upper_neigh_part = dot(hidden_mean, grad, ((0,), (0,)))
    first_core = place_ref[1] == 0
    upper_keep = jnp.where(first_core, upper_self_part, upper_neigh_part)
    upper_send = jnp.where(first_core, upper_neigh_part, upper_self_part)
    gain_high, gain_low = halves(jnp.sum(gain_sum, axis=0, keepdims=True))
    shift_high, shift_low = halves(jnp.sum(shift_sum, axis=0, keepdims=True))
    sums = [gain_high, gain_low, shift_high, shift_low]
    sums_ref[...] = jnp.concatenate(
        [s.astype(F32) for s in sums] + [jnp.zeros((12, hidden_width), F32)], axis=0
    ).astype(BF)
    lower = None
    first = 0
    for a in acrosses:
        part = dot(a[...], both[first : first + a.shape[1], :])
        lower = part if lower is None else lower + part
        first += a.shape[1]
    piece, upper_piece = width // batches, hidden_width // batches
    for block, upper, ref in ((0, upper_keep, keep_ref), (2, upper_send, send_ref)):
        for d in range(batches):
            parts = []
            for lane in (0, hidden_width):
                for j in (0, 1):
                    row = (block + j) * width + d * piece
                    parts.append(lower[row : row + piece, lane : lane + hidden_width])
            parts.append(upper[d * upper_piece : (d + 1) * upper_piece, :])
            ref[d, :, :] = jnp.concatenate(parts, axis=0).astype(ref.dtype)


def merge_kernel(keep_ref, got_ref, sums_ref, got_sums_ref, out_ref):
    batches, rows, _ = keep_ref.shape
    mine, theirs = sums_ref[...].astype(F32), got_sums_ref[...].astype(F32)
    sums = []
    for j in (0, 2):
        sums += halves(
            (mine[j : j + 1] + mine[j + 1 : j + 2]) + (theirs[j : j + 1] + theirs[j + 1 : j + 2])
        )
    tail = jnp.concatenate(
        [s.astype(F32) for s in sums] + [jnp.zeros((12, mine.shape[1]), F32)], axis=0
    ).astype(BF)
    for d in range(batches):
        out_ref[d, :rows, :] = (keep_ref[d, :, :] + got_ref[d, :, :].astype(F32)).astype(BF)
        out_ref[d, rows:, :] = tail


def finish_kernel(row_total, parts_ref, stats_ref, gain_ref, column_ref, out_ref, gain_out, shift_out):
    batches, all_rows, _ = parts_ref.shape
    total = parts_ref[0, :, :].astype(F32)
    for d in range(1, batches):
        total = total + parts_ref[d, :, :].astype(F32)
    rows = all_rows - 16
    pieces = column_ref.shape[1]
    grad_gain = total[rows : rows + 1] + total[rows + 1 : rows + 2]
    grad_shift = total[rows + 2 : rows + 3] + total[rows + 3 : rows + 4]
    inv_std = lax.rsqrt(stats_ref[1:2, :] / row_total + 1e-05)
    outer = dot(
        column_ref[...],
        jnp.broadcast_to(grad_shift / row_total, (8, grad_shift.shape[1])),
        ((0,), (0,)),
        lax.Precision.HIGHEST,
    )
    lower = (gain_ref[...] * inv_std) * (
        total[:pieces] - outer - total[pieces : 2 * pieces] * (grad_gain / row_total)
    )
    out_ref[...] = jnp.concatenate([lower, total[2 * pieces : rows]], axis=0).astype(BF)
    gain_out[...] = grad_gain
    shift_out[...] = grad_shift


def place_kernel(masks, group_ref, parts_ref, self_ref, neigh_ref, upper_ref):
    piece = self_ref.shape[0] // len(masks)
    upper_piece = upper_ref.shape[0] // len(masks)
    for i, mask in enumerate(masks):
        d = group_ref[0] ^ mask
        rows = parts_ref[i, :, :].astype(F32)
        self_ref[pl.ds(pl.multiple_of(d * piece, piece), piece), :] = rows[:piece]
        neigh_ref[pl.ds(pl.multiple_of(d * piece, piece), piece), :] = rows[piece : 2 * piece]
        upper_ref[pl.ds(pl.multiple_of(d * upper_piece, upper_piece), upper_piece), :] = rows[
            2 * piece :
        ]


def swap(value, axis, mask):
    return lax.ppermute(value, axis, [(i, i ^ mask) for i in range(lax.axis_size(axis))])


SMEM = pl.BlockSpec(memory_space=pltpu.SMEM)


def on_device(
    node_feats,
    seed_ids,
    first_hop,
    second_hop,
    lower_self,
    lower_neighbour,
    norm_gain,
    norm_shift,
    upper_self,
    upper_neighbour,
    embed_grad,
):
    feats, batches = lax.axis_size("feat"), lax.axis_size("batch")
    chips = feats // 2
    feat, batch = lax.axis_index("feat"), lax.axis_index("batch")
    core, chip = feat % 2, feat // 2
    table_rows, width = node_feats.shape
    hidden_width = lower_self.shape[1]
    fan_one, fan_two = first_hop.shape[1], second_hop.shape[2]
    slots = fan_one + 1
    own_seeds = embed_grad.shape[0]
    seeds = own_seeds * chips
    row_total = own_seeds * slots * feats * batches
    rows = seeds * slots

    peer_feats = swap(node_feats, "feat", 1)
    peer_self = swap(lower_self, "feat", 1)
    peer_neigh = swap(lower_neighbour, "feat", 1)
    grads = jnp.zeros((seeds, hidden_width), BF)
    for mask in range(chips):
        part = embed_grad if mask == 0 else swap(embed_grad, "feat", 2 * mask)
        grads = lax.dynamic_update_slice(grads, part, ((chip ^ mask) * own_seeds, 0))

    def mine(ids):
        split = ids.reshape(chips, 2, own_seeds, *ids.shape[1:])
        part = lax.dynamic_index_in_dim(split, core, 1, keepdims=False)
        return part.reshape(seeds, *ids.shape[1:])

    near = mine(first_hop)
    self_ids = jnp.concatenate([mine(seed_ids)[:, None], near], axis=1).T
    self_ids = self_ids.reshape(-1, 1, LANES)

    def padded(ids, fan):
        return jnp.pad(ids, ((0, 0), (0, 0), (0, SLOT - fan)), constant_values=-1)

    neigh_ids = jnp.concatenate(
        [padded(near[None], fan_one), padded(mine(second_hop).transpose(1, 0, 2), fan_two)], axis=0
    )
    in_group = (jnp.arange(seeds, dtype=jnp.int32) % GROUP)[None, :, None]
    high = jnp.where(neigh_ids < 0, -1, (neigh_ids >> 8) * GROUP + in_group)
    shape = (slots, seeds // GROUP, LOW)
    counts = count_rows(high.reshape(shape), (neigh_ids & (LOW - 1)).reshape(shape), table_rows)

    weights = (lower_self, peer_self, lower_neighbour, peer_neigh)
    per_slot = seeds // LANES
    pairs, acrosses = [], []
    first = 0
    for share in CHUNKS:
        across, pre_act = pick_rows(
            first * per_slot,
            share * per_slot,
            self_ids,
            counts,
            node_feats,
            peer_feats,
            weights,
            per_slot,
            (fan_one, fan_two),
        )
        acrosses.append(across)
        mask = 2
        other = swap(pre_act, "feat", mask)
        while 2 * mask < feats:
            mask *= 2
            pre_act = (pre_act.astype(F32) + other.astype(F32)).astype(BF)
            other = swap(pre_act, "feat", mask)
        pairs += [pre_act, other]
        first += share

    tile = jax.ShapeDtypeStruct((8, hidden_width), F32)
    keep, send = pl.pallas_call(
        functools.partial(stats_kernel, len(CHUNKS)),
        out_shape=[tile, tile],
        compiler_params=params(40),
        name="stats",
    )(*pairs, *acrosses)

    def joined(mine, other, count):
        gap = mine[0:1] - other[0:1]
        return jnp.concatenate(
            [
                (mine[0:1] + other[0:1]) * 0.5,
                mine[1:2] + other[1:2] + gap * gap * (count * 0.5),
                mine[2:] + other[2:],
            ],
            axis=0,
        )

    count = float(rows)
    stats = joined(keep, swap(send, "feat", 1), count)
    mask = 1
    while mask < batches:
        count *= 2
        stats = joined(stats, swap(stats, "batch", mask), count)
        mask *= 2

    gain_row, shift_row = norm_gain[None, :], norm_shift[None, :]
    place = jnp.stack([chip, core]).astype(jnp.int32)
    per_group = 4 * width // batches + hidden_width // batches
    operands = [
        *pairs,
        *acrosses,
        stats,
        gain_row,
        shift_row,
        upper_self,
        upper_neighbour,
        grads,
    ]
    vmem = pl.BlockSpec(memory_space=pltpu.VMEM)
    embedding, keep, send, sums = pl.pallas_call(
        functools.partial(middle_kernel, len(CHUNKS), slots, row_total, batches),
        in_specs=[SMEM] + [vmem] * len(operands),
        out_shape=[
            jax.ShapeDtypeStruct((own_seeds, hidden_width), BF),
            jax.ShapeDtypeStruct((batches, per_group, hidden_width), F32),
            jax.ShapeDtypeStruct((batches, per_group, hidden_width), BF),
            jax.ShapeDtypeStruct((16, hidden_width), BF),
        ],
        scratch_shapes=[
            pltpu.VMEM((rows, 2 * hidden_width), BF),
            pltpu.VMEM((seeds, hidden_width), F32),
        ],
        compiler_params=params(40),
        name="middle",
    )(place, *operands)

    parts = pl.pallas_call(
        merge_kernel,
        out_shape=jax.ShapeDtypeStruct((batches, per_group + 16, hidden_width), BF),
        compiler_params=params(16),
        name="merge",
    )(keep, swap(send, "feat", 1), sums, swap(sums, "feat", 1))
    parts = lax.all_to_all(parts, "batch", 0, 0)

    piece = width // batches
    column = lax.dynamic_slice(stats[2:4], (0, batch * piece), (2, piece)).reshape(1, 2 * piece)
    column = jnp.pad(column, ((0, 7), (0, 0)))
    out_rows = 2 * piece + hidden_width // batches
    line = jax.ShapeDtypeStruct((1, hidden_width), F32)
    done, grad_gain, grad_shift = pl.pallas_call(
        functools.partial(finish_kernel, row_total),
        out_shape=[jax.ShapeDtypeStruct((out_rows, hidden_width), BF), line, line],
        compiler_params=params(16),
        name="finish",
    )(parts, stats, gain_row, column)

    gathered, masks = done[None], [0]
    mask = batches // 2
    while mask:
        gathered = jnp.concatenate([gathered, swap(gathered, "batch", mask)], axis=0)
        masks += [m ^ mask for m in masks]
        mask //= 2
    grad_self, grad_neigh, upper = pl.pallas_call(
        functools.partial(place_kernel, tuple(masks)),
        in_specs=[SMEM, vmem],
        out_shape=[
            jax.ShapeDtypeStruct((width, hidden_width), F32),
            jax.ShapeDtypeStruct((width, hidden_width), F32),
            jax.ShapeDtypeStruct((hidden_width, hidden_width), F32),
        ],
        compiler_params=params(16),
        name="place",
    )(batch.astype(jnp.int32)[None], gathered)
    upper_other = swap(upper, "feat", 1)
    return (
        embedding,
        grad_self,
        grad_neigh,
        jnp.where(core == 0, upper, upper_other),
        jnp.where(core == 0, upper_other, upper),
        grad_gain[0],
        grad_shift[0],
    )


CHUNKS = (4, 4, 3)


def solution(mesh):
    return jax.shard_map(
        on_device,
        mesh=mesh,
        in_specs=(
            P("batch", "feat"),
            P("batch"),
            P("batch", None),
            P("batch", None, None),
            P("feat", None),
            P("feat", None),
            P(),
            P(),
            P(),
            P(),
            P(("batch", "feat"), None),
        ),
        out_specs=(
            P(("batch", "feat"), None),
            P("feat", None),
            P("feat", None),
            P(),
            P(),
            P(),
            P(),
        ),
        check_vma=False,
    )
```

time: 567 us -> 129 us (0.23)
  waiting for transfers between devices: 168 us -> 48 us
  blocking collectives: 119 us -> 0 us
  other arithmetic: 108 us -> 1.11 us
  matrix products: 74.6 us -> 0 us
  local copies, waits for them, and re-layouts: 80.2 us -> 20.7 us
  Pallas kernels: 0 us -> 36.7 us
  starting transfers between devices: 0.16 us -> 20.4 us
  between operations: 13.9 us -> 1.14 us
    psum x3 -> x0, blocking collectives: 119 us -> none  [the longest x1 41 us: on_device(): lax.psum(jnp.sum(centred * centred, axis=0), ('feat', 'batch')) / row_total]
    psum x2 -> x0, waiting for transfers between devices: 113 us -> none  [the longest x1 79.4 us: on_device(): lax.psum((lower_self_part, lower_neigh_part, upper_self_part, upper_neigh...]
    reduce_sum x20 -> x0, other arithmetic: 104 us -> none  [the longest x8 93.7 us: one_block(): jnp.sum((far_part[:, :, :, None] == positions).astype(jnp.float32), axis=2)]
    dot_general x34 -> x0, matrix products: 74.6 us -> none  [the longest x8 26.9 us: one_block(): jnp.dot(picker, node_feats, preferred_element_type=jnp.float32)]
    convert_element_type x16 -> x0, local copies, waits for them, and re-layouts: 54.6 us -> none  [one_block(): far_counts = jnp.sum((far_part[:, :, :, None] == positions).astype(jnp.fl...]
    pallas_call x0 -> x9, Pallas kernels: none -> 36.7 us  [the longest x3 24.3 us: pick_rows(): pl.pallas_call(functools.partial(pick_kernel, first_block, per_slot, fans...]
    reduce_scatter x1 -> x0, waiting for transfers between devices: 36.6 us -> none  [on_device(): lax.psum_scatter(jnp.dot(self_block, lower_self, preferred_element_type=j...]
    ppermute x0 -> x17, waiting for transfers between devices: none -> 29.2 us  [swap(): lax.ppermute(value, axis, [(i, i ^ mask) for i in range(lax.axis_size(axi...]
  transfers between devices with their start and end apart: 4 -> 18, of which waited for: 4 -> 10; matrix products, arithmetic and copies ran while one was open for 1% -> 3% of each run, Pallas kernels for 0% -> 17%
where the time goes in v1:
time: 129 us; the launch traced here: 128 us
  waiting for transfers between devices  48 us (37%)
  Pallas kernels  36.7 us (28%)
  local copies, waits for them, and re-layouts  20.7 us (16%)
  starting transfers between devices  20.4 us (16%)
    ppermute x17, waiting for transfers between devices, swap(): lax.ppermute(value, axis, [(i, i ^ mask) for i in range(lax.axis_size(axi...  29.2 us
    pallas_call x3, Pallas kernels, pick_rows(): pl.pallas_call(functools.partial(pick_kernel, first_block, per_slot, fans...  24.3 us
    all_to_all x1, waiting for transfers between devices, on_device(): parts = lax.all_to_all(parts, 'batch', 0, 0)  18.9 us
    unnamed x56, local copies, waits for them, and re-layouts  17.3 us
    ppermute x17, starting transfers between devices, swap(): lax.ppermute(value, axis, [(i, i ^ mask) for i in range(lax.axis_size(axi...  14.6 us
    all_to_all x1, starting transfers between devices, on_device(): parts = lax.all_to_all(parts, 'batch', 0, 0)  5.82 us
    pallas_call x1, Pallas kernels, count_rows(): pl.pallas_call(count_kernel, grid=(steps,), in_specs=[spec, spec], out_sp...  5.4 us
    pallas_call x1, Pallas kernels, on_device(): pl.pallas_call(functools.partial(middle_kernel, len(CHUNKS), slots, row_t...  3.28 us
  transfers between devices with their start and end apart: 18, of which 10 were waited for; matrix products, arithmetic and copies ran while one was open for 3% of the time, Pallas kernels for 17%

profile of v1, /device:TPU:0, one launch (start us, length us, event | category | flops | bytes accessed | tf_op | source)
XLA Modules:
  0.0 128.1 jit_solution(11916402090970531820)
XLA Ops:
  0.6 0.5 collective-permute-start
  1.1 0.1 collective-permute-start.1
  1.2 0.4 collective-permute-start.2
  1.7 0.8 reshape.59
  2.5 0.1 copy.25
  2.6 0.1 concatenate.36
  2.7 0.1 add.103
  2.8 0.1 add.104
  2.9 1.1 reshape.62
  4.0 0.1 constant_dynamic-slice_fusion.1
  4.1 0.3 copy.22
  4.4 0.1 pad.13
  4.5 0.3 concatenate.37
  4.8 0.0 copy-start.26
  4.9 5.4 %count_rows.1.count_ref = bf16[1408,4096]{1,0:T(8,128)(2,1)S(1)} custom-call(s32[11,8,256]{2,1,0:T(8,128)S(1)} %get-tuple-element.46.high_ref, s32[11,8,256]{2,1,0:T(8,128)S(1)} %get-tuple-element.45.low_ref), custom_call_target="tpu_custom_call" | custom-call | flops 2952790016 | bytes 11534336 | tf_op jit(solution)/shard_map/count_rows/pallas_call | solution.py:56
  10.3 4.2 %copy-done = bf16[1408,4096]{1,0:T(8,128)(2,1)} copy-done((bf16[1408,4096]{1,0:T(8,128)(2,1)}, bf16[1408,4096]{1,0:T(8,128)(2,1)S(1)}, u32[]{:S(2)}) %copy-start) | copy-done | bytes 11534360
  14.5 0.1 reshape.60
  14.6 0.1 reshape.58
  14.7 0.1 broadcast_in_dim_reshape.6
  14.9 0.6 copy-done.9
  15.5 4.3 %copy-done.1 = bf16[1408,4096]{1,0:T(8,128)(2,1)S(1)} copy-done((bf16[1408,4096]{1,0:T(8,128)(2,1)S(1)}, bf16[1408,4096]{1,0:T(8,128)(2,1)}, u32[]{:S(2)}) %copy-start.1) | copy-done | bytes 11534360
  19.8 0.9 copy-done.10
  20.7 8.6 %pick_rows.4 = (bf16[1024,512]{1,0:T(8,128)(2,1)S(1)}, bf16[512,256]{1,0:T(8,128)(2,1)S(1)}) custom-call(s32[11,1,128]{2,1,0:T(1,128)S(1)} %reshape.61.ids_ref, bf16[1408,4096]{1,0:T(8,128)(2,1)S(1)} %copy-done.1, bf16[4096,256]{1,0:T(8,128)(2,1)S(1)} %copy-done.2, bf16[4096,256]{1,0:T(8,128)(2,1)} %collective-permute-done.peer_ref, ...), custom_call_target="tpu_custom_call" | custom-call | flops 4294967296 | bytes 8388608 | tf_op jit(solution)/shard_map/pick_rows/pallas_call | solution.py:125
  29.3 2.6 %collective-permute-start.4 = (bf16[512,256]{1,0:T(8,128)(2,1)S(1)}, bf16[512,256]{1,0:T(8,128)(2,1)S(1)}, u32[]{:S(2)}, u32[]{:S(2)}) collective-permute-start(bf16[512,256]{1,0:T(8,128)(2,1)S(1)} %get-tuple-element.26.refs_2_), channel_id=1, source_target_pairs={{0,16},{8,24},{16,0},{24,8},{1,17},{9,25},{17,1},{25,9},{2,18},{10... | collective-permute-start | bytes 786440 | tf_op jit(solution)/shard_map/ppermute | solution.py:318
  31.9 8.6 %pick_rows.3 = (bf16[1024,512]{1,0:T(8,128)(2,1)S(1)}, bf16[512,256]{1,0:T(8,128)(2,1)S(1)}) custom-call(s32[11,1,128]{2,1,0:T(1,128)S(1)} %reshape.61.ids_ref, bf16[1408,4096]{1,0:T(8,128)(2,1)S(1)} %copy-done.1, bf16[4096,256]{1,0:T(8,128)(2,1)S(1)} %copy-done.2, bf16[4096,256]{1,0:T(8,128)(2,1)} %collective-permute-done.peer_ref, ...), custom_call_target="tpu_custom_call" | custom-call | flops 4294967296 | bytes 8388608 | tf_op jit(solution)/shard_map/pick_rows/pallas_call | solution.py:125
  40.5 0.1 collective-permute-start.3
  40.6 7.2 %pick_rows.5 = (bf16[1024,384]{1,0:T(8,128)(2,1)S(1)}, bf16[384,256]{1,0:T(8,128)(2,1)S(1)}) custom-call(s32[11,1,128]{2,1,0:T(1,128)S(1)} %reshape.61.ids_ref, bf16[1408,4096]{1,0:T(8,128)(2,1)S(1)} %copy-done.1, bf16[4096,256]{1,0:T(8,128)(2,1)S(1)} %copy-done.2, bf16[4096,256]{1,0:T(8,128)(2,1)} %collective-permute-done.peer_ref, ...), custom_call_target="tpu_custom_call" | custom-call | flops 3221225472 | bytes 7340032 | tf_op jit(solution)/shard_map/pick_rows/pallas_call | solution.py:125
  47.8 1.7 %collective-permute-start.5 = (bf16[384,256]{1,0:T(8,128)(2,1)S(1)}, bf16[384,256]{1,0:T(8,128)(2,1)S(1)}, u32[]{:S(2)}, u32[]{:S(2)}) collective-permute-start(bf16[384,256]{1,0:T(8,128)(2,1)S(1)} %get-tuple-element.27.refs_4_), channel_id=1, source_target_pairs={{0,16},{8,24},{16,0},{24,8},{1,17},{9,25},{17,1},{25,9},{2,18},{10... | collective-permute-start | bytes 589832 | tf_op jit(solution)/shard_map/ppermute | solution.py:318
  49.5 5.3 %collective-permute-done.5.refs_5_ = bf16[384,256]{1,0:T(8,128)(2,1)S(1)} collective-permute-done((bf16[384,256]{1,0:T(8,128)(2,1)S(1)}, bf16[384,256]{1,0:T(8,128)(2,1)S(1)}, u32[]{:S(2)}, u32[]{:S(2)}) %collective-permute-start.5) | collective-permute-done | bytes 196640 | tf_op jit(solution)/shard_map/ppermute | solution.py:318
  54.9 1.0 stats.1
  56.0 0.1 collective-permute-start.6
  56.1 1.4 %collective-permute-start.10 = (bf16[64,256]{1,0:T(8,128)(2,1)S(1)}, bf16[64,256]{1,0:T(8,128)(2,1)S(1)}, u32[]{:S(2)}, u32[]{:S(2)}) collective-permute-start(bf16[64,256]{1,0:T(8,128)(2,1)S(1)} %copy-done.25), channel_id=1, source_target_pairs={{0,16},{8,24},{16,0},{24,8},{1,17},{9,25},{17,1},{25,9},{2,18},{10... | collective-permute-start | bytes 98312 | tf_op jit(solution)/shard_map/ppermute | solution.py:318
  57.6 1.6 %collective-permute-start.7 = (f32[8,256]{1,0:T(8,128)S(1)}, f32[8,256]{1,0:T(8,128)S(1)}, u32[]{:S(2)}, u32[]{:S(2)}) collective-permute-start(f32[8,256]{1,0:T(8,128)S(1)} %pad_maximum_fusion.3), channel_id=1, source_target_pairs={{0,1},{1,0},{2,3},{3,2},{4,5},{5,4},{6,7},{7,6},{8,9},{9,8},{10,11... | collective-permute-start | bytes 24584 | tf_op jit(solution)/shard_map/ppermute | solution.py:318
  59.2 2.1 %collective-permute-done.7 = f32[8,256]{1,0:T(8,128)S(1)} collective-permute-done((f32[8,256]{1,0:T(8,128)S(1)}, f32[8,256]{1,0:T(8,128)S(1)}, u32[]{:S(2)}, u32[]{:S(2)}) %collective-permute-start.7) | collective-permute-done | bytes 8224 | tf_op jit(solution)/shard_map/ppermute | solution.py:318
  61.3 1.6 %collective-permute-start.8 = (f32[8,256]{1,0:T(8,128)S(1)}, f32[8,256]{1,0:T(8,128)S(1)}, u32[]{:S(2)}, u32[]{:S(2)}) collective-permute-start(f32[8,256]{1,0:T(8,128)S(1)} %pad_maximum_fusion.4), channel_id=1, source_target_pairs={{0,2},{1,3},{2,0},{3,1},{4,6},{5,7},{6,4},{7,5},{8,10},{9,11},{10,... | collective-permute-start | bytes 24584 | tf_op jit(solution)/shard_map/ppermute | solution.py:318
  63.0 0.1 pad_add_fusion.place_ref
  63.0 2.0 %collective-permute-done.8 = f32[8,256]{1,0:T(8,128)S(1)} collective-permute-done((f32[8,256]{1,0:T(8,128)S(1)}, f32[8,256]{1,0:T(8,128)S(1)}, u32[]{:S(2)}, u32[]{:S(2)}) %collective-permute-start.8) | collective-permute-done | bytes 8224 | tf_op jit(solution)/shard_map/ppermute | solution.py:318
  65.1 2.6 %collective-permute-start.9 = (f32[8,256]{1,0:T(8,128)S(1)}, f32[8,256]{1,0:T(8,128)S(1)}, u32[]{:S(2)}, u32[]{:S(2)}) collective-permute-start(f32[8,256]{1,0:T(8,128)S(1)} %pad_maximum_fusion.5), channel_id=1, source_target_pairs={{0,4},{1,5},{2,6},{3,7},{4,0},{5,1},{6,2},{7,3},{8,12},{9,13},{10,... | collective-permute-start | bytes 24584 | tf_op jit(solution)/shard_map/ppermute | solution.py:318
  67.7 2.0 %collective-permute-done.9 = f32[8,256]{1,0:T(8,128)S(1)} collective-permute-done((f32[8,256]{1,0:T(8,128)S(1)}, f32[8,256]{1,0:T(8,128)S(1)}, u32[]{:S(2)}, u32[]{:S(2)}) %collective-permute-start.9) | collective-permute-done | bytes 8224 | tf_op jit(solution)/shard_map/ppermute | solution.py:318
  69.8 1.2 copy-done.4
  71.0 1.1 copy-done.6
  72.1 0.9 copy-done.12
  73.1 0.9 copy-done.14
  74.0 0.9 copy-done.16
  75.0 0.9 copy-done.18
  75.9 0.9 copy-done.20
  76.8 3.3 %middle.1 = (bf16[64,256]{1,0:T(8,128)(2,1)}, f32[8,160,256]{2,1,0:T(8,128)S(1)}, bf16[8,160,256]{2,1,0:T(8,128)(2,1)S(1)}, bf16[16,256]{1,0:T(8,128)(2,1)S(1)}) custom-call(s32[2]{0:T(128)S(1)} %pad_add_fusion.place_ref, bf16[512,256]{1,0:T(8,128)(2,1)S(1)} %copy-done.16, bf16[512,256]{1,0:T(8,128)(2,1)S(1)} %copy-done.18, bf16[512,256]{1,0:T(8,128)(2,1)S(1)} %copy-done.12, ...), custom_call_target="tpu_custom_call" | custom-call | tf_op jit(solution)/shard_map/middle/pallas_call | solution.py:445
  80.1 0.1 collective-permute-start.11
  80.2 0.5 collective-permute-start.12
  80.7 1.6 %collective-permute-done.12.got_sums_ref = bf16[16,256]{1,0:T(8,128)(2,1)S(1)} collective-permute-done((bf16[16,256]{1,0:T(8,128)(2,1)S(1)}, bf16[16,256]{1,0:T(8,128)(2,1)S(1)}, u32[]{:S(2)}, u32[]{:S(2)}) %collective-permute-start.12) | collective-permute-done | bytes 8224 | tf_op jit(solution)/shard_map/ppermute | solution.py:318
  82.3 1.0 merge.1
  83.3 5.8 %all-to-all-start = ((bf16[8,176,256]{2,1,0:T(8,128)(2,1)}), bf16[8,176,256]{2,1,0:T(8,128)(2,1)S(1)}, u32[]{:S(2)}, u32[]{:S(2)}) async-start(bf16[8,176,256]{2,1,0:T(8,128)(2,1)} %merge.1), calls=%async_computation | async-start | bytes 1441792 | tf_op jit(solution)/shard_map/all_to_all | solution.py:468
  89.1 0.1 constant_dynamic-slice_fusion
  89.2 0.1 reshape.64
  89.3 18.9 %all-to-all-done.parts_ref = bf16[8,176,256]{2,1,0:T(8,128)(2,1)S(1)} async-done(((bf16[8,176,256]{2,1,0:T(8,128)(2,1)}), bf16[8,176,256]{2,1,0:T(8,128)(2,1)S(1)}, u32[]{:S(2)}, u32[]{:S(2)}) %all-to-all-start) | async-done | bytes 720928 | tf_op jit(solution)/shard_map/all_to_all | solution.py:468
  108.2 0.8 finish.1
  109.0 5.4 %collective-permute-done.13 = bf16[1,96,256]{2,1,0:T(8,128)(2,1)S(1)} collective-permute-done((bf16[1,96,256]{2,1,0:T(8,128)(2,1)S(1)}, bf16[1,96,256]{2,1,0:T(8,128)(2,1)S(1)}, u32[]{:S(2)}, u32[]{:S(2)}) %collective-permute-start.13) | collective-permute-done | bytes 49184 | tf_op jit(solution)/shard_map/ppermute | solution.py:318
  114.4 0.1 collective-permute-start.14
  114.5 4.5 %collective-permute-done.14 = bf16[2,96,256]{2,1,0:T(8,128)(2,1)S(1)} collective-permute-done((bf16[2,96,256]{2,1,0:T(8,128)(2,1)S(1)}, bf16[2,96,256]{2,1,0:T(8,128)(2,1)S(1)}, u32[]{:S(2)}, u32[]{:S(2)}) %collective-permute-start.14) | collective-permute-done | bytes 98336 | tf_op jit(solution)/shard_map/ppermute | solution.py:318
  119.1 1.1 collective-permute-start.15
  120.2 4.7 %collective-permute-done.15 = bf16[4,96,256]{2,1,0:T(8,128)(2,1)S(1)} collective-permute-done((bf16[4,96,256]{2,1,0:T(8,128)(2,1)S(1)}, bf16[4,96,256]{2,1,0:T(8,128)(2,1)S(1)}, u32[]{:S(2)}, u32[]{:S(2)}) %collective-permute-start.15) | collective-permute-done | bytes 196640 | tf_op jit(solution)/shard_map/ppermute | solution.py:318
  124.9 0.8 place.1
  125.7 1.5 %collective-permute-done.16 = f32[256,256]{1,0:T(8,128)S(1)} collective-permute-done((f32[256,256]{1,0:T(8,128)S(1)}, f32[256,256]{1,0:T(8,128)S(1)}, u32[]{:S(2)}, u32[]{:S(2)}) %collective-permute-start.16) | collective-permute-done | bytes 262176 | tf_op jit(solution)/shard_map/ppermute | solution.py:318
  127.3 0.8 broadcast_select_fusion
  (81 shorter events, 0.4 us)
Async XLA Ops:
  0.6 14.9 %collective-permute-start = (bf16[4096,256]{1,0:T(8,128)(2,1)}, bf16[4096,256]{1,0:T(8,128)(2,1)}, u32[]{:S(2)}, u32[]{:S(2)}) collective-permute-start(bf16[4096,256]{1,0:T(8,128)(2,1)} %own_ref.5), channel_id=1, source_target_pairs={{0,8},{8,0},{16,24},{24,16},{1,9},{9,1},{17,25},{25,17},{2,10},{10... | collective-permute-start | bytes 6291464 | tf_op jit(solution)/shard_map/ppermute | solution.py:318
  1.1 13.7 %collective-permute-start.1 = (bf16[256,256]{1,0:T(8,128)(2,1)}, bf16[256,256]{1,0:T(8,128)(2,1)S(1)}, u32[]{:S(2)}, u32[]{:S(2)}) collective-permute-start(bf16[256,256]{1,0:T(8,128)(2,1)} %self_own_ref.5), channel_id=1, source_target_pairs={{0,8},{8,0},{16,24},{24,16},{1,9},{9,1},{17,25},{25,17},{2,10},{10... | collective-permute-start | bytes 393224 | tf_op jit(solution)/shard_map/ppermute | solution.py:318
  1.2 13.6 %collective-permute-start.2 = (bf16[256,256]{1,0:T(8,128)(2,1)}, bf16[256,256]{1,0:T(8,128)(2,1)S(1)}, u32[]{:S(2)}, u32[]{:S(2)}) collective-permute-start(bf16[256,256]{1,0:T(8,128)(2,1)} %neigh_own_ref.5), channel_id=1, source_target_pairs={{0,8},{8,0},{16,24},{24,16},{1,9},{9,1},{17,25},{25,17},{2,10},{10... | collective-permute-start | bytes 393224 | tf_op jit(solution)/shard_map/ppermute | solution.py:318
  4.8 9.8 %copy-start.26 = (s32[256]{0:T(256)S(1)}, s32[256]{0:T(256)}, u32[]{:S(2)}) copy-start(s32[256]{0:T(256)} %param.12) | copy-start | bytes 3076
  4.8 10.7 %copy-start.2 = (bf16[4096,256]{1,0:T(8,128)(2,1)S(1)}, bf16[4096,256]{1,0:T(8,128)(2,1)}, u32[]{:S(2)}) copy-start(bf16[4096,256]{1,0:T(8,128)(2,1)} %own_ref.5) | copy-start | bytes 6291460
  4.8 10.7 %copy-start.7 = (bf16[256,256]{1,0:T(8,128)(2,1)S(1)}, bf16[256,256]{1,0:T(8,128)(2,1)}, u32[]{:S(2)}) copy-start(bf16[256,256]{1,0:T(8,128)(2,1)} %self_own_ref.5) | copy-start | bytes 393220
  4.9 10.7 %copy-start.8 = (bf16[256,256]{1,0:T(8,128)(2,1)S(1)}, bf16[256,256]{1,0:T(8,128)(2,1)}, u32[]{:S(2)}) copy-start(bf16[256,256]{1,0:T(8,128)(2,1)} %neigh_own_ref.5) | copy-start | bytes 393220
  10.3 4.3 %copy-start = (bf16[1408,4096]{1,0:T(8,128)(2,1)}, bf16[1408,4096]{1,0:T(8,128)(2,1)S(1)}, u32[]{:S(2)}) copy-start(bf16[1408,4096]{1,0:T(8,128)(2,1)S(1)} %count_rows.1.count_ref) | copy-start | bytes 34603012
  14.8 0.7 copy-start.9
  15.5 4.3 %copy-start.1 = (bf16[1408,4096]{1,0:T(8,128)(2,1)S(1)}, bf16[1408,4096]{1,0:T(8,128)(2,1)}, u32[]{:S(2)}) copy-start(bf16[1408,4096]{1,0:T(8,128)(2,1)} %copy-done) | copy-start | bytes 34603012
  19.8 0.9 copy-start.10
  29.3 25.6 %copy-start.11 = (bf16[512,256]{1,0:T(8,128)(2,1)}, bf16[512,256]{1,0:T(8,128)(2,1)S(1)}, u32[]{:S(2)}) copy-start(bf16[512,256]{1,0:T(8,128)(2,1)S(1)} %get-tuple-element.26.refs_2_) | copy-start | bytes 786436
  29.3 25.5 %collective-permute-start.4 = (bf16[512,256]{1,0:T(8,128)(2,1)S(1)}, bf16[512,256]{1,0:T(8,128)(2,1)S(1)}, u32[]{:S(2)}, u32[]{:S(2)}) collective-permute-start(bf16[512,256]{1,0:T(8,128)(2,1)S(1)} %get-tuple-element.26.refs_2_), channel_id=1, source_target_pairs={{0,16},{8,24},{16,0},{24,8},{1,17},{9,25},{17,1},{25,9},{2,18},{10... | collective-permute-start | bytes 786440 | tf_op jit(solution)/shard_map/ppermute | solution.py:318
  40.5 14.4 %copy-start.3 = (bf16[1024,512]{1,0:T(8,128)(2,1)}, bf16[1024,512]{1,0:T(8,128)(2,1)S(1)}, u32[]{:S(2)}) copy-start(bf16[1024,512]{1,0:T(8,128)(2,1)S(1)} %get-tuple-element.28.refs_6_) | copy-start | bytes 3145732
  40.5 14.4 %copy-start.15 = (bf16[512,256]{1,0:T(8,128)(2,1)}, bf16[512,256]{1,0:T(8,128)(2,1)S(1)}, u32[]{:S(2)}) copy-start(bf16[512,256]{1,0:T(8,128)(2,1)S(1)} %get-tuple-element.25.refs_0_) | copy-start | bytes 786436
  40.5 14.4 %collective-permute-start.3 = (bf16[512,256]{1,0:T(8,128)(2,1)S(1)}, bf16[512,256]{1,0:T(8,128)(2,1)S(1)}, u32[]{:S(2)}, u32[]{:S(2)}) collective-permute-start(bf16[512,256]{1,0:T(8,128)(2,1)S(1)} %get-tuple-element.25.refs_0_), channel_id=1, source_target_pairs={{0,16},{8,24},{16,0},{24,8},{1,17},{9,25},{17,1},{25,9},{2,18},{10... | collective-permute-start | bytes 786440 | tf_op jit(solution)/shard_map/ppermute | solution.py:318
  47.8 8.2 %copy-start.5 = (bf16[1024,384]{1,0:T(8,128)(2,1)}, bf16[1024,384]{1,0:T(8,128)(2,1)S(1)}, u32[]{:S(2)}) copy-start(bf16[1024,384]{1,0:T(8,128)(2,1)S(1)} %get-tuple-element.30.refs_8_) | copy-start | bytes 2359300
  47.8 8.2 %copy-start.19 = (bf16[384,256]{1,0:T(8,128)(2,1)}, bf16[384,256]{1,0:T(8,128)(2,1)S(1)}, u32[]{:S(2)}) copy-start(bf16[384,256]{1,0:T(8,128)(2,1)S(1)} %get-tuple-element.27.refs_4_) | copy-start | bytes 589828
  47.8 7.0 %collective-permute-start.5 = (bf16[384,256]{1,0:T(8,128)(2,1)S(1)}, bf16[384,256]{1,0:T(8,128)(2,1)S(1)}, u32[]{:S(2)}, u32[]{:S(2)}) collective-permute-start(bf16[384,256]{1,0:T(8,128)(2,1)S(1)} %get-tuple-element.27.refs_4_), channel_id=1, source_target_pairs={{0,16},{8,24},{16,0},{24,8},{1,17},{9,25},{17,1},{25,9},{2,18},{10... | collective-permute-start | bytes 589832 | tf_op jit(solution)/shard_map/ppermute | solution.py:318
  54.8 1.2 copy-start.13
  54.8 1.2 copy-start.17
  54.9 1.2 copy-start.25
  54.9 14.8 %copy-start.21 = (bf16[256,256]{1,0:T(8,128)(2,1)S(1)}, bf16[256,256]{1,0:T(8,128)(2,1)}, u32[]{:S(2)}) copy-start(bf16[256,256]{1,0:T(8,128)(2,1)} %refs_12_.1) | copy-start | bytes 393220
  54.9 14.8 %copy-start.22 = (bf16[256,256]{1,0:T(8,128)(2,1)S(1)}, bf16[256,256]{1,0:T(8,128)(2,1)}, u32[]{:S(2)}) copy-start(bf16[256,256]{1,0:T(8,128)(2,1)} %refs_13_.1) | copy-start | bytes 393220
  54.9 14.8 %copy-start.23 = (f32[256]{0:T(256)S(1)}, f32[256]{0:T(256)}, u32[]{:S(2)}) copy-start(f32[256]{0:T(256)} %param.17) | copy-start | bytes 3076
  54.9 14.8 %copy-start.24 = (f32[256]{0:T(256)S(1)}, f32[256]{0:T(256)}, u32[]{:S(2)}) copy-start(f32[256]{0:T(256)} %param.18) | copy-start | bytes 3076
  56.0 1.5 %collective-permute-start.6 = (f32[8,256]{1,0:T(8,128)S(1)}, f32[8,256]{1,0:T(8,128)S(1)}, u32[]{:S(2)}, u32[]{:S(2)}) collective-permute-start(f32[8,256]{1,0:T(8,128)S(1)} %get-tuple-element.32), channel_id=1, source_target_pairs={{0,8},{8,0},{16,24},{24,16},{1,9},{9,1},{17,25},{25,17},{2,10},{10... | collective-permute-start | bytes 24584 | tf_op jit(solution)/shard_map/ppermute | solution.py:318
  56.1 11.6 %collective-permute-start.10 = (bf16[64,256]{1,0:T(8,128)(2,1)S(1)}, bf16[64,256]{1,0:T(8,128)(2,1)S(1)}, u32[]{:S(2)}, u32[]{:S(2)}) collective-permute-start(bf16[64,256]{1,0:T(8,128)(2,1)S(1)} %copy-done.25), channel_id=1, source_target_pairs={{0,16},{8,24},{16,0},{24,8},{1,17},{9,25},{17,1},{25,9},{2,18},{10... | collective-permute-start | bytes 98312 | tf_op jit(solution)/shard_map/ppermute | solution.py:318
  57.6 3.7 %collective-permute-start.7 = (f32[8,256]{1,0:T(8,128)S(1)}, f32[8,256]{1,0:T(8,128)S(1)}, u32[]{:S(2)}, u32[]{:S(2)}) collective-permute-start(f32[8,256]{1,0:T(8,128)S(1)} %pad_maximum_fusion.3), channel_id=1, source_target_pairs={{0,1},{1,0},{2,3},{3,2},{4,5},{5,4},{6,7},{7,6},{8,9},{9,8},{10,11... | collective-permute-start | bytes 24584 | tf_op jit(solution)/shard_map/ppermute | solution.py:318
  61.3 3.7 %collective-permute-start.8 = (f32[8,256]{1,0:T(8,128)S(1)}, f32[8,256]{1,0:T(8,128)S(1)}, u32[]{:S(2)}, u32[]{:S(2)}) collective-permute-start(f32[8,256]{1,0:T(8,128)S(1)} %pad_maximum_fusion.4), channel_id=1, source_target_pairs={{0,2},{1,3},{2,0},{3,1},{4,6},{5,7},{6,4},{7,5},{8,10},{9,11},{10,... | collective-permute-start | bytes 24584 | tf_op jit(solution)/shard_map/ppermute | solution.py:318
  65.1 4.6 %collective-permute-start.9 = (f32[8,256]{1,0:T(8,128)S(1)}, f32[8,256]{1,0:T(8,128)S(1)}, u32[]{:S(2)}, u32[]{:S(2)}) collective-permute-start(f32[8,256]{1,0:T(8,128)S(1)} %pad_maximum_fusion.5), channel_id=1, source_target_pairs={{0,4},{1,5},{2,6},{3,7},{4,0},{5,1},{6,2},{7,3},{8,12},{9,13},{10,... | collective-permute-start | bytes 24584 | tf_op jit(solution)/shard_map/ppermute | solution.py:318
  69.7 1.2 copy-start.4
  71.0 1.1 copy-start.6
  72.1 0.9 copy-start.12
  73.1 0.9 copy-start.14
  74.0 0.9 copy-start.16
  75.0 0.9 copy-start.18
  75.9 0.9 copy-start.20
  80.1 2.2 %collective-permute-start.11 = (bf16[8,160,256]{2,1,0:T(8,128)(2,1)S(1)}, bf16[8,160,256]{2,1,0:T(8,128)(2,1)S(1)}, u32[]{:S(2)}, u32[]{:S(2)}) collective-permute-start(bf16[8,160,256]{2,1,0:T(8,128)(2,1)S(1)} %get-tuple-element.35), channel_id=1, source_target_pairs={{0,8},{8,0},{16,24},{24,16},{1,9},{9,1},{17,25},{25,17},{2,10},{10... | collective-permute-start | bytes 1966088 | tf_op jit(solution)/shard_map/ppermute | solution.py:318
  80.2 2.1 %collective-permute-start.12 = (bf16[16,256]{1,0:T(8,128)(2,1)S(1)}, bf16[16,256]{1,0:T(8,128)(2,1)S(1)}, u32[]{:S(2)}, u32[]{:S(2)}) collective-permute-start(bf16[16,256]{1,0:T(8,128)(2,1)S(1)} %get-tuple-element.36.sums_ref), channel_id=1, source_target_pairs={{0,8},{8,0},{16,24},{24,16},{1,9},{9,1},{17,25},{25,17},{2,10},{10... | collective-permute-start | bytes 24584 | tf_op jit(solution)/shard_map/ppermute | solution.py:318
  83.3 24.9 %all-to-all-start = ((bf16[8,176,256]{2,1,0:T(8,128)(2,1)}), bf16[8,176,256]{2,1,0:T(8,128)(2,1)S(1)}, u32[]{:S(2)}, u32[]{:S(2)}) async-start(bf16[8,176,256]{2,1,0:T(8,128)(2,1)} %merge.1), calls=%async_computation | async-start | bytes 1441792 | tf_op jit(solution)/shard_map/all_to_all | solution.py:468
  109.0 5.4 %collective-permute-start.13 = (bf16[1,96,256]{2,1,0:T(8,128)(2,1)S(1)}, bf16[1,96,256]{2,1,0:T(8,128)(2,1)S(1)}, u32[]{:S(2)}, u32[]{:S(2)}) collective-permute-start(bf16[1,96,256]{2,1,0:T(8,128)(2,1)S(1)} %bitcast.21), channel_id=1, source_target_pairs={{0,4},{1,5},{2,6},{3,7},{4,0},{5,1},{6,2},{7,3},{8,12},{9,13},{10,... | collective-permute-start | bytes 147464 | tf_op jit(solution)/shard_map/ppermute | solution.py:318
  114.4 4.7 %collective-permute-start.14 = (bf16[2,96,256]{2,1,0:T(8,128)(2,1)S(1)}, bf16[2,96,256]{2,1,0:T(8,128)(2,1)S(1)}, u32[]{:S(2)}, u32[]{:S(2)}) collective-permute-start(bf16[2,96,256]{2,1,0:T(8,128)(2,1)S(1)} %pad_maximum_fusion.2), channel_id=1, source_target_pairs={{0,2},{1,3},{2,0},{3,1},{4,6},{5,7},{6,4},{7,5},{8,10},{9,11},{10,... | collective-permute-start | bytes 294920 | tf_op jit(solution)/shard_map/ppermute | solution.py:318
  119.1 5.7 %collective-permute-start.15 = (bf16[4,96,256]{2,1,0:T(8,128)(2,1)S(1)}, bf16[4,96,256]{2,1,0:T(8,128)(2,1)S(1)}, u32[]{:S(2)}, u32[]{:S(2)}) collective-permute-start(bf16[4,96,256]{2,1,0:T(8,128)(2,1)S(1)} %pad_maximum_fusion.1), channel_id=1, source_target_pairs={{0,1},{1,0},{2,3},{3,2},{4,5},{5,4},{6,7},{7,6},{8,9},{9,8},{10,11... | collective-permute-start | bytes 589832 | tf_op jit(solution)/shard_map/ppermute | solution.py:318
  125.7 1.5 %collective-permute-start.16 = (f32[256,256]{1,0:T(8,128)S(1)}, f32[256,256]{1,0:T(8,128)S(1)}, u32[]{:S(2)}, u32[]{:S(2)}) collective-permute-start(f32[256,256]{1,0:T(8,128)S(1)} %get-tuple-element.40), channel_id=1, source_target_pairs={{0,8},{8,0},{16,24},{24,16},{1,9},{9,1},{17,25},{25,17},{2,10},{10... | collective-permute-start | bytes 786440 | tf_op jit(solution)/shard_map/ppermute | solution.py:318

commit v2 on v1

v2 whole, which is shorter than its diff:
```python
import functools

import jax
import jax.numpy as jnp
from jax import lax
from jax.experimental import pallas as pl
from jax.experimental.pallas import tpu as pltpu
from jax.sharding import PartitionSpec as P

BF = jnp.bfloat16
F32 = jnp.float32
LANES = 128
LOW = 256
SLOT = 16
GROUP = LOW // SLOT
MIB = 2**20


def dot(left, right, dims=((1,), (0,)), precision=None):
    return lax.dot_general(
        left, right, (dims, ((), ())), preferred_element_type=F32, precision=precision
    )


def params(mib):
    return pltpu.CompilerParams(vmem_limit_bytes=mib * MIB)


VMEM = pl.BlockSpec(memory_space=pltpu.VMEM)
SMEM = pl.BlockSpec(memory_space=pltpu.SMEM)
HBM = pl.BlockSpec(memory_space=pltpu.HBM)


def halves(value):
    high = value.astype(BF)
    return high, (value - high.astype(F32)).astype(BF)


def build_kernel(
    place_ref,
    seed_in,
    near_in,
    far_in,
    out_ref,
    seed_ref,
    near_ref,
    far_ref,
    keys,
    own_group,
    spread,
    own_slot,
    sems,
):
    groups = LANES // GROUP
    per_slot = seed_ref.shape[1] // (2 * LANES)
    step, steps = pl.program_id(0), pl.num_programs(0)
    first_core = place_ref[1] == 0

    def mine(ids, p):
        parts = []
        for q in range(per_slot):
            left = ids[:, 2 * q * LANES : (2 * q + 1) * LANES]
            right = ids[:, (2 * q + 1) * LANES : (2 * q + 2) * LANES]
            low_half = lax.broadcasted_iota(jnp.int32, left.shape, 1) < LANES // 2
            even = jnp.where(low_half, left, pltpu.roll(right, LANES // 2, 1))
            odd = jnp.where(low_half, pltpu.roll(left, LANES // 2, 1), right)
            parts.append(jnp.where(first_core, even, odd))
        part = parts[0]
        for q in range(1, per_slot):
            part = jnp.where(p == q, parts[q], part)
        return part

    def flag(shape, test):
        row = lax.broadcasted_iota(jnp.int32, shape, 0)
        lane = lax.broadcasted_iota(jnp.int32, shape, 1)
        return jnp.where(test(row, lane), 1.0, 0.0).astype(BF)

    def widen(part):
        tiled = jnp.concatenate([part.astype(F32).astype(BF)] * groups, axis=0) * own_group[...]
        return dot(tiled, spread[...]).astype(BF) * own_slot[...]

    def wide_of(ids, self_row, p):
        part = mine(ids, p)
        gap = SLOT - part.shape[0]
        part = jnp.concatenate([part, jnp.full((gap, LANES), -1, jnp.int32)], axis=0)
        own = mine(jnp.broadcast_to(self_row, (8, self_row.shape[1])), p).astype(F32)
        high = widen(lax.shift_right_arithmetic(part, 8))
        return high, widen(jnp.bitwise_and(part, LOW - 1)), jnp.concatenate([own, own], axis=1)

    def keys_of(high, low, own):
        gather = flag((groups, LANES), lambda r, c: r == c // SLOT)
        in_group = (lax.broadcasted_iota(jnp.int32, (groups, LOW), 1) % GROUP).astype(F32)
        return dot(gather, high) * GROUP + in_group, dot(gather, low), own

    def keep(values, at):
        for j, value in enumerate(values):
            keys[at, j, :, :] = value

    @pl.when(step == 0)
    def _():
        copies = [
            pltpu.make_async_copy(a, b, sems.at[i])
            for i, (a, b) in enumerate(((seed_in, seed_ref), (near_in, near_ref), (far_in, far_ref)))
        ]
        for copy in copies:
            copy.start()
        own_group[...] = flag((LANES, LANES), lambda r, c: r // SLOT == c // GROUP)
        spread[...] = flag((LANES, LOW), lambda r, c: r % GROUP == c % GROUP)
        own_slot[...] = flag((LANES, LOW), lambda r, c: r % SLOT == c // GROUP)
        for copy in copies:
            copy.wait()
        keep(keys_of(*wide_of(near_ref[...], seed_ref[...], 0)), 0)

    now = step % 2
    later = jnp.minimum(step + 1, steps - 1)
    slot = later // per_slot
    back = jnp.maximum(slot - 1, 0)
    ids = far_ref[back, :, :]
    self_row = near_ref[pl.ds(back, 1), :]
    if per_slot > 1:
        padded = jnp.concatenate(
            [near_ref[...], jnp.full((ids.shape[0] - near_ref.shape[0], ids.shape[1]), -1, jnp.int32)]
        )
        ids = jnp.where(slot == 0, padded, ids)
        self_row = jnp.where(slot == 0, seed_ref[...], self_row)
    later_wide = wide_of(ids, self_row, later % per_slot)

    index = lax.broadcasted_iota(jnp.int32, (LOW, LOW), 0).astype(BF)
    one = jnp.ones((LOW, LOW), BF)
    zero = jnp.zeros((LOW, LOW), BF)
    def store(g, counts):
        counts = counts.astype(BF)
        for h in range(LOW // GROUP):
            out_ref[g * GROUP : (g + 1) * GROUP, h * LOW : (h + 1) * LOW] = counts[
                h * GROUP : (h + 1) * GROUP, :
            ]

    lanes = lax.broadcasted_iota(jnp.int32, (LANES, LANES), 1)
    ids = jnp.broadcast_to(keys[now, 2, 0:1, :LANES], (LANES, LANES)).T.astype(jnp.int32)
    low = jnp.bitwise_and(ids, LOW - 1)
    high = lax.shift_right_logical(ids, 8).astype(BF)
    bases = [
        jnp.where(lanes + LANES * part == low, 1.0, 0.0).astype(BF) for part in range(LOW // LANES)
    ]
    tiles = [(h, part) for h in range(out_ref.shape[1] // LOW) for part in range(LOW // LANES)]
    share = -(-len(tiles) // groups)
    waiting = []
    later_keys = None
    for g in range(groups):
        left = jnp.where(index == keys[now, 0, g : g + 1, :].astype(BF), one, zero)
        right = jnp.where(index == keys[now, 1, g : g + 1, :].astype(BF), one, zero)
        waiting.append((g, dot(left, right, ((1,), (1,)))))
        if g == 6:
            later_keys = keys_of(*later_wide)
        for h, part in tiles[g * share : (g + 1) * share]:
            at = h * LOW + part * LANES
            out_ref[LANES:, at : at + LANES] = jnp.where(
                high == BF(h), bases[part], jnp.zeros_like(bases[part])
            )
        if len(waiting) > 1:
            store(*waiting.pop(0))
    for item in waiting:
        store(*item)
    keep(later_keys, 1 - now)


def build_rows(place, seeds, near, far, table_rows):
    steps = (near.shape[0] + 1) * seeds.shape[1] // (2 * LANES)
    groups = LANES // GROUP
    return pl.pallas_call(
        build_kernel,
        grid=(steps,),
        in_specs=[SMEM, HBM, HBM, HBM],
        out_specs=pl.BlockSpec((2 * LANES, table_rows), lambda i: (i, 0)),
        out_shape=jax.ShapeDtypeStruct((steps * 2 * LANES, table_rows), BF),
        scratch_shapes=[
            pltpu.VMEM(seeds.shape, jnp.int32),
            pltpu.VMEM(near.shape, jnp.int32),
            pltpu.VMEM(far.shape, jnp.int32),
            pltpu.VMEM((2, 3, groups, LOW), F32),
            pltpu.VMEM((LANES, LANES), BF),
            pltpu.VMEM((LANES, LOW), BF),
            pltpu.VMEM((LANES, LOW), BF),
            pltpu.SemaphoreType.DMA((3,)),
        ],
        compiler_params=params(12),
        cost_estimate=pl.CostEstimate(
            flops=2 * steps * groups * LOW**3,
            bytes_accessed=4 * steps * LANES * table_rows,
            transcendentals=0,
        ),
        name="build_rows",
    )(place, seeds, near, far)


def pick_kernel(
    first_block,
    start,
    blocks,
    per_slot,
    fans,
    rows_ref,
    own_ref,
    peer_ref,
    self_own_ref,
    self_peer_ref,
    neigh_own_ref,
    neigh_peer_ref,
    across_ref,
    pre_ref,
    column_ref,
    peer,
    sem,
):
    width = own_ref.shape[1]
    step = pl.program_id(0)
    fetch = pltpu.make_async_copy(peer_ref, peer, sem)

    @pl.when(step == 0)
    def _():
        fetch.start()

    total = None
    columns = []
    for i, (table, weight_self, weight_neigh) in enumerate(
        ((own_ref, self_own_ref, neigh_own_ref), (peer, self_peer_ref, neigh_peer_ref))
    ):
        if i == 1:

            @pl.when(step == 0)
            def _():
                fetch.wait()

        self_parts, neigh_parts = [], []
        for b in range(blocks):
            block = first_block + step * blocks + b
            share = jnp.where(block < per_slot, F32(1.0 / fans[0]), F32(1.0 / fans[1]))
            at = start + 2 * b * LANES
            picked = dot(rows_ref[at : at + 2 * LANES, :], table[...])
            neigh_parts.append((picked[:LANES] * share).astype(BF))
            self_parts.append(picked[LANES:].astype(BF))
        for j, parts in enumerate((self_parts, neigh_parts)):
            features = jnp.concatenate(parts, axis=0)
            part = dot(features, (weight_self, weight_neigh)[j][...])
            total = part if total is None else total + part
            columns.append(dot(jnp.ones((8, features.shape[0]), BF), features))
            for b in range(blocks):
                across_ref[
                    (2 * i + j) * width : (2 * i + j + 1) * width, b * LANES : (b + 1) * LANES
                ] = parts[b].T
    pre_ref[...] = total.astype(BF)
    columns = jnp.concatenate(columns, axis=1)

    @pl.when(step == 0)
    def _():
        column_ref[...] = columns

    @pl.when(step > 0)
    def _():
        column_ref[...] += columns


def pick_rows(first_block, count, rows, own, peer, weights, per_slot, fans):
    table_rows, width = own.shape
    hidden_width = weights[0].shape[1]
    total = count * LANES
    resident = rows.size * 2 <= 32 * MIB
    if resident:
        blocks, start, rows_spec = count, first_block * 2 * LANES, VMEM
    else:
        blocks, start = per_slot, 0
        skip = first_block // blocks
        rows_spec = pl.BlockSpec((blocks * 2 * LANES, table_rows), lambda i: (i + skip, 0))
    return pl.pallas_call(
        functools.partial(pick_kernel, first_block, start, blocks, per_slot, fans),
        grid=(count // blocks,),
        in_specs=[rows_spec, VMEM, HBM] + [VMEM] * 4,
        out_specs=[
            pl.BlockSpec((4 * width, blocks * LANES), lambda i: (0, i)),
            pl.BlockSpec((blocks * LANES, hidden_width), lambda i: (i, 0)),
            pl.BlockSpec((8, 4 * width), lambda i: (0, 0)),
        ],
        out_shape=[
            jax.ShapeDtypeStruct((4 * width, total), BF),
            jax.ShapeDtypeStruct((total, hidden_width), BF),
            jax.ShapeDtypeStruct((8, 4 * width), F32),
        ],
        scratch_shapes=[
            pltpu.VMEM(peer.shape, BF),
            pltpu.SemaphoreType.DMA,
        ],
        compiler_params=params(16 if resident else 24),
        cost_estimate=pl.CostEstimate(
            flops=8 * total * table_rows * width,
            bytes_accessed=2 * total * table_rows + 4 * table_rows * width,
            transcendentals=0,
        ),
        name="pick_rows",
    )(rows, own, peer, *weights)


def stats_kernel(chunks, *refs):
    pairs, columns = refs[: 2 * chunks], refs[2 * chunks : 3 * chunks]
    keep_ref, send_ref, total = refs[3 * chunks :]
    width = columns[0].shape[1] // 4
    rows = total.shape[0]
    mean = 0.0
    first = 0
    for i in range(chunks):
        value = pairs[2 * i][...].astype(F32) + pairs[2 * i + 1][...].astype(F32)
        total[first : first + value.shape[0], :] = value
        mean = mean + jnp.sum(value, axis=0, keepdims=True)
        first += value.shape[0]
    mean = mean / rows
    gap = total[...] - mean
    square = jnp.sum(gap * gap, axis=0, keepdims=True)
    column = sum(c[0:1, :] for c in columns)
    pad = jnp.zeros((4, mean.shape[1]), F32)
    lanes = mean.shape[1] - width
    for ref, first in ((keep_ref, 0), (send_ref, 2)):
        parts = [column[:, (first + j) * width : (first + j + 1) * width] for j in range(2)]
        if lanes:
            parts = [jnp.concatenate([p, jnp.zeros((1, lanes), F32)], axis=1) for p in parts]
        ref[...] = jnp.concatenate([mean, square, *parts, pad], axis=0)


def join_kernel(count, mine_ref, other_ref, out_ref):
    mine, other = mine_ref[...], other_ref[...]
    gap = mine[0:1] - other[0:1]
    out_ref[...] = jnp.concatenate(
        [
            (mine[0:1] + other[0:1]) * 0.5,
            mine[1:2] + other[1:2] + gap * gap * (count * 0.5),
            mine[2:] + other[2:],
        ],
        axis=0,
    )


def joined(mine, other, count):
    return pl.pallas_call(
        functools.partial(join_kernel, count),
        in_specs=[VMEM, VMEM],
        out_specs=VMEM,
        out_shape=jax.ShapeDtypeStruct(mine.shape, mine.dtype),
        compiler_params=params(1),
        name="join",
    )(mine, other)


def middle_kernel(
    chunks,
    slots,
    row_total,
    batches,
    place_ref,
    *refs,
):
    pairs, acrosses = refs[: 2 * chunks], refs[2 * chunks : 3 * chunks]
    chips = len(refs) - 3 * chunks - 12
    grad_parts = refs[3 * chunks : 3 * chunks + chips]
    (
        stats_ref,
        gain_ref,
        shift_ref,
        upper_self_ref,
        upper_neigh_ref,
        embed_ref,
        keep_ref,
        send_ref,
        sums_ref,
        both,
        embed_all,
        grad_all,
    ) = refs[3 * chunks + chips :]
    own_seeds, hidden_width = grad_parts[0].shape
    seeds = own_seeds * chips
    width = acrosses[0].shape[0] // 4
    for mask, part in enumerate(grad_parts):
        at = pl.multiple_of((place_ref[0] ^ mask) * own_seeds, own_seeds)
        grad_all[pl.ds(at, own_seeds), :] = part[...].astype(F32)
    fan_one = slots - 1
    mean = stats_ref[0:1, :]
    inv_std = lax.rsqrt(stats_ref[1:2, :] / row_total + 1e-05)
    gain, shift = gain_ref[...], shift_ref[...]
    grad = grad_all[...].astype(BF)
    d_self = dot(grad, upper_self_ref[...], ((1,), (1,)))
    d_mean = dot(grad, upper_neigh_ref[...], ((1,), (1,))) / fan_one
    gain_sum = shift_sum = hidden_sum = own_rows = None
    places = [(i, k) for i in range(chunks) for k in range(pairs[2 * i].shape[0] // seeds)]
    for slot, (i, k) in enumerate(places):
        span = slice(k * seeds, (k + 1) * seeds)
        pre_act = pairs[2 * i][span, :].astype(F32) + pairs[2 * i + 1][span, :].astype(F32)
        span = slice(slot * seeds, (slot + 1) * seeds)
        normed = (pre_act - mean) * inv_std
        shifted = gain * normed + shift
        sigmoid_v = 1.0 / (1.0 + jnp.exp(-shifted))
        hidden = (shifted * sigmoid_v).astype(BF)
        if slot == 0:
            own_rows = hidden
        else:
            hidden_sum = hidden.astype(F32) + (0.0 if hidden_sum is None else hidden_sum)
        grad_hidden = d_self if slot == 0 else d_mean
        grad_shifted = grad_hidden * sigmoid_v * (1.0 + shifted * (1.0 - sigmoid_v))
        gain_part = grad_shifted * normed
        gain_sum = gain_part if gain_sum is None else gain_sum + gain_part
        shift_sum = grad_shifted if shift_sum is None else shift_sum + grad_shifted
        both[span, :hidden_width] = grad_shifted.astype(BF)
        both[span, hidden_width:] = normed.astype(BF)
    hidden_mean = (hidden_sum / fan_one).astype(BF)
    embed_all[...] = dot(own_rows, upper_self_ref[...]) + dot(hidden_mean, upper_neigh_ref[...])
    start = pl.multiple_of(place_ref[0] * own_seeds, own_seeds)
    embed_ref[...] = embed_all[pl.ds(start, own_seeds), :].astype(BF)
    upper_self_part = dot(own_rows, grad, ((0,), (0,)))
    upper_neigh_part = dot(hidden_mean, grad, ((0,), (0,)))
    first_core = place_ref[1] == 0
    upper_keep = jnp.where(first_core, upper_self_part, upper_neigh_part)
    upper_send = jnp.where(first_core, upper_neigh_part, upper_self_part)
    gain_high, gain_low = halves(jnp.sum(gain_sum, axis=0, keepdims=True))
    shift_high, shift_low = halves(jnp.sum(shift_sum, axis=0, keepdims=True))
    sums = [gain_high, gain_low, shift_high, shift_low]
    sums_ref[...] = jnp.concatenate(
        [s.astype(F32) for s in sums] + [jnp.zeros((12, hidden_width), F32)], axis=0
    ).astype(BF)
    lower = None
    first = 0
    for a in acrosses:
        part = dot(a[...], both[first : first + a.shape[1], :])
        lower = part if lower is None else lower + part
        first += a.shape[1]
    piece, upper_piece = width // batches, hidden_width // batches
    for block, upper, ref in ((0, upper_keep, keep_ref), (2, upper_send, send_ref)):
        for d in range(batches):
            parts = []
            for lane in (0, hidden_width):
                for j in (0, 1):
                    row = (block + j) * width + d * piece
                    parts.append(lower[row : row + piece, lane : lane + hidden_width])
            parts.append(upper[d * upper_piece : (d + 1) * upper_piece, :])
            ref[d, :, :] = jnp.concatenate(parts, axis=0).astype(ref.dtype)


def merge_kernel(keep_ref, got_ref, sums_ref, got_sums_ref, out_ref):
    batches, rows, _ = keep_ref.shape
    mine, theirs = sums_ref[...].astype(F32), got_sums_ref[...].astype(F32)
    sums = []
    for j in (0, 2):
        sums += halves(
            (mine[j : j + 1] + mine[j + 1 : j + 2]) + (theirs[j : j + 1] + theirs[j + 1 : j + 2])
        )
    tail = jnp.concatenate(
        [s.astype(F32) for s in sums] + [jnp.zeros((12, mine.shape[1]), F32)], axis=0
    ).astype(BF)
    for d in range(batches):
        out_ref[d, :rows, :] = (keep_ref[d, :, :] + got_ref[d, :, :].astype(F32)).astype(BF)
        out_ref[d, rows:, :] = tail


def finish_kernel(row_total, parts_ref, stats_ref, gain_ref, column_ref, out_ref, gain_out, shift_out):
    batches, all_rows, _ = parts_ref.shape
    total = parts_ref[0, :, :].astype(F32)
    for d in range(1, batches):
        total = total + parts_ref[d, :, :].astype(F32)
    rows = all_rows - 16
    pieces = column_ref.shape[1]
    grad_gain = total[rows : rows + 1] + total[rows + 1 : rows + 2]
    grad_shift = total[rows + 2 : rows + 3] + total[rows + 3 : rows + 4]
    inv_std = lax.rsqrt(stats_ref[1:2, :] / row_total + 1e-05)
    outer = dot(
        column_ref[...],
        jnp.broadcast_to(grad_shift / row_total, (8, grad_shift.shape[1])),
        ((0,), (0,)),
        lax.Precision.HIGHEST,
    )
    lower = (gain_ref[...] * inv_std) * (
        total[:pieces] - outer - total[pieces : 2 * pieces] * (grad_gain / row_total)
    )
    out_ref[...] = jnp.concatenate([lower, total[2 * pieces : rows]], axis=0).astype(BF)
    gain_out[...] = grad_gain
    shift_out[...] = grad_shift


def place_kernel(masks, group_ref, parts_ref, self_ref, neigh_ref, upper_ref):
    piece = self_ref.shape[0] // len(masks)
    upper_piece = upper_ref.shape[0] // len(masks)
    for i, mask in enumerate(masks):
        d = group_ref[0] ^ mask
        rows = parts_ref[i, :, :].astype(F32)
        self_ref[pl.ds(pl.multiple_of(d * piece, piece), piece), :] = rows[:piece]
        neigh_ref[pl.ds(pl.multiple_of(d * piece, piece), piece), :] = rows[piece : 2 * piece]
        upper_ref[pl.ds(pl.multiple_of(d * upper_piece, upper_piece), upper_piece), :] = rows[
            2 * piece :
        ]


def swap(value, axis, mask):
    return lax.ppermute(value, axis, [(i, i ^ mask) for i in range(lax.axis_size(axis))])


def on_device(
    node_feats,
    seed_ids,
    first_hop,
    second_hop,
    lower_self,
    lower_neighbour,
    norm_gain,
    norm_shift,
    upper_self,
    upper_neighbour,
    embed_grad,
):
    feats, batches = lax.axis_size("feat"), lax.axis_size("batch")
    chips = feats // 2
    feat, batch = lax.axis_index("feat"), lax.axis_index("batch")
    core, chip = feat % 2, feat // 2
    table_rows, width = node_feats.shape
    hidden_width = lower_self.shape[1]
    fan_one, fan_two = first_hop.shape[1], second_hop.shape[2]
    slots = fan_one + 1
    own_seeds = embed_grad.shape[0]
    seeds = own_seeds * chips
    row_total = own_seeds * slots * feats * batches
    rows = seeds * slots

    peer_feats = swap(node_feats, "feat", 1)
    peer_self = swap(lower_self, "feat", 1)
    peer_neigh = swap(lower_neighbour, "feat", 1)
    grads = [embed_grad] + [swap(embed_grad, "feat", 2 * mask) for mask in range(1, chips)]

    place = jnp.stack([chip, core]).astype(jnp.int32)
    picks = build_rows(
        place, seed_ids[None, :], first_hop.T, second_hop.transpose(1, 2, 0), table_rows
    )

    weights = (lower_self, peer_self, lower_neighbour, peer_neigh)
    per_slot = seeds // LANES
    pairs, acrosses, columns = [], [], []
    first = 0
    for share in CHUNKS:
        across, pre_act, column = pick_rows(
            first * per_slot,
            share * per_slot,
            picks,
            node_feats,
            peer_feats,
            weights,
            per_slot,
            (fan_one, fan_two),
        )
        acrosses.append(across)
        columns.append(column)
        mask = 2
        other = swap(pre_act, "feat", mask)
        while 2 * mask < feats:
            mask *= 2
            pre_act = (pre_act.astype(F32) + other.astype(F32)).astype(BF)
            other = swap(pre_act, "feat", mask)
        pairs += [pre_act, other]
        first += share

    tile = jax.ShapeDtypeStruct((8, hidden_width), F32)
    keep, send = pl.pallas_call(
        functools.partial(stats_kernel, len(CHUNKS)),
        out_shape=[tile, tile],
        scratch_shapes=[pltpu.VMEM((rows, hidden_width), F32)],
        compiler_params=params(16),
        name="stats",
    )(*pairs, *columns)

    count = float(rows)
    stats = joined(keep, swap(send, "feat", 1), count)
    mask = 1
    while mask < batches:
        count *= 2
        stats = joined(stats, swap(stats, "batch", mask), count)
        mask *= 2

    gain_row, shift_row = norm_gain[None, :], norm_shift[None, :]
    per_group = 4 * width // batches + hidden_width // batches
    operands = [
        *pairs,
        *acrosses,
        *grads,
        stats,
        gain_row,
        shift_row,
        upper_self,
        upper_neighbour,
    ]
    embedding, keep, send, sums = pl.pallas_call(
        functools.partial(middle_kernel, len(CHUNKS), slots, row_total, batches),
        in_specs=[SMEM] + [VMEM] * len(operands),
        out_shape=[
            jax.ShapeDtypeStruct((own_seeds, hidden_width), BF),
            jax.ShapeDtypeStruct((batches, per_group, hidden_width), F32),
            jax.ShapeDtypeStruct((batches, per_group, hidden_width), BF),
            jax.ShapeDtypeStruct((16, hidden_width), BF),
        ],
        scratch_shapes=[
            pltpu.VMEM((rows, 2 * hidden_width), BF),
            pltpu.VMEM((seeds, hidden_width), F32),
            pltpu.VMEM((seeds, hidden_width), F32),
        ],
        compiler_params=params(24),
        name="middle",
    )(place, *operands)

    parts = pl.pallas_call(
        merge_kernel,
        out_shape=jax.ShapeDtypeStruct((batches, per_group + 16, hidden_width), BF),
        compiler_params=params(16),
        name="merge",
    )(keep, swap(send, "feat", 1), sums, swap(sums, "feat", 1))
    parts = lax.all_to_all(parts, "batch", 0, 0)

    piece = width // batches
    column = lax.dynamic_slice(stats[2:4], (0, batch * piece), (2, piece)).reshape(1, 2 * piece)
    column = jnp.pad(column, ((0, 7), (0, 0)))
    out_rows = 2 * piece + hidden_width // batches
    line = jax.ShapeDtypeStruct((1, hidden_width), F32)
    done, grad_gain, grad_shift = pl.pallas_call(
        functools.partial(finish_kernel, row_total),
        out_shape=[jax.ShapeDtypeStruct((out_rows, hidden_width), BF), line, line],
        compiler_params=params(16),
        name="finish",
    )(parts, stats, gain_row, column)

    gathered, masks = done[None], [0]
    mask = batches // 2
    while mask:
        gathered = jnp.concatenate([gathered, swap(gathered, "batch", mask)], axis=0)
        masks += [m ^ mask for m in masks]
        mask //= 2
    grad_self, grad_neigh, upper = pl.pallas_call(
        functools.partial(place_kernel, tuple(masks)),
        in_specs=[SMEM, VMEM],
        out_shape=[
            jax.ShapeDtypeStruct((width, hidden_width), F32),
            jax.ShapeDtypeStruct((width, hidden_width), F32),
            jax.ShapeDtypeStruct((hidden_width, hidden_width), F32),
        ],
        compiler_params=params(16),
        name="place",
    )(batch.astype(jnp.int32)[None], gathered)
    upper_other = swap(upper, "feat", 1)
    return (
        embedding,
        grad_self,
        grad_neigh,
        jnp.where(core == 0, upper, upper_other),
        jnp.where(core == 0, upper_other, upper),
        grad_gain[0],
        grad_shift[0],
    )


CHUNKS = (3, 2, 2, 2, 2)


def solution(mesh):
    return jax.shard_map(
        on_device,
        mesh=mesh,
        in_specs=(
            P("batch", "feat"),
            P("batch"),
            P("batch", None),
            P("batch", None, None),
            P("feat", None),
            P("feat", None),
            P(),
            P(),
            P(),
            P(),
            P(("batch", "feat"), None),
        ),
        out_specs=(
            P(("batch", "feat"), None),
            P("feat", None),
            P("feat", None),
            P(),
            P(),
            P(),
            P(),
        ),
        check_vma=False,
    )
```

time: 129 us -> 107 us (0.83)
  local copies, waits for them, and re-layouts: 20.7 us -> 2.53 us
  Pallas kernels: 36.7 us -> 33.3 us
  starting transfers between devices: 20.4 us -> 22.6 us
  waiting for transfers between devices: 48 us -> 46.6 us
    unnamed x56 -> x22, local copies, waits for them, and re-layouts: 17.3 us -> 2.35 us
    pallas_call x4 -> x10, Pallas kernels: 29.7 us -> 26.4 us  [the longest x5 17.8 us: pick_rows(): pl.pallas_call(functools.partial(pick_kernel, first_block, start, blocks,...]
    ppermute x17 -> x19, starting transfers between devices: 14.6 us -> 16.7 us  [swap(): lax.ppermute(value, axis, [(i, i ^ mask) for i in range(lax.axis_size(axi...]
    reshape x5 -> x0, local copies, waits for them, and re-layouts: 2.08 us -> none  [the longest x3 1.99 us: mine(): split = ids.reshape(chips, 2, own_seeds, *ids.shape[1:])]
    ppermute x17 -> x19, waiting for transfers between devices: 29.2 us -> 27.8 us  [swap(): lax.ppermute(value, axis, [(i, i ^ mask) for i in range(lax.axis_size(axi...]
  transfers between devices with their start and end apart: 18 -> 20, of which waited for: 10 -> 10; matrix products, arithmetic and copies ran while one was open for 3% -> 0% of each run, Pallas kernels for 17% -> 22%
where the time goes in v2:
time: 107 us
  waiting for transfers between devices  46.6 us (44%)
  Pallas kernels  33.3 us (31%)
  starting transfers between devices  22.6 us (21%)
  local copies, waits for them, and re-layouts  2.53 us (2%)
    ppermute x19, waiting for transfers between devices, swap(): lax.ppermute(value, axis, [(i, i ^ mask) for i in range(lax.axis_size(axi...  27.8 us
    all_to_all x1, waiting for transfers between devices, on_device(): parts = lax.all_to_all(parts, 'batch', 0, 0)  18.9 us
    pallas_call x5, Pallas kernels, pick_rows(): pl.pallas_call(functools.partial(pick_kernel, first_block, start, blocks,...  17.8 us
    ppermute x19, starting transfers between devices, swap(): lax.ppermute(value, axis, [(i, i ^ mask) for i in range(lax.axis_size(axi...  16.7 us
    pallas_call x1, Pallas kernels, build_rows(): pl.pallas_call(build_kernel, grid=(steps,), in_specs=[SMEM, HBM, HBM, HBM...  8.6 us
    all_to_all x1, starting transfers between devices, on_device(): parts = lax.all_to_all(parts, 'batch', 0, 0)  5.84 us
    pallas_call x1, Pallas kernels, on_device(): pl.pallas_call(functools.partial(middle_kernel, len(CHUNKS), slots, row_t...  3.75 us
    unnamed x22, local copies, waits for them, and re-layouts  2.35 us
  transfers between devices with their start and end apart: 20, of which 10 were waited for; matrix products, arithmetic and copies ran while one was open for 0% of the time, Pallas kernels for 22%

profile of v2, /device:TPU:0, one launch (start us, length us, event | category | flops | bytes accessed | tf_op | source)
XLA Modules:
  0.0 106.8 jit_solution(498663914351333636)
XLA Ops:
  0.6 0.5 collective-permute-start
  1.1 0.1 collective-permute-start.1
  1.2 0.4 collective-permute-start.2
  1.7 0.1 pad_add_fusion.place_ref
  1.7 0.9 copy-done.3
  2.7 0.7 copy-done.7
  3.4 0.7 copy-done.9
  4.1 8.6 %build_rows.1.rows_ref = bf16[2816,4096]{1,0:T(8,128)(2,1)S(1)} custom-call(s32[2]{0:T(128)S(1)} %pad_add_fusion.place_ref, s32[1,256]{1,0:T(1,128)S(1)} %bitcast.19, s32[10,256]{1,0:T(8,128)S(1)} %bitcast.16, s32[10,15,256]{2,1,0:T(8,128)S(1)} %bitcast.15), custom_call_target="tpu_custom_call" | custom-call | flops 2952790016 | bytes 23068672 | tf_op jit(solution)/shard_map/build_rows/pallas_call | solution.py:170
  12.7 0.0 collective-permute-done.1.self_peer_ref
  12.7 0.0 collective-permute-done.2.neigh_peer_ref
  12.7 0.0 collective-permute-done.peer_ref
  12.7 0.0 copy-done
  12.7 3.1 %pick_rows.9 = (bf16[1024,256]{1,0:T(8,128)(2,1)S(1)}, bf16[256,256]{1,0:T(8,128)(2,1)S(1)}, f32[8,1024]{1,0:T(8,128)S(1)}) custom-call(bf16[2816,4096]{1,0:T(8,128)(2,1)S(1)} %build_rows.1.rows_ref, bf16[4096,256]{1,0:T(8,128)(2,1)S(1)} %copy-done, bf16[4096,256]{1,0:T(8,128)(2,1)S(1)} %collective-permute-done.peer_ref, bf16[256,256]{1,0:T(8,128)(2,1)S(1)} %copy-done.1, ...), custom_call_target="tpu_custom_call" | custom-call | flops 2147483648 | bytes 6291456 | tf_op jit(solution)/shard_map/pick_rows/pallas_call | solution.py:274
  15.8 2.6 %collective-permute-start.7 = (bf16[256,256]{1,0:T(8,128)(2,1)S(1)}, bf16[256,256]{1,0:T(8,128)(2,1)S(1)}, u32[]{:S(2)}, u32[]{:S(2)}) collective-permute-start(bf16[256,256]{1,0:T(8,128)(2,1)S(1)} %get-tuple-element.38.refs_8_), channel_id=1, source_target_pairs={{0,16},{8,24},{16,0},{24,8},{1,17},{9,25},{17,1},{25,9},{2,18},{10... | collective-permute-start | bytes 393224 | tf_op jit(solution)/shard_map/ppermute | solution.py:497
  18.5 3.1 %pick_rows.8 = (bf16[1024,256]{1,0:T(8,128)(2,1)S(1)}, bf16[256,256]{1,0:T(8,128)(2,1)S(1)}, f32[8,1024]{1,0:T(8,128)S(1)}) custom-call(bf16[2816,4096]{1,0:T(8,128)(2,1)S(1)} %build_rows.1.rows_ref, bf16[4096,256]{1,0:T(8,128)(2,1)S(1)} %copy-done, bf16[4096,256]{1,0:T(8,128)(2,1)S(1)} %collective-permute-done.peer_ref, bf16[256,256]{1,0:T(8,128)(2,1)S(1)} %copy-done.1, ...), custom_call_target="tpu_custom_call" | custom-call | flops 2147483648 | bytes 6291456 | tf_op jit(solution)/shard_map/pick_rows/pallas_call | solution.py:274
  21.6 0.1 collective-permute-start.6
  21.6 3.1 %pick_rows.7 = (bf16[1024,256]{1,0:T(8,128)(2,1)S(1)}, bf16[256,256]{1,0:T(8,128)(2,1)S(1)}, f32[8,1024]{1,0:T(8,128)S(1)}) custom-call(bf16[2816,4096]{1,0:T(8,128)(2,1)S(1)} %build_rows.1.rows_ref, bf16[4096,256]{1,0:T(8,128)(2,1)S(1)} %copy-done, bf16[4096,256]{1,0:T(8,128)(2,1)S(1)} %collective-permute-done.peer_ref, bf16[256,256]{1,0:T(8,128)(2,1)S(1)} %copy-done.1, ...), custom_call_target="tpu_custom_call" | custom-call | flops 2147483648 | bytes 6291456 | tf_op jit(solution)/shard_map/pick_rows/pallas_call | solution.py:274
  24.7 2.1 %collective-permute-start.5 = (bf16[256,256]{1,0:T(8,128)(2,1)S(1)}, bf16[256,256]{1,0:T(8,128)(2,1)S(1)}, u32[]{:S(2)}, u32[]{:S(2)}) collective-permute-start(bf16[256,256]{1,0:T(8,128)(2,1)S(1)} %get-tuple-element.36.refs_4_), channel_id=1, source_target_pairs={{0,16},{8,24},{16,0},{24,8},{1,17},{9,25},{17,1},{25,9},{2,18},{10... | collective-permute-start | bytes 393224 | tf_op jit(solution)/shard_map/ppermute | solution.py:497
  26.8 5.2 %pick_rows.5 = (bf16[1024,384]{1,0:T(8,128)(2,1)S(1)}, bf16[384,256]{1,0:T(8,128)(2,1)S(1)}, f32[8,1024]{1,0:T(8,128)S(1)}) custom-call(bf16[2816,4096]{1,0:T(8,128)(2,1)S(1)} %build_rows.1.rows_ref, bf16[4096,256]{1,0:T(8,128)(2,1)S(1)} %copy-done, bf16[4096,256]{1,0:T(8,128)(2,1)S(1)} %collective-permute-done.peer_ref, bf16[256,256]{1,0:T(8,128)(2,1)S(1)} %copy-done.1, ...), custom_call_target="tpu_custom_call" | custom-call | flops 3221225472 | bytes 7340032 | tf_op jit(solution)/shard_map/pick_rows/pallas_call | solution.py:274
  32.1 0.0 copy-start.6
  32.1 0.0 copy-start.4
  32.1 0.0 copy-start.5
  32.1 0.0 copy-start.8
  32.1 0.0 copy-start.10
  32.1 0.1 collective-permute-start.3
  32.2 3.3 %pick_rows.6 = (bf16[1024,256]{1,0:T(8,128)(2,1)S(1)}, bf16[256,256]{1,0:T(8,128)(2,1)S(1)}, f32[8,1024]{1,0:T(8,128)S(1)}) custom-call(bf16[2816,4096]{1,0:T(8,128)(2,1)S(1)} %build_rows.1.rows_ref, bf16[4096,256]{1,0:T(8,128)(2,1)S(1)} %copy-done, bf16[4096,256]{1,0:T(8,128)(2,1)S(1)} %collective-permute-done.peer_ref, bf16[256,256]{1,0:T(8,128)(2,1)S(1)} %copy-done.1, ...), custom_call_target="tpu_custom_call" | custom-call | flops 2147483648 | bytes 6291456 | tf_op jit(solution)/shard_map/pick_rows/pallas_call | solution.py:274
  35.5 2.1 %collective-permute-start.4 = (bf16[256,256]{1,0:T(8,128)(2,1)S(1)}, bf16[256,256]{1,0:T(8,128)(2,1)S(1)}, u32[]{:S(2)}, u32[]{:S(2)}) collective-permute-start(bf16[256,256]{1,0:T(8,128)(2,1)S(1)} %get-tuple-element.35.refs_2_), channel_id=1, source_target_pairs={{0,16},{8,24},{16,0},{24,8},{1,17},{9,25},{17,1},{25,9},{2,18},{10... | collective-permute-start | bytes 393224 | tf_op jit(solution)/shard_map/ppermute | solution.py:497
  37.6 0.0 collective-permute-done.7.refs_9_
  37.6 0.0 collective-permute-done.6.refs_7_
  37.6 0.0 collective-permute-done.5.refs_5_
  37.6 3.8 %collective-permute-done.4.refs_3_ = bf16[256,256]{1,0:T(8,128)(2,1)S(1)} collective-permute-done((bf16[256,256]{1,0:T(8,128)(2,1)S(1)}, bf16[256,256]{1,0:T(8,128)(2,1)S(1)}, u32[]{:S(2)}, u32[]{:S(2)}) %collective-permute-start.4) | collective-permute-done | bytes 131104 | tf_op jit(solution)/shard_map/ppermute | solution.py:497
  41.4 0.0 collective-permute-done.3.refs_1_
  41.4 0.5 stats.1
  41.9 0.1 collective-permute-start.9
  42.0 1.2 %collective-permute-start.8 = (bf16[64,256]{1,0:T(8,128)(2,1)S(1)}, bf16[64,256]{1,0:T(8,128)(2,1)S(1)}, u32[]{:S(2)}, u32[]{:S(2)}) collective-permute-start(bf16[64,256]{1,0:T(8,128)(2,1)S(1)} %copy-done.6), channel_id=1, source_target_pairs={{0,16},{8,24},{16,0},{24,8},{1,17},{9,25},{17,1},{25,9},{2,18},{10... | collective-permute-start | bytes 98312 | tf_op jit(solution)/shard_map/ppermute | solution.py:497
  43.2 0.0 collective-permute-done.9.other_ref
  43.2 1.6 %collective-permute-start.10 = (f32[8,256]{1,0:T(8,128)S(1)}, f32[8,256]{1,0:T(8,128)S(1)}, u32[]{:S(2)}, u32[]{:S(2)}) collective-permute-start(f32[8,256]{1,0:T(8,128)S(1)} %join.4.mine_ref), channel_id=1, source_target_pairs={{0,1},{1,0},{2,3},{3,2},{4,5},{5,4},{6,7},{7,6},{8,9},{9,8},{10,11... | collective-permute-start | bytes 24584 | tf_op jit(solution)/shard_map/ppermute | solution.py:497
  44.8 2.1 %collective-permute-done.10.other_ref = f32[8,256]{1,0:T(8,128)S(1)} collective-permute-done((f32[8,256]{1,0:T(8,128)S(1)}, f32[8,256]{1,0:T(8,128)S(1)}, u32[]{:S(2)}, u32[]{:S(2)}) %collective-permute-start.10) | collective-permute-done | bytes 8224 | tf_op jit(solution)/shard_map/ppermute | solution.py:497
  46.9 1.6 %collective-permute-start.11 = (f32[8,256]{1,0:T(8,128)S(1)}, f32[8,256]{1,0:T(8,128)S(1)}, u32[]{:S(2)}, u32[]{:S(2)}) collective-permute-start(f32[8,256]{1,0:T(8,128)S(1)} %join.5.mine_ref), channel_id=1, source_target_pairs={{0,2},{1,3},{2,0},{3,1},{4,6},{5,7},{6,4},{7,5},{8,10},{9,11},{10,... | collective-permute-start | bytes 24584 | tf_op jit(solution)/shard_map/ppermute | solution.py:497
  48.5 2.1 %collective-permute-done.11.other_ref = f32[8,256]{1,0:T(8,128)S(1)} collective-permute-done((f32[8,256]{1,0:T(8,128)S(1)}, f32[8,256]{1,0:T(8,128)S(1)}, u32[]{:S(2)}, u32[]{:S(2)}) %collective-permute-start.11) | collective-permute-done | bytes 8224 | tf_op jit(solution)/shard_map/ppermute | solution.py:497
  50.6 2.6 %collective-permute-start.12 = (f32[8,256]{1,0:T(8,128)S(1)}, f32[8,256]{1,0:T(8,128)S(1)}, u32[]{:S(2)}, u32[]{:S(2)}) collective-permute-start(f32[8,256]{1,0:T(8,128)S(1)} %join.6.mine_ref), channel_id=1, source_target_pairs={{0,4},{1,5},{2,6},{3,7},{4,0},{5,1},{6,2},{7,3},{8,12},{9,13},{10,... | collective-permute-start | bytes 24584 | tf_op jit(solution)/shard_map/ppermute | solution.py:497
  53.2 2.0 %collective-permute-done.12.other_ref = f32[8,256]{1,0:T(8,128)S(1)} collective-permute-done((f32[8,256]{1,0:T(8,128)S(1)}, f32[8,256]{1,0:T(8,128)S(1)}, u32[]{:S(2)}, u32[]{:S(2)}) %collective-permute-start.12) | collective-permute-done | bytes 8224 | tf_op jit(solution)/shard_map/ppermute | solution.py:497
  55.2 0.0 collective-permute-done.8.refs_16_
  55.2 3.8 %middle.1 = (bf16[64,256]{1,0:T(8,128)(2,1)}, f32[8,160,256]{2,1,0:T(8,128)S(1)}, bf16[8,160,256]{2,1,0:T(8,128)(2,1)S(1)}, bf16[16,256]{1,0:T(8,128)(2,1)S(1)}) custom-call(s32[2]{0:T(128)S(1)} %pad_add_fusion.place_ref, bf16[384,256]{1,0:T(8,128)(2,1)S(1)} %get-tuple-element.34.refs_0_, bf16[384,256]{1,0:T(8,128)(2,1)S(1)} %collective-permute-done.3.refs_1_, ...), custom_call_target="tpu_custom_call" | custom-call | tf_op jit(solution)/shard_map/middle/pallas_call | solution.py:591
  59.0 0.0 collective-permute-start.13
  59.0 0.5 collective-permute-start.14
  59.5 1.6 %collective-permute-done.14.got_sums_ref = bf16[16,256]{1,0:T(8,128)(2,1)S(1)} collective-permute-done((bf16[16,256]{1,0:T(8,128)(2,1)S(1)}, bf16[16,256]{1,0:T(8,128)(2,1)S(1)}, u32[]{:S(2)}, u32[]{:S(2)}) %collective-permute-start.14) | collective-permute-done | bytes 8224 | tf_op jit(solution)/shard_map/ppermute | solution.py:497
  61.1 0.0 collective-permute-done.13.got_ref
  61.1 1.0 merge.1
  62.1 5.8 %all-to-all-start = ((bf16[8,176,256]{2,1,0:T(8,128)(2,1)}), bf16[8,176,256]{2,1,0:T(8,128)(2,1)S(1)}, u32[]{:S(2)}, u32[]{:S(2)}) async-start(bf16[8,176,256]{2,1,0:T(8,128)(2,1)} %merge.1), calls=%async_computation | async-start | bytes 1441792 | tf_op jit(solution)/shard_map/all_to_all | solution.py:615
  67.9 0.1 constant_dynamic-slice_fusion
  68.0 0.1 reshape.17
  68.1 18.9 %all-to-all-done.parts_ref = bf16[8,176,256]{2,1,0:T(8,128)(2,1)S(1)} async-done(((bf16[8,176,256]{2,1,0:T(8,128)(2,1)}), bf16[8,176,256]{2,1,0:T(8,128)(2,1)S(1)}, u32[]{:S(2)}, u32[]{:S(2)}) %all-to-all-start) | async-done | bytes 720928 | tf_op jit(solution)/shard_map/all_to_all | solution.py:615
  86.9 0.8 finish.1
  87.7 0.0 collective-permute-start.15
  87.7 5.4 %collective-permute-done.15 = bf16[1,96,256]{2,1,0:T(8,128)(2,1)S(1)} collective-permute-done((bf16[1,96,256]{2,1,0:T(8,128)(2,1)S(1)}, bf16[1,96,256]{2,1,0:T(8,128)(2,1)S(1)}, u32[]{:S(2)}, u32[]{:S(2)}) %collective-permute-start.15) | collective-permute-done | bytes 49184 | tf_op jit(solution)/shard_map/ppermute | solution.py:497
  93.1 0.1 collective-permute-start.16
  93.3 4.5 %collective-permute-done.16 = bf16[2,96,256]{2,1,0:T(8,128)(2,1)S(1)} collective-permute-done((bf16[2,96,256]{2,1,0:T(8,128)(2,1)S(1)}, bf16[2,96,256]{2,1,0:T(8,128)(2,1)S(1)}, u32[]{:S(2)}, u32[]{:S(2)}) %collective-permute-start.16) | collective-permute-done | bytes 98336 | tf_op jit(solution)/shard_map/ppermute | solution.py:497
  97.9 1.1 collective-permute-start.17
  98.9 4.7 %collective-permute-done.17 = bf16[4,96,256]{2,1,0:T(8,128)(2,1)S(1)} collective-permute-done((bf16[4,96,256]{2,1,0:T(8,128)(2,1)S(1)}, bf16[4,96,256]{2,1,0:T(8,128)(2,1)S(1)}, u32[]{:S(2)}, u32[]{:S(2)}) %collective-permute-start.17) | collective-permute-done | bytes 196640 | tf_op jit(solution)/shard_map/ppermute | solution.py:497
  103.6 0.8 place.1
  104.5 0.0 collective-permute-start.18
  104.5 1.5 %collective-permute-done.18 = f32[256,256]{1,0:T(8,128)S(1)} collective-permute-done((f32[256,256]{1,0:T(8,128)S(1)}, f32[256,256]{1,0:T(8,128)S(1)}, u32[]{:S(2)}, u32[]{:S(2)}) %collective-permute-start.18) | collective-permute-done | bytes 262176 | tf_op jit(solution)/shard_map/ppermute | solution.py:497
  106.0 0.8 broadcast_select_fusion
  (22 shorter events, 0.1 us)
Async XLA Ops:
  0.6 12.1 %collective-permute-start = (bf16[4096,256]{1,0:T(8,128)(2,1)}, bf16[4096,256]{1,0:T(8,128)(2,1)S(1)}, u32[]{:S(2)}, u32[]{:S(2)}) collective-permute-start(bf16[4096,256]{1,0:T(8,128)(2,1)} %own_ref.9), channel_id=1, source_target_pairs={{0,8},{8,0},{16,24},{24,16},{1,9},{9,1},{17,25},{25,17},{2,10},{10... | collective-permute-start | bytes 6291464 | tf_op jit(solution)/shard_map/ppermute | solution.py:497
  1.1 11.5 %collective-permute-start.1 = (bf16[256,256]{1,0:T(8,128)(2,1)}, bf16[256,256]{1,0:T(8,128)(2,1)S(1)}, u32[]{:S(2)}, u32[]{:S(2)}) collective-permute-start(bf16[256,256]{1,0:T(8,128)(2,1)} %self_own_ref.9), channel_id=1, source_target_pairs={{0,8},{8,0},{16,24},{24,16},{1,9},{9,1},{17,25},{25,17},{2,10},{10... | collective-permute-start | bytes 393224 | tf_op jit(solution)/shard_map/ppermute | solution.py:497
  1.2 11.4 %collective-permute-start.2 = (bf16[256,256]{1,0:T(8,128)(2,1)}, bf16[256,256]{1,0:T(8,128)(2,1)S(1)}, u32[]{:S(2)}, u32[]{:S(2)}) collective-permute-start(bf16[256,256]{1,0:T(8,128)(2,1)} %neigh_own_ref.9), channel_id=1, source_target_pairs={{0,8},{8,0},{16,24},{24,16},{1,9},{9,1},{17,25},{25,17},{2,10},{10... | collective-permute-start | bytes 393224 | tf_op jit(solution)/shard_map/ppermute | solution.py:497
  1.7 0.9 copy-start.3
  2.7 0.7 copy-start.7
  3.4 0.7 copy-start.9
  4.0 8.6 %copy-start = (bf16[4096,256]{1,0:T(8,128)(2,1)S(1)}, bf16[4096,256]{1,0:T(8,128)(2,1)}, u32[]{:S(2)}) copy-start(bf16[4096,256]{1,0:T(8,128)(2,1)} %own_ref.9) | copy-start | bytes 6291460
  4.1 8.7 %copy-start.1 = (bf16[256,256]{1,0:T(8,128)(2,1)S(1)}, bf16[256,256]{1,0:T(8,128)(2,1)}, u32[]{:S(2)}) copy-start(bf16[256,256]{1,0:T(8,128)(2,1)} %self_own_ref.9) | copy-start | bytes 393220
  4.1 8.7 %copy-start.2 = (bf16[256,256]{1,0:T(8,128)(2,1)S(1)}, bf16[256,256]{1,0:T(8,128)(2,1)}, u32[]{:S(2)}) copy-start(bf16[256,256]{1,0:T(8,128)(2,1)} %neigh_own_ref.9) | copy-start | bytes 393220
  15.8 21.7 %collective-permute-start.7 = (bf16[256,256]{1,0:T(8,128)(2,1)S(1)}, bf16[256,256]{1,0:T(8,128)(2,1)S(1)}, u32[]{:S(2)}, u32[]{:S(2)}) collective-permute-start(bf16[256,256]{1,0:T(8,128)(2,1)S(1)} %get-tuple-element.38.refs_8_), channel_id=1, source_target_pairs={{0,16},{8,24},{16,0},{24,8},{1,17},{9,25},{17,1},{25,9},{2,18},{10... | collective-permute-start | bytes 393224 | tf_op jit(solution)/shard_map/ppermute | solution.py:497
  21.6 16.0 %collective-permute-start.6 = (bf16[256,256]{1,0:T(8,128)(2,1)S(1)}, bf16[256,256]{1,0:T(8,128)(2,1)S(1)}, u32[]{:S(2)}, u32[]{:S(2)}) collective-permute-start(bf16[256,256]{1,0:T(8,128)(2,1)S(1)} %get-tuple-element.37.refs_6_), channel_id=1, source_target_pairs={{0,16},{8,24},{16,0},{24,8},{1,17},{9,25},{17,1},{25,9},{2,18},{10... | collective-permute-start | bytes 393224 | tf_op jit(solution)/shard_map/ppermute | solution.py:497
  24.7 12.8 %collective-permute-start.5 = (bf16[256,256]{1,0:T(8,128)(2,1)S(1)}, bf16[256,256]{1,0:T(8,128)(2,1)S(1)}, u32[]{:S(2)}, u32[]{:S(2)}) collective-permute-start(bf16[256,256]{1,0:T(8,128)(2,1)S(1)} %get-tuple-element.36.refs_4_), channel_id=1, source_target_pairs={{0,16},{8,24},{16,0},{24,8},{1,17},{9,25},{17,1},{25,9},{2,18},{10... | collective-permute-start | bytes 393224 | tf_op jit(solution)/shard_map/ppermute | solution.py:497
  32.1 9.9 %copy-start.6 = (bf16[64,256]{1,0:T(8,128)(2,1)S(1)}, bf16[64,256]{1,0:T(8,128)(2,1)}, u32[]{:S(2)}) copy-start(bf16[64,256]{1,0:T(8,128)(2,1)} %refs_15_.1) | copy-start | bytes 98308
  32.1 23.1 %copy-start.4 = (bf16[256,256]{1,0:T(8,128)(2,1)S(1)}, bf16[256,256]{1,0:T(8,128)(2,1)}, u32[]{:S(2)}) copy-start(bf16[256,256]{1,0:T(8,128)(2,1)} %refs_20_.1) | copy-start | bytes 393220
  32.1 23.1 %copy-start.5 = (bf16[256,256]{1,0:T(8,128)(2,1)S(1)}, bf16[256,256]{1,0:T(8,128)(2,1)}, u32[]{:S(2)}) copy-start(bf16[256,256]{1,0:T(8,128)(2,1)} %refs_21_.1) | copy-start | bytes 393220
  32.1 23.1 %copy-start.8 = (f32[256]{0:T(256)S(1)}, f32[256]{0:T(256)}, u32[]{:S(2)}) copy-start(f32[256]{0:T(256)} %param.17) | copy-start | bytes 3076
  32.1 23.1 %copy-start.10 = (f32[256]{0:T(256)S(1)}, f32[256]{0:T(256)}, u32[]{:S(2)}) copy-start(f32[256]{0:T(256)} %param.18) | copy-start | bytes 3076
  32.1 9.3 %collective-permute-start.3 = (bf16[384,256]{1,0:T(8,128)(2,1)S(1)}, bf16[384,256]{1,0:T(8,128)(2,1)S(1)}, u32[]{:S(2)}, u32[]{:S(2)}) collective-permute-start(bf16[384,256]{1,0:T(8,128)(2,1)S(1)} %get-tuple-element.34.refs_0_), channel_id=1, source_target_pairs={{0,16},{8,24},{16,0},{24,8},{1,17},{9,25},{17,1},{25,9},{2,18},{10... | collective-permute-start | bytes 589832 | tf_op jit(solution)/shard_map/ppermute | solution.py:497
  35.5 5.9 %collective-permute-start.4 = (bf16[256,256]{1,0:T(8,128)(2,1)S(1)}, bf16[256,256]{1,0:T(8,128)(2,1)S(1)}, u32[]{:S(2)}, u32[]{:S(2)}) collective-permute-start(bf16[256,256]{1,0:T(8,128)(2,1)S(1)} %get-tuple-element.35.refs_2_), channel_id=1, source_target_pairs={{0,16},{8,24},{16,0},{24,8},{1,17},{9,25},{17,1},{25,9},{2,18},{10... | collective-permute-start | bytes 393224 | tf_op jit(solution)/shard_map/ppermute | solution.py:497
  41.9 1.3 %collective-permute-start.9 = (f32[8,256]{1,0:T(8,128)S(1)}, f32[8,256]{1,0:T(8,128)S(1)}, u32[]{:S(2)}, u32[]{:S(2)}) collective-permute-start(f32[8,256]{1,0:T(8,128)S(1)} %get-tuple-element.50), channel_id=1, source_target_pairs={{0,8},{8,0},{16,24},{24,16},{1,9},{9,1},{17,25},{25,17},{2,10},{10... | collective-permute-start | bytes 24584 | tf_op jit(solution)/shard_map/ppermute | solution.py:497
  42.0 13.2 %collective-permute-start.8 = (bf16[64,256]{1,0:T(8,128)(2,1)S(1)}, bf16[64,256]{1,0:T(8,128)(2,1)S(1)}, u32[]{:S(2)}, u32[]{:S(2)}) collective-permute-start(bf16[64,256]{1,0:T(8,128)(2,1)S(1)} %copy-done.6), channel_id=1, source_target_pairs={{0,16},{8,24},{16,0},{24,8},{1,17},{9,25},{17,1},{25,9},{2,18},{10... | collective-permute-start | bytes 98312 | tf_op jit(solution)/shard_map/ppermute | solution.py:497
  43.2 3.7 %collective-permute-start.10 = (f32[8,256]{1,0:T(8,128)S(1)}, f32[8,256]{1,0:T(8,128)S(1)}, u32[]{:S(2)}, u32[]{:S(2)}) collective-permute-start(f32[8,256]{1,0:T(8,128)S(1)} %join.4.mine_ref), channel_id=1, source_target_pairs={{0,1},{1,0},{2,3},{3,2},{4,5},{5,4},{6,7},{7,6},{8,9},{9,8},{10,11... | collective-permute-start | bytes 24584 | tf_op jit(solution)/shard_map/ppermute | solution.py:497
  46.9 3.7 %collective-permute-start.11 = (f32[8,256]{1,0:T(8,128)S(1)}, f32[8,256]{1,0:T(8,128)S(1)}, u32[]{:S(2)}, u32[]{:S(2)}) collective-permute-start(f32[8,256]{1,0:T(8,128)S(1)} %join.5.mine_ref), channel_id=1, source_target_pairs={{0,2},{1,3},{2,0},{3,1},{4,6},{5,7},{6,4},{7,5},{8,10},{9,11},{10,... | collective-permute-start | bytes 24584 | tf_op jit(solution)/shard_map/ppermute | solution.py:497
  50.6 4.5 %collective-permute-start.12 = (f32[8,256]{1,0:T(8,128)S(1)}, f32[8,256]{1,0:T(8,128)S(1)}, u32[]{:S(2)}, u32[]{:S(2)}) collective-permute-start(f32[8,256]{1,0:T(8,128)S(1)} %join.6.mine_ref), channel_id=1, source_target_pairs={{0,4},{1,5},{2,6},{3,7},{4,0},{5,1},{6,2},{7,3},{8,12},{9,13},{10,... | collective-permute-start | bytes 24584 | tf_op jit(solution)/shard_map/ppermute | solution.py:497
  59.0 2.1 %collective-permute-start.13 = (bf16[8,160,256]{2,1,0:T(8,128)(2,1)S(1)}, bf16[8,160,256]{2,1,0:T(8,128)(2,1)S(1)}, u32[]{:S(2)}, u32[]{:S(2)}) collective-permute-start(bf16[8,160,256]{2,1,0:T(8,128)(2,1)S(1)} %get-tuple-element.53), channel_id=1, source_target_pairs={{0,8},{8,0},{16,24},{24,16},{1,9},{9,1},{17,25},{25,17},{2,10},{10... | collective-permute-start | bytes 1966088 | tf_op jit(solution)/shard_map/ppermute | solution.py:497
  59.0 2.1 %collective-permute-start.14 = (bf16[16,256]{1,0:T(8,128)(2,1)S(1)}, bf16[16,256]{1,0:T(8,128)(2,1)S(1)}, u32[]{:S(2)}, u32[]{:S(2)}) collective-permute-start(bf16[16,256]{1,0:T(8,128)(2,1)S(1)} %get-tuple-element.54.sums_ref), channel_id=1, source_target_pairs={{0,8},{8,0},{16,24},{24,16},{1,9},{9,1},{17,25},{25,17},{2,10},{10... | collective-permute-start | bytes 24584 | tf_op jit(solution)/shard_map/ppermute | solution.py:497
  62.1 24.9 %all-to-all-start = ((bf16[8,176,256]{2,1,0:T(8,128)(2,1)}), bf16[8,176,256]{2,1,0:T(8,128)(2,1)S(1)}, u32[]{:S(2)}, u32[]{:S(2)}) async-start(bf16[8,176,256]{2,1,0:T(8,128)(2,1)} %merge.1), calls=%async_computation | async-start | bytes 1441792 | tf_op jit(solution)/shard_map/all_to_all | solution.py:615
  87.7 5.4 %collective-permute-start.15 = (bf16[1,96,256]{2,1,0:T(8,128)(2,1)S(1)}, bf16[1,96,256]{2,1,0:T(8,128)(2,1)S(1)}, u32[]{:S(2)}, u32[]{:S(2)}) collective-permute-start(bf16[1,96,256]{2,1,0:T(8,128)(2,1)S(1)} %bitcast.11), channel_id=1, source_target_pairs={{0,4},{1,5},{2,6},{3,7},{4,0},{5,1},{6,2},{7,3},{8,12},{9,13},{10,... | collective-permute-start | bytes 147464 | tf_op jit(solution)/shard_map/ppermute | solution.py:497
  93.1 4.7 %collective-permute-start.16 = (bf16[2,96,256]{2,1,0:T(8,128)(2,1)S(1)}, bf16[2,96,256]{2,1,0:T(8,128)(2,1)S(1)}, u32[]{:S(2)}, u32[]{:S(2)}) collective-permute-start(bf16[2,96,256]{2,1,0:T(8,128)(2,1)S(1)} %pad_maximum_fusion.2), channel_id=1, source_target_pairs={{0,2},{1,3},{2,0},{3,1},{4,6},{5,7},{6,4},{7,5},{8,10},{9,11},{10,... | collective-permute-start | bytes 294920 | tf_op jit(solution)/shard_map/ppermute | solution.py:497
  97.9 5.7 %collective-permute-start.17 = (bf16[4,96,256]{2,1,0:T(8,128)(2,1)S(1)}, bf16[4,96,256]{2,1,0:T(8,128)(2,1)S(1)}, u32[]{:S(2)}, u32[]{:S(2)}) collective-permute-start(bf16[4,96,256]{2,1,0:T(8,128)(2,1)S(1)} %pad_maximum_fusion.1), channel_id=1, source_target_pairs={{0,1},{1,0},{2,3},{3,2},{4,5},{5,4},{6,7},{7,6},{8,9},{9,8},{10,11... | collective-permute-start | bytes 589832 | tf_op jit(solution)/shard_map/ppermute | solution.py:497
  104.5 1.5 %collective-permute-start.18 = (f32[256,256]{1,0:T(8,128)S(1)}, f32[256,256]{1,0:T(8,128)S(1)}, u32[]{:S(2)}, u32[]{:S(2)}) collective-permute-start(f32[256,256]{1,0:T(8,128)S(1)} %get-tuple-element.58), channel_id=1, source_target_pairs={{0,8},{8,0},{16,24},{24,16},{1,9},{9,1},{17,25},{25,17},{2,10},{10... | collective-permute-start | bytes 786440 | tf_op jit(solution)/shard_map/ppermute | solution.py:497

commit v3 on v2

--- a/solution.py
+++ b/solution.py
@@ -209,41 +209,30 @@
     across_ref,
     pre_ref,
     column_ref,
-    peer,
-    sem,
 ):
     width = own_ref.shape[1]
     step = pl.program_id(0)
-    fetch = pltpu.make_async_copy(peer_ref, peer, sem)
-
-    @pl.when(step == 0)
-    def _():
-        fetch.start()
-
+    tables = (own_ref, peer_ref)
+    picked = [
+        [dot(rows_ref[at : at + 2 * LANES, :], table[...]) for table in tables]
+        for at in range(start, start + 2 * blocks * LANES, 2 * LANES)
+    ]
     total = None
     columns = []
-    for i, (table, weight_self, weight_neigh) in enumerate(
-        ((own_ref, self_own_ref, neigh_own_ref), (peer, self_peer_ref, neigh_peer_ref))
-    ):
-        if i == 1:
-
-            @pl.when(step == 0)
-            def _():
-                fetch.wait()
-
+    for i in range(2):
         self_parts, neigh_parts = [], []
         for b in range(blocks):
             block = first_block + step * blocks + b
             share = jnp.where(block < per_slot, F32(1.0 / fans[0]), F32(1.0 / fans[1]))
-            at = start + 2 * b * LANES
-            picked = dot(rows_ref[at : at + 2 * LANES, :], table[...])
-            neigh_parts.append((picked[:LANES] * share).astype(BF))
-            self_parts.append(picked[LANES:].astype(BF))
+            neigh_parts.append((picked[b][i][:LANES] * share).astype(BF))
+            self_parts.append(picked[b][i][LANES:].astype(BF))
+        weights = ((self_own_ref, neigh_own_ref), (self_peer_ref, neigh_peer_ref))[i]
         for j, parts in enumerate((self_parts, neigh_parts)):
-            features = jnp.concatenate(parts, axis=0)
-            part = dot(features, (weight_self, weight_neigh)[j][...])
+            part = dot(jnp.concatenate(parts, axis=0), weights[j][...])
             total = part if total is None else total + part
-            columns.append(dot(jnp.ones((8, features.shape[0]), BF), features))
+            columns.append(
+                sum(jnp.sum(p.astype(F32).reshape(-1, 8, width), axis=0) for p in parts)
+            )
             for b in range(blocks):
                 across_ref[
                     (2 * i + j) * width : (2 * i + j + 1) * width, b * LANES : (b + 1) * LANES
@@ -274,7 +263,7 @@
     return pl.pallas_call(
         functools.partial(pick_kernel, first_block, start, blocks, per_slot, fans),
         grid=(count // blocks,),
-        in_specs=[rows_spec, VMEM, HBM] + [VMEM] * 4,
+        in_specs=[rows_spec] + [VMEM] * 6,
         out_specs=[
             pl.BlockSpec((4 * width, blocks * LANES), lambda i: (0, i)),
             pl.BlockSpec((blocks * LANES, hidden_width), lambda i: (i, 0)),
@@ -285,11 +274,7 @@
             jax.ShapeDtypeStruct((total, hidden_width), BF),
             jax.ShapeDtypeStruct((8, 4 * width), F32),
         ],
-        scratch_shapes=[
-            pltpu.VMEM(peer.shape, BF),
-            pltpu.SemaphoreType.DMA,
-        ],
-        compiler_params=params(16 if resident else 24),
+        compiler_params=params(12 if resident else 22),
         cost_estimate=pl.CostEstimate(
             flops=8 * total * table_rows * width,
             bytes_accessed=2 * total * table_rows + 4 * table_rows * width,
@@ -314,7 +299,7 @@
     mean = mean / rows
     gap = total[...] - mean
     square = jnp.sum(gap * gap, axis=0, keepdims=True)
-    column = sum(c[0:1, :] for c in columns)
+    column = jnp.sum(sum(c[...] for c in columns), axis=0, keepdims=True)
     pad = jnp.zeros((4, mean.shape[1]), F32)
     lanes = mean.shape[1] - width
     for ref, first in ((keep_ref, 0), (send_ref, 2)):
@@ -655,7 +640,7 @@
     )
 
 
-CHUNKS = (3, 2, 2, 2, 2)
+CHUNKS = (2, 3, 3, 3)
 
 
 def solution(mesh):

time: 107 us -> 103 us (0.963)
  Pallas kernels: 33.3 us -> 29.6 us
  starting transfers between devices: 22.6 us -> 20.8 us
  waiting for transfers between devices: 46.6 us -> 48 us
    pallas_call x5 -> x4, Pallas kernels: 17.8 us -> 14 us  [pick_rows(): pl.pallas_call(functools.partial(pick_kernel, first_block, start, blocks,...]
    ppermute x19 -> x18, starting transfers between devices: 16.7 us -> 15 us  [swap(): lax.ppermute(value, axis, [(i, i ^ mask) for i in range(lax.axis_size(axi...]
    ppermute x19 -> x18, waiting for transfers between devices: 27.8 us -> 29.1 us  [swap(): lax.ppermute(value, axis, [(i, i ^ mask) for i in range(lax.axis_size(axi...]
  transfers between devices with their start and end apart: 20 -> 19, of which waited for: 10 -> 10; matrix products, arithmetic and copies ran while one was open for 0% -> 0% of each run, Pallas kernels for 22% -> 18%
where the time goes in v3:
time: 103 us
  waiting for transfers between devices  48 us (47%)
  Pallas kernels  29.6 us (29%)
  starting transfers between devices  20.8 us (20%)
  local copies, waits for them, and re-layouts  2.53 us (2%)
    ppermute x18, waiting for transfers between devices, swap(): lax.ppermute(value, axis, [(i, i ^ mask) for i in range(lax.axis_size(axi...  29.1 us
    all_to_all x1, waiting for transfers between devices, on_device(): parts = lax.all_to_all(parts, 'batch', 0, 0)  18.9 us
    ppermute x18, starting transfers between devices, swap(): lax.ppermute(value, axis, [(i, i ^ mask) for i in range(lax.axis_size(axi...  15 us
    pallas_call x4, Pallas kernels, pick_rows(): pl.pallas_call(functools.partial(pick_kernel, first_block, start, blocks,...  14 us
    pallas_call x1, Pallas kernels, build_rows(): pl.pallas_call(build_kernel, grid=(steps,), in_specs=[SMEM, HBM, HBM, HBM...  8.6 us
    all_to_all x1, starting transfers between devices, on_device(): parts = lax.all_to_all(parts, 'batch', 0, 0)  5.83 us
    pallas_call x1, Pallas kernels, on_device(): pl.pallas_call(functools.partial(middle_kernel, len(CHUNKS), slots, row_t...  3.78 us
    unnamed x22, local copies, waits for them, and re-layouts  2.35 us
  transfers between devices with their start and end apart: 19, of which 10 were waited for; matrix products, arithmetic and copies ran while one was open for 0% of the time, Pallas kernels for 18%

profile of v3, /device:TPU:0, one launch (start us, length us, event | category | flops | bytes accessed | tf_op | source)
XLA Modules:
  0.0 102.8 jit_solution(16380389679964620022)
XLA Ops:
  0.6 0.5 collective-permute-start
  1.1 0.1 collective-permute-start.1
  1.2 0.4 collective-permute-start.2
  1.7 0.1 pad_add_fusion.place_ref
  1.7 0.9 copy-done.3
  2.7 0.7 copy-done.7
  3.4 0.7 copy-done.9
  4.1 8.6 %build_rows.1.rows_ref = bf16[2816,4096]{1,0:T(8,128)(2,1)S(1)} custom-call(s32[2]{0:T(128)S(1)} %pad_add_fusion.place_ref, s32[1,256]{1,0:T(1,128)S(1)} %bitcast.19, s32[10,256]{1,0:T(8,128)S(1)} %bitcast.16, s32[10,15,256]{2,1,0:T(8,128)S(1)} %bitcast.15), custom_call_target="tpu_custom_call" | custom-call | flops 2952790016 | bytes 23068672 | tf_op jit(solution)/shard_map/build_rows/pallas_call | solution.py:170
  12.7 0.0 collective-permute-done.1.self_peer_ref
  12.7 0.0 collective-permute-done.2.neigh_peer_ref
  12.7 0.0 collective-permute-done.peer_ref
  12.7 0.0 copy-done
  12.7 0.0 copy-done.1
  12.7 0.0 copy-done.2
  12.7 3.8 %pick_rows.7 = (bf16[1024,384]{1,0:T(8,128)(2,1)S(1)}, bf16[384,256]{1,0:T(8,128)(2,1)S(1)}, f32[8,1024]{1,0:T(8,128)S(1)}) custom-call(bf16[2816,4096]{1,0:T(8,128)(2,1)S(1)} %build_rows.1.rows_ref, bf16[4096,256]{1,0:T(8,128)(2,1)S(1)} %copy-done, bf16[4096,256]{1,0:T(8,128)(2,1)S(1)} %collective-permute-done.peer_ref, bf16[256,256]{1,0:T(8,128)(2,1)S(1)} %copy-done.1, ...), custom_call_target="tpu_custom_call" | custom-call | flops 3221225472 | bytes 7340032 | tf_op jit(solution)/shard_map/pick_rows/pallas_call | solution.py:263
  16.5 2.6 %collective-permute-start.6 = (bf16[384,256]{1,0:T(8,128)(2,1)S(1)}, bf16[384,256]{1,0:T(8,128)(2,1)S(1)}, u32[]{:S(2)}, u32[]{:S(2)}) collective-permute-start(bf16[384,256]{1,0:T(8,128)(2,1)S(1)} %get-tuple-element.34.refs_6_), channel_id=1, source_target_pairs={{0,16},{8,24},{16,0},{24,8},{1,17},{9,25},{17,1},{25,9},{2,18},{10... | collective-permute-start | bytes 589832 | tf_op jit(solution)/shard_map/ppermute | solution.py:482
  19.1 3.8 %pick_rows.6 = (bf16[1024,384]{1,0:T(8,128)(2,1)S(1)}, bf16[384,256]{1,0:T(8,128)(2,1)S(1)}, f32[8,1024]{1,0:T(8,128)S(1)}) custom-call(bf16[2816,4096]{1,0:T(8,128)(2,1)S(1)} %build_rows.1.rows_ref, bf16[4096,256]{1,0:T(8,128)(2,1)S(1)} %copy-done, bf16[4096,256]{1,0:T(8,128)(2,1)S(1)} %collective-permute-done.peer_ref, bf16[256,256]{1,0:T(8,128)(2,1)S(1)} %copy-done.1, ...), custom_call_target="tpu_custom_call" | custom-call | flops 3221225472 | bytes 7340032 | tf_op jit(solution)/shard_map/pick_rows/pallas_call | solution.py:263
  22.9 0.1 collective-permute-start.5
  23.0 3.8 %pick_rows.5 = (bf16[1024,384]{1,0:T(8,128)(2,1)S(1)}, bf16[384,256]{1,0:T(8,128)(2,1)S(1)}, f32[8,1024]{1,0:T(8,128)S(1)}) custom-call(bf16[2816,4096]{1,0:T(8,128)(2,1)S(1)} %build_rows.1.rows_ref, bf16[4096,256]{1,0:T(8,128)(2,1)S(1)} %copy-done, bf16[4096,256]{1,0:T(8,128)(2,1)S(1)} %collective-permute-done.peer_ref, bf16[256,256]{1,0:T(8,128)(2,1)S(1)} %copy-done.1, ...), custom_call_target="tpu_custom_call" | custom-call | flops 3221225472 | bytes 7340032 | tf_op jit(solution)/shard_map/pick_rows/pallas_call | solution.py:263
  26.7 0.0 copy-start.6
  26.7 0.0 copy-start.4
  26.7 0.0 copy-start.5
  26.7 0.0 copy-start.8
  26.8 0.0 copy-start.10
  26.8 2.1 %collective-permute-start.4 = (bf16[384,256]{1,0:T(8,128)(2,1)S(1)}, bf16[384,256]{1,0:T(8,128)(2,1)S(1)}, u32[]{:S(2)}, u32[]{:S(2)}) collective-permute-start(bf16[384,256]{1,0:T(8,128)(2,1)S(1)} %get-tuple-element.32.refs_2_), channel_id=1, source_target_pairs={{0,16},{8,24},{16,0},{24,8},{1,17},{9,25},{17,1},{25,9},{2,18},{10... | collective-permute-start | bytes 589832 | tf_op jit(solution)/shard_map/ppermute | solution.py:482
  28.8 2.8 %pick_rows.4 = (bf16[1024,256]{1,0:T(8,128)(2,1)S(1)}, bf16[256,256]{1,0:T(8,128)(2,1)S(1)}, f32[8,1024]{1,0:T(8,128)S(1)}) custom-call(bf16[2816,4096]{1,0:T(8,128)(2,1)S(1)} %build_rows.1.rows_ref, bf16[4096,256]{1,0:T(8,128)(2,1)S(1)} %copy-done, bf16[4096,256]{1,0:T(8,128)(2,1)S(1)} %collective-permute-done.peer_ref, bf16[256,256]{1,0:T(8,128)(2,1)S(1)} %copy-done.1, ...), custom_call_target="tpu_custom_call" | custom-call | flops 2147483648 | bytes 6291456 | tf_op jit(solution)/shard_map/pick_rows/pallas_call | solution.py:263
  31.6 0.1 collective-permute-start.3
  31.7 5.2 %collective-permute-done.3.refs_1_ = bf16[256,256]{1,0:T(8,128)(2,1)S(1)} collective-permute-done((bf16[256,256]{1,0:T(8,128)(2,1)S(1)}, bf16[256,256]{1,0:T(8,128)(2,1)S(1)}, u32[]{:S(2)}, u32[]{:S(2)}) %collective-permute-start.3) | collective-permute-done | bytes 131104 | tf_op jit(solution)/shard_map/ppermute | solution.py:482
  36.9 0.0 collective-permute-done.6.refs_7_
  36.9 0.0 collective-permute-done.5.refs_5_
  36.9 0.0 collective-permute-done.4.refs_3_
  36.9 0.5 stats.1
  37.5 0.1 collective-permute-start.8
  37.5 0.0 copy-done.6
  37.5 1.5 %collective-permute-start.7 = (bf16[64,256]{1,0:T(8,128)(2,1)S(1)}, bf16[64,256]{1,0:T(8,128)(2,1)S(1)}, u32[]{:S(2)}, u32[]{:S(2)}) collective-permute-start(bf16[64,256]{1,0:T(8,128)(2,1)S(1)} %copy-done.6), channel_id=1, source_target_pairs={{0,16},{8,24},{16,0},{24,8},{1,17},{9,25},{17,1},{25,9},{2,18},{10... | collective-permute-start | bytes 98312 | tf_op jit(solution)/shard_map/ppermute | solution.py:482
  39.0 0.0 collective-permute-done.8.other_ref
  39.0 1.6 %collective-permute-start.9 = (f32[8,256]{1,0:T(8,128)S(1)}, f32[8,256]{1,0:T(8,128)S(1)}, u32[]{:S(2)}, u32[]{:S(2)}) collective-permute-start(f32[8,256]{1,0:T(8,128)S(1)} %join.4.mine_ref), channel_id=1, source_target_pairs={{0,1},{1,0},{2,3},{3,2},{4,5},{5,4},{6,7},{7,6},{8,9},{9,8},{10,11... | collective-permute-start | bytes 24584 | tf_op jit(solution)/shard_map/ppermute | solution.py:482
  40.6 2.1 %collective-permute-done.9.other_ref = f32[8,256]{1,0:T(8,128)S(1)} collective-permute-done((f32[8,256]{1,0:T(8,128)S(1)}, f32[8,256]{1,0:T(8,128)S(1)}, u32[]{:S(2)}, u32[]{:S(2)}) %collective-permute-start.9) | collective-permute-done | bytes 8224 | tf_op jit(solution)/shard_map/ppermute | solution.py:482
  42.8 1.6 %collective-permute-start.10 = (f32[8,256]{1,0:T(8,128)S(1)}, f32[8,256]{1,0:T(8,128)S(1)}, u32[]{:S(2)}, u32[]{:S(2)}) collective-permute-start(f32[8,256]{1,0:T(8,128)S(1)} %join.5.mine_ref), channel_id=1, source_target_pairs={{0,2},{1,3},{2,0},{3,1},{4,6},{5,7},{6,4},{7,5},{8,10},{9,11},{10,... | collective-permute-start | bytes 24584 | tf_op jit(solution)/shard_map/ppermute | solution.py:482
  44.3 2.1 %collective-permute-done.10.other_ref = f32[8,256]{1,0:T(8,128)S(1)} collective-permute-done((f32[8,256]{1,0:T(8,128)S(1)}, f32[8,256]{1,0:T(8,128)S(1)}, u32[]{:S(2)}, u32[]{:S(2)}) %collective-permute-start.10) | collective-permute-done | bytes 8224 | tf_op jit(solution)/shard_map/ppermute | solution.py:482
  46.4 2.6 %collective-permute-start.11 = (f32[8,256]{1,0:T(8,128)S(1)}, f32[8,256]{1,0:T(8,128)S(1)}, u32[]{:S(2)}, u32[]{:S(2)}) collective-permute-start(f32[8,256]{1,0:T(8,128)S(1)} %join.6.mine_ref), channel_id=1, source_target_pairs={{0,4},{1,5},{2,6},{3,7},{4,0},{5,1},{6,2},{7,3},{8,12},{9,13},{10,... | collective-permute-start | bytes 24584 | tf_op jit(solution)/shard_map/ppermute | solution.py:482
  49.0 2.0 %collective-permute-done.11.other_ref = f32[8,256]{1,0:T(8,128)S(1)} collective-permute-done((f32[8,256]{1,0:T(8,128)S(1)}, f32[8,256]{1,0:T(8,128)S(1)}, u32[]{:S(2)}, u32[]{:S(2)}) %collective-permute-start.11) | collective-permute-done | bytes 8224 | tf_op jit(solution)/shard_map/ppermute | solution.py:482
  51.0 0.0 collective-permute-done.7.refs_13_
  51.0 3.8 %middle.1 = (bf16[64,256]{1,0:T(8,128)(2,1)}, f32[8,160,256]{2,1,0:T(8,128)S(1)}, bf16[8,160,256]{2,1,0:T(8,128)(2,1)S(1)}, bf16[16,256]{1,0:T(8,128)(2,1)S(1)}) custom-call(s32[2]{0:T(128)S(1)} %pad_add_fusion.place_ref, bf16[256,256]{1,0:T(8,128)(2,1)S(1)} %get-tuple-element.31.refs_0_, bf16[256,256]{1,0:T(8,128)(2,1)S(1)} %collective-permute-done.3.refs_1_, ...), custom_call_target="tpu_custom_call" | custom-call | tf_op jit(solution)/shard_map/middle/pallas_call | solution.py:576
  54.8 0.1 collective-permute-start.12
  54.9 0.5 collective-permute-start.13
  55.4 1.6 %collective-permute-done.13.got_sums_ref = bf16[16,256]{1,0:T(8,128)(2,1)S(1)} collective-permute-done((bf16[16,256]{1,0:T(8,128)(2,1)S(1)}, bf16[16,256]{1,0:T(8,128)(2,1)S(1)}, u32[]{:S(2)}, u32[]{:S(2)}) %collective-permute-start.13) | collective-permute-done | bytes 8224 | tf_op jit(solution)/shard_map/ppermute | solution.py:482
  57.0 0.0 collective-permute-done.12.got_ref
  57.0 1.0 merge.1
  58.0 5.8 %all-to-all-start = ((bf16[8,176,256]{2,1,0:T(8,128)(2,1)}), bf16[8,176,256]{2,1,0:T(8,128)(2,1)S(1)}, u32[]{:S(2)}, u32[]{:S(2)}) async-start(bf16[8,176,256]{2,1,0:T(8,128)(2,1)} %merge.1), calls=%async_computation | async-start | bytes 1441792 | tf_op jit(solution)/shard_map/all_to_all | solution.py:600
  63.9 0.1 constant_dynamic-slice_fusion
  63.9 0.1 reshape.17
  64.0 18.9 %all-to-all-done.parts_ref = bf16[8,176,256]{2,1,0:T(8,128)(2,1)S(1)} async-done(((bf16[8,176,256]{2,1,0:T(8,128)(2,1)}), bf16[8,176,256]{2,1,0:T(8,128)(2,1)S(1)}, u32[]{:S(2)}, u32[]{:S(2)}) %all-to-all-start) | async-done | bytes 720928 | tf_op jit(solution)/shard_map/all_to_all | solution.py:600
  82.9 0.8 finish.1
  83.7 0.0 collective-permute-start.14
  83.7 5.4 %collective-permute-done.14 = bf16[1,96,256]{2,1,0:T(8,128)(2,1)S(1)} collective-permute-done((bf16[1,96,256]{2,1,0:T(8,128)(2,1)S(1)}, bf16[1,96,256]{2,1,0:T(8,128)(2,1)S(1)}, u32[]{:S(2)}, u32[]{:S(2)}) %collective-permute-start.14) | collective-permute-done | bytes 49184 | tf_op jit(solution)/shard_map/ppermute | solution.py:482
  89.1 0.1 collective-permute-start.15
  89.2 4.5 %collective-permute-done.15 = bf16[2,96,256]{2,1,0:T(8,128)(2,1)S(1)} collective-permute-done((bf16[2,96,256]{2,1,0:T(8,128)(2,1)S(1)}, bf16[2,96,256]{2,1,0:T(8,128)(2,1)S(1)}, u32[]{:S(2)}, u32[]{:S(2)}) %collective-permute-start.15) | collective-permute-done | bytes 98336 | tf_op jit(solution)/shard_map/ppermute | solution.py:482
  93.8 1.1 %collective-permute-start.16 = (bf16[4,96,256]{2,1,0:T(8,128)(2,1)S(1)}, bf16[4,96,256]{2,1,0:T(8,128)(2,1)S(1)}, u32[]{:S(2)}, u32[]{:S(2)}) collective-permute-start(bf16[4,96,256]{2,1,0:T(8,128)(2,1)S(1)} %pad_maximum_fusion.1), channel_id=1, source_target_pairs={{0,1},{1,0},{2,3},{3,2},{4,5},{5,4},{6,7},{7,6},{8,9},{9,8},{10,11... | collective-permute-start | bytes 589832 | tf_op jit(solution)/shard_map/ppermute | solution.py:482
  94.9 4.7 %collective-permute-done.16 = bf16[4,96,256]{2,1,0:T(8,128)(2,1)S(1)} collective-permute-done((bf16[4,96,256]{2,1,0:T(8,128)(2,1)S(1)}, bf16[4,96,256]{2,1,0:T(8,128)(2,1)S(1)}, u32[]{:S(2)}, u32[]{:S(2)}) %collective-permute-start.16) | collective-permute-done | bytes 196640 | tf_op jit(solution)/shard_map/ppermute | solution.py:482
  99.6 0.8 place.1
  100.4 0.0 collective-permute-start.17
  100.4 1.5 %collective-permute-done.17 = f32[256,256]{1,0:T(8,128)S(1)} collective-permute-done((f32[256,256]{1,0:T(8,128)S(1)}, f32[256,256]{1,0:T(8,128)S(1)}, u32[]{:S(2)}, u32[]{:S(2)}) %collective-permute-start.17) | collective-permute-done | bytes 262176 | tf_op jit(solution)/shard_map/ppermute | solution.py:482
  102.0 0.8 broadcast_select_fusion
  (19 shorter events, 0.1 us)
Async XLA Ops:
  0.6 12.1 %collective-permute-start = (bf16[4096,256]{1,0:T(8,128)(2,1)}, bf16[4096,256]{1,0:T(8,128)(2,1)S(1)}, u32[]{:S(2)}, u32[]{:S(2)}) collective-permute-start(bf16[4096,256]{1,0:T(8,128)(2,1)} %own_ref.7), channel_id=1, source_target_pairs={{0,8},{8,0},{16,24},{24,16},{1,9},{9,1},{17,25},{25,17},{2,10},{10... | collective-permute-start | bytes 6291464 | tf_op jit(solution)/shard_map/ppermute | solution.py:482
  1.1 11.5 %collective-permute-start.1 = (bf16[256,256]{1,0:T(8,128)(2,1)}, bf16[256,256]{1,0:T(8,128)(2,1)S(1)}, u32[]{:S(2)}, u32[]{:S(2)}) collective-permute-start(bf16[256,256]{1,0:T(8,128)(2,1)} %self_own_ref.7), channel_id=1, source_target_pairs={{0,8},{8,0},{16,24},{24,16},{1,9},{9,1},{17,25},{25,17},{2,10},{10... | collective-permute-start | bytes 393224 | tf_op jit(solution)/shard_map/ppermute | solution.py:482
  1.2 11.4 %collective-permute-start.2 = (bf16[256,256]{1,0:T(8,128)(2,1)}, bf16[256,256]{1,0:T(8,128)(2,1)S(1)}, u32[]{:S(2)}, u32[]{:S(2)}) collective-permute-start(bf16[256,256]{1,0:T(8,128)(2,1)} %neigh_own_ref.7), channel_id=1, source_target_pairs={{0,8},{8,0},{16,24},{24,16},{1,9},{9,1},{17,25},{25,17},{2,10},{10... | collective-permute-start | bytes 393224 | tf_op jit(solution)/shard_map/ppermute | solution.py:482
  1.7 0.9 copy-start.3
  2.7 0.7 copy-start.7
  3.4 0.7 copy-start.9
  4.0 8.6 %copy-start = (bf16[4096,256]{1,0:T(8,128)(2,1)S(1)}, bf16[4096,256]{1,0:T(8,128)(2,1)}, u32[]{:S(2)}) copy-start(bf16[4096,256]{1,0:T(8,128)(2,1)} %own_ref.7) | copy-start | bytes 6291460
  4.1 8.7 %copy-start.1 = (bf16[256,256]{1,0:T(8,128)(2,1)S(1)}, bf16[256,256]{1,0:T(8,128)(2,1)}, u32[]{:S(2)}) copy-start(bf16[256,256]{1,0:T(8,128)(2,1)} %self_own_ref.7) | copy-start | bytes 393220
  4.1 8.7 %copy-start.2 = (bf16[256,256]{1,0:T(8,128)(2,1)S(1)}, bf16[256,256]{1,0:T(8,128)(2,1)}, u32[]{:S(2)}) copy-start(bf16[256,256]{1,0:T(8,128)(2,1)} %neigh_own_ref.7) | copy-start | bytes 393220
  16.5 20.4 %collective-permute-start.6 = (bf16[384,256]{1,0:T(8,128)(2,1)S(1)}, bf16[384,256]{1,0:T(8,128)(2,1)S(1)}, u32[]{:S(2)}, u32[]{:S(2)}) collective-permute-start(bf16[384,256]{1,0:T(8,128)(2,1)S(1)} %get-tuple-element.34.refs_6_), channel_id=1, source_target_pairs={{0,16},{8,24},{16,0},{24,8},{1,17},{9,25},{17,1},{25,9},{2,18},{10... | collective-permute-start | bytes 589832 | tf_op jit(solution)/shard_map/ppermute | solution.py:482
  22.9 14.1 %collective-permute-start.5 = (bf16[384,256]{1,0:T(8,128)(2,1)S(1)}, bf16[384,256]{1,0:T(8,128)(2,1)S(1)}, u32[]{:S(2)}, u32[]{:S(2)}) collective-permute-start(bf16[384,256]{1,0:T(8,128)(2,1)S(1)} %get-tuple-element.33.refs_4_), channel_id=1, source_target_pairs={{0,16},{8,24},{16,0},{24,8},{1,17},{9,25},{17,1},{25,9},{2,18},{10... | collective-permute-start | bytes 589832 | tf_op jit(solution)/shard_map/ppermute | solution.py:482
  26.7 10.8 %copy-start.6 = (bf16[64,256]{1,0:T(8,128)(2,1)S(1)}, bf16[64,256]{1,0:T(8,128)(2,1)}, u32[]{:S(2)}) copy-start(bf16[64,256]{1,0:T(8,128)(2,1)} %refs_12_.1) | copy-start | bytes 98308
  26.7 24.3 %copy-start.4 = (bf16[256,256]{1,0:T(8,128)(2,1)S(1)}, bf16[256,256]{1,0:T(8,128)(2,1)}, u32[]{:S(2)}) copy-start(bf16[256,256]{1,0:T(8,128)(2,1)} %refs_17_.1) | copy-start | bytes 393220
  26.7 24.3 %copy-start.5 = (bf16[256,256]{1,0:T(8,128)(2,1)S(1)}, bf16[256,256]{1,0:T(8,128)(2,1)}, u32[]{:S(2)}) copy-start(bf16[256,256]{1,0:T(8,128)(2,1)} %refs_18_.1) | copy-start | bytes 393220
  26.7 24.3 %copy-start.8 = (f32[256]{0:T(256)S(1)}, f32[256]{0:T(256)}, u32[]{:S(2)}) copy-start(f32[256]{0:T(256)} %param.17) | copy-start | bytes 3076
  26.8 24.3 %copy-start.10 = (f32[256]{0:T(256)S(1)}, f32[256]{0:T(256)}, u32[]{:S(2)}) copy-start(f32[256]{0:T(256)} %param.18) | copy-start | bytes 3076
  26.8 10.2 %collective-permute-start.4 = (bf16[384,256]{1,0:T(8,128)(2,1)S(1)}, bf16[384,256]{1,0:T(8,128)(2,1)S(1)}, u32[]{:S(2)}, u32[]{:S(2)}) collective-permute-start(bf16[384,256]{1,0:T(8,128)(2,1)S(1)} %get-tuple-element.32.refs_2_), channel_id=1, source_target_pairs={{0,16},{8,24},{16,0},{24,8},{1,17},{9,25},{17,1},{25,9},{2,18},{10... | collective-permute-start | bytes 589832 | tf_op jit(solution)/shard_map/ppermute | solution.py:482
  31.6 5.3 %collective-permute-start.3 = (bf16[256,256]{1,0:T(8,128)(2,1)S(1)}, bf16[256,256]{1,0:T(8,128)(2,1)S(1)}, u32[]{:S(2)}, u32[]{:S(2)}) collective-permute-start(bf16[256,256]{1,0:T(8,128)(2,1)S(1)} %get-tuple-element.31.refs_0_), channel_id=1, source_target_pairs={{0,16},{8,24},{16,0},{24,8},{1,17},{9,25},{17,1},{25,9},{2,18},{10... | collective-permute-start | bytes 393224 | tf_op jit(solution)/shard_map/ppermute | solution.py:482
  37.5 1.6 %collective-permute-start.8 = (f32[8,256]{1,0:T(8,128)S(1)}, f32[8,256]{1,0:T(8,128)S(1)}, u32[]{:S(2)}, u32[]{:S(2)}) collective-permute-start(f32[8,256]{1,0:T(8,128)S(1)} %get-tuple-element.44), channel_id=1, source_target_pairs={{0,8},{8,0},{16,24},{24,16},{1,9},{9,1},{17,25},{25,17},{2,10},{10... | collective-permute-start | bytes 24584 | tf_op jit(solution)/shard_map/ppermute | solution.py:482
  37.5 13.4 %collective-permute-start.7 = (bf16[64,256]{1,0:T(8,128)(2,1)S(1)}, bf16[64,256]{1,0:T(8,128)(2,1)S(1)}, u32[]{:S(2)}, u32[]{:S(2)}) collective-permute-start(bf16[64,256]{1,0:T(8,128)(2,1)S(1)} %copy-done.6), channel_id=1, source_target_pairs={{0,16},{8,24},{16,0},{24,8},{1,17},{9,25},{17,1},{25,9},{2,18},{10... | collective-permute-start | bytes 98312 | tf_op jit(solution)/shard_map/ppermute | solution.py:482
  39.0 3.7 %collective-permute-start.9 = (f32[8,256]{1,0:T(8,128)S(1)}, f32[8,256]{1,0:T(8,128)S(1)}, u32[]{:S(2)}, u32[]{:S(2)}) collective-permute-start(f32[8,256]{1,0:T(8,128)S(1)} %join.4.mine_ref), channel_id=1, source_target_pairs={{0,1},{1,0},{2,3},{3,2},{4,5},{5,4},{6,7},{7,6},{8,9},{9,8},{10,11... | collective-permute-start | bytes 24584 | tf_op jit(solution)/shard_map/ppermute | solution.py:482
  42.8 3.7 %collective-permute-start.10 = (f32[8,256]{1,0:T(8,128)S(1)}, f32[8,256]{1,0:T(8,128)S(1)}, u32[]{:S(2)}, u32[]{:S(2)}) collective-permute-start(f32[8,256]{1,0:T(8,128)S(1)} %join.5.mine_ref), channel_id=1, source_target_pairs={{0,2},{1,3},{2,0},{3,1},{4,6},{5,7},{6,4},{7,5},{8,10},{9,11},{10,... | collective-permute-start | bytes 24584 | tf_op jit(solution)/shard_map/ppermute | solution.py:482
  46.4 4.5 %collective-permute-start.11 = (f32[8,256]{1,0:T(8,128)S(1)}, f32[8,256]{1,0:T(8,128)S(1)}, u32[]{:S(2)}, u32[]{:S(2)}) collective-permute-start(f32[8,256]{1,0:T(8,128)S(1)} %join.6.mine_ref), channel_id=1, source_target_pairs={{0,4},{1,5},{2,6},{3,7},{4,0},{5,1},{6,2},{7,3},{8,12},{9,13},{10,... | collective-permute-start | bytes 24584 | tf_op jit(solution)/shard_map/ppermute | solution.py:482
  54.8 2.2 %collective-permute-start.12 = (bf16[8,160,256]{2,1,0:T(8,128)(2,1)S(1)}, bf16[8,160,256]{2,1,0:T(8,128)(2,1)S(1)}, u32[]{:S(2)}, u32[]{:S(2)}) collective-permute-start(bf16[8,160,256]{2,1,0:T(8,128)(2,1)S(1)} %get-tuple-element.47), channel_id=1, source_target_pairs={{0,8},{8,0},{16,24},{24,16},{1,9},{9,1},{17,25},{25,17},{2,10},{10... | collective-permute-start | bytes 1966088 | tf_op jit(solution)/shard_map/ppermute | solution.py:482
  54.9 2.1 %collective-permute-start.13 = (bf16[16,256]{1,0:T(8,128)(2,1)S(1)}, bf16[16,256]{1,0:T(8,128)(2,1)S(1)}, u32[]{:S(2)}, u32[]{:S(2)}) collective-permute-start(bf16[16,256]{1,0:T(8,128)(2,1)S(1)} %get-tuple-element.48.sums_ref), channel_id=1, source_target_pairs={{0,8},{8,0},{16,24},{24,16},{1,9},{9,1},{17,25},{25,17},{2,10},{10... | collective-permute-start | bytes 24584 | tf_op jit(solution)/shard_map/ppermute | solution.py:482
  58.0 24.9 %all-to-all-start = ((bf16[8,176,256]{2,1,0:T(8,128)(2,1)}), bf16[8,176,256]{2,1,0:T(8,128)(2,1)S(1)}, u32[]{:S(2)}, u32[]{:S(2)}) async-start(bf16[8,176,256]{2,1,0:T(8,128)(2,1)} %merge.1), calls=%async_computation | async-start | bytes 1441792 | tf_op jit(solution)/shard_map/all_to_all | solution.py:600
  83.7 5.4 %collective-permute-start.14 = (bf16[1,96,256]{2,1,0:T(8,128)(2,1)S(1)}, bf16[1,96,256]{2,1,0:T(8,128)(2,1)S(1)}, u32[]{:S(2)}, u32[]{:S(2)}) collective-permute-start(bf16[1,96,256]{2,1,0:T(8,128)(2,1)S(1)} %bitcast.11), channel_id=1, source_target_pairs={{0,4},{1,5},{2,6},{3,7},{4,0},{5,1},{6,2},{7,3},{8,12},{9,13},{10,... | collective-permute-start | bytes 147464 | tf_op jit(solution)/shard_map/ppermute | solution.py:482
  89.1 4.7 %collective-permute-start.15 = (bf16[2,96,256]{2,1,0:T(8,128)(2,1)S(1)}, bf16[2,96,256]{2,1,0:T(8,128)(2,1)S(1)}, u32[]{:S(2)}, u32[]{:S(2)}) collective-permute-start(bf16[2,96,256]{2,1,0:T(8,128)(2,1)S(1)} %pad_maximum_fusion.2), channel_id=1, source_target_pairs={{0,2},{1,3},{2,0},{3,1},{4,6},{5,7},{6,4},{7,5},{8,10},{9,11},{10,... | collective-permute-start | bytes 294920 | tf_op jit(solution)/shard_map/ppermute | solution.py:482
  93.8 5.7 %collective-permute-start.16 = (bf16[4,96,256]{2,1,0:T(8,128)(2,1)S(1)}, bf16[4,96,256]{2,1,0:T(8,128)(2,1)S(1)}, u32[]{:S(2)}, u32[]{:S(2)}) collective-permute-start(bf16[4,96,256]{2,1,0:T(8,128)(2,1)S(1)} %pad_maximum_fusion.1), channel_id=1, source_target_pairs={{0,1},{1,0},{2,3},{3,2},{4,5},{5,4},{6,7},{7,6},{8,9},{9,8},{10,11... | collective-permute-start | bytes 589832 | tf_op jit(solution)/shard_map/ppermute | solution.py:482
  100.4 1.5 %collective-permute-start.17 = (f32[256,256]{1,0:T(8,128)S(1)}, f32[256,256]{1,0:T(8,128)S(1)}, u32[]{:S(2)}, u32[]{:S(2)}) collective-permute-start(f32[256,256]{1,0:T(8,128)S(1)} %get-tuple-element.52), channel_id=1, source_target_pairs={{0,8},{8,0},{16,24},{24,16},{1,9},{9,1},{17,25},{25,17},{2,10},{10... | collective-permute-start | bytes 786440 | tf_op jit(solution)/shard_map/ppermute | solution.py:482

commit v4 on v3

--- a/solution.py
+++ b/solution.py
@@ -28,7 +28,6 @@
 
 VMEM = pl.BlockSpec(memory_space=pltpu.VMEM)
 SMEM = pl.BlockSpec(memory_space=pltpu.SMEM)
-HBM = pl.BlockSpec(memory_space=pltpu.HBM)
 
 
 def halves(value):
@@ -38,21 +37,16 @@
 
 def build_kernel(
     place_ref,
-    seed_in,
-    near_in,
-    far_in,
+    own_ref,
+    far_ref,
     out_ref,
-    seed_ref,
-    near_ref,
-    far_ref,
     keys,
     own_group,
     spread,
     own_slot,
-    sems,
 ):
     groups = LANES // GROUP
-    per_slot = seed_ref.shape[1] // (2 * LANES)
+    per_slot = own_ref.shape[1] // (2 * LANES)
     step, steps = pl.program_id(0), pl.num_programs(0)
     first_core = place_ref[1] == 0
 
@@ -98,31 +92,23 @@
 
     @pl.when(step == 0)
     def _():
-        copies = [
-            pltpu.make_async_copy(a, b, sems.at[i])
-            for i, (a, b) in enumerate(((seed_in, seed_ref), (near_in, near_ref), (far_in, far_ref)))
-        ]
-        for copy in copies:
-            copy.start()
         own_group[...] = flag((LANES, LANES), lambda r, c: r // SLOT == c // GROUP)
         spread[...] = flag((LANES, LOW), lambda r, c: r % GROUP == c % GROUP)
         own_slot[...] = flag((LANES, LOW), lambda r, c: r % SLOT == c // GROUP)
-        for copy in copies:
-            copy.wait()
-        keep(keys_of(*wide_of(near_ref[...], seed_ref[...], 0)), 0)
+        keep(keys_of(*wide_of(own_ref[1:, :], own_ref[0:1, :], 0)), 0)
 
     now = step % 2
     later = jnp.minimum(step + 1, steps - 1)
     slot = later // per_slot
     back = jnp.maximum(slot - 1, 0)
     ids = far_ref[back, :, :]
-    self_row = near_ref[pl.ds(back, 1), :]
+    self_row = own_ref[pl.ds(back + 1, 1), :]
     if per_slot > 1:
         padded = jnp.concatenate(
-            [near_ref[...], jnp.full((ids.shape[0] - near_ref.shape[0], ids.shape[1]), -1, jnp.int32)]
+            [own_ref[1:, :], jnp.full((ids.shape[0] + 1 - own_ref.shape[0], ids.shape[1]), -1, jnp.int32)]
         )
         ids = jnp.where(slot == 0, padded, ids)
-        self_row = jnp.where(slot == 0, seed_ref[...], self_row)
+        self_row = jnp.where(slot == 0, own_ref[0:1, :], self_row)
     later_wide = wide_of(ids, self_row, later % per_slot)
 
     index = lax.broadcasted_iota(jnp.int32, (LOW, LOW), 0).astype(BF)
@@ -164,24 +150,20 @@
     keep(later_keys, 1 - now)
 
 
-def build_rows(place, seeds, near, far, table_rows):
-    steps = (near.shape[0] + 1) * seeds.shape[1] // (2 * LANES)
+def build_rows(place, own, far, table_rows):
+    steps = own.shape[0] * own.shape[1] // (2 * LANES)
     groups = LANES // GROUP
     return pl.pallas_call(
         build_kernel,
         grid=(steps,),
-        in_specs=[SMEM, HBM, HBM, HBM],
+        in_specs=[SMEM, VMEM, VMEM],
         out_specs=pl.BlockSpec((2 * LANES, table_rows), lambda i: (i, 0)),
         out_shape=jax.ShapeDtypeStruct((steps * 2 * LANES, table_rows), BF),
         scratch_shapes=[
-            pltpu.VMEM(seeds.shape, jnp.int32),
-            pltpu.VMEM(near.shape, jnp.int32),
-            pltpu.VMEM(far.shape, jnp.int32),
             pltpu.VMEM((2, 3, groups, LOW), F32),
             pltpu.VMEM((LANES, LANES), BF),
             pltpu.VMEM((LANES, LOW), BF),
             pltpu.VMEM((LANES, LOW), BF),
-            pltpu.SemaphoreType.DMA((3,)),
         ],
         compiler_params=params(12),
         cost_estimate=pl.CostEstimate(
@@ -190,7 +172,7 @@
             transcendentals=0,
         ),
         name="build_rows",
-    )(place, seeds, near, far)
+    )(place, own, far)
 
 
 def pick_kernel(
@@ -425,31 +407,64 @@
             ref[d, :, :] = jnp.concatenate(parts, axis=0).astype(ref.dtype)
 
 
-def merge_kernel(keep_ref, got_ref, sums_ref, got_sums_ref, out_ref):
-    batches, rows, _ = keep_ref.shape
-    mine, theirs = sums_ref[...].astype(F32), got_sums_ref[...].astype(F32)
+def joined_sums(mine, theirs):
     sums = []
     for j in (0, 2):
-        sums += halves(
-            (mine[j : j + 1] + mine[j + 1 : j + 2]) + (theirs[j : j + 1] + theirs[j + 1 : j + 2])
-        )
-    tail = jnp.concatenate(
-        [s.astype(F32) for s in sums] + [jnp.zeros((12, mine.shape[1]), F32)], axis=0
-    ).astype(BF)
-    for d in range(batches):
-        out_ref[d, :rows, :] = (keep_ref[d, :, :] + got_ref[d, :, :].astype(F32)).astype(BF)
-        out_ref[d, rows:, :] = tail
-
-
-def finish_kernel(row_total, parts_ref, stats_ref, gain_ref, column_ref, out_ref, gain_out, shift_out):
-    batches, all_rows, _ = parts_ref.shape
-    total = parts_ref[0, :, :].astype(F32)
-    for d in range(1, batches):
-        total = total + parts_ref[d, :, :].astype(F32)
-    rows = all_rows - 16
+        sums += halves((mine[j : j + 1] + mine[j + 1 : j + 2]) + (theirs[j : j + 1] + theirs[j + 1 : j + 2]))
+    fill = jnp.zeros((12, mine.shape[1]), F32)
+    return jnp.concatenate([s.astype(F32) for s in sums] + [fill], axis=0)
+
+
+def merge_kernel(
+    orders, place_ref, keep_ref, got_ref, sums_ref, got_sums_ref, kept_ref, sent_ref, tail_ref
+):
+    batches, rows, _ = keep_ref.shape
+    tail = joined_sums(sums_ref[...].astype(F32), got_sums_ref[...].astype(F32)).astype(BF)
+    half = batches // 2
+    for i in range(batches):
+        d = place_ref[2] ^ jnp.where(place_ref[1] == 0, orders[0][i], orders[1][i])
+        value = keep_ref[d, :, :] + got_ref[d, :, :].astype(F32)
+        if i < half:
+            kept_ref[i, :, :] = value
+        else:
+            sent_ref[(i - half) * rows : (i - half + 1) * rows, :] = value.astype(BF)
+    sent_ref[half * rows :, :] = tail
+    tail_ref[...] = tail
+
+
+def halve_kernel(keep_ref, got_ref, tail_ref, kept_ref, sent_ref, new_tail_ref):
+    pieces, rows, _ = keep_ref.shape
+    half = pieces // 2
+    got_tail = got_ref[pieces * rows :, :].astype(F32)
+    tail = joined_sums(tail_ref[...].astype(F32), got_tail).astype(BF)
+    for i in range(pieces):
+        value = keep_ref[i, :, :] + got_ref[i * rows : (i + 1) * rows, :].astype(F32)
+        if i < half:
+            kept_ref[i, :, :] = value
+        else:
+            sent_ref[(i - half) * rows : (i - half + 1) * rows, :] = value.astype(BF)
+    sent_ref[half * rows :, :] = tail
+    new_tail_ref[...] = tail
+
+
+def finish_kernel(
+    row_total,
+    keep_ref,
+    got_ref,
+    tail_ref,
+    stats_ref,
+    gain_ref,
+    column_ref,
+    out_ref,
+    gain_out,
+    shift_out,
+):
+    rows = keep_ref.shape[1]
+    total = keep_ref[0, :, :] + got_ref[:rows, :].astype(F32)
+    sums = joined_sums(tail_ref[...].astype(F32), got_ref[rows:, :].astype(F32))
     pieces = column_ref.shape[1]
-    grad_gain = total[rows : rows + 1] + total[rows + 1 : rows + 2]
-    grad_shift = total[rows + 2 : rows + 3] + total[rows + 3 : rows + 4]
+    grad_gain = sums[0:1] + sums[1:2]
+    grad_shift = sums[2:3] + sums[3:4]
     inv_std = lax.rsqrt(stats_ref[1:2, :] / row_total + 1e-05)
     outer = dot(
         column_ref[...],
@@ -465,9 +480,15 @@
     shift_out[...] = grad_shift
 
 
-def place_kernel(masks, group_ref, parts_ref, self_ref, neigh_ref, upper_ref):
+def place_kernel(
+    masks, group_ref, parts_ref, gain_ref, shift_ref, self_ref, neigh_ref, upper_ref
+):
     piece = self_ref.shape[0] // len(masks)
-    upper_piece = upper_ref.shape[0] // len(masks)
+    upper_piece = (upper_ref.shape[0] - 8) // len(masks)
+    hidden_width = upper_ref.shape[1]
+    upper_ref[upper_ref.shape[0] - 8 :, :] = jnp.concatenate(
+        [gain_ref[...], shift_ref[...], jnp.zeros((6, hidden_width), F32)], axis=0
+    )
     for i, mask in enumerate(masks):
         d = group_ref[0] ^ mask
         rows = parts_ref[i, :, :].astype(F32)
@@ -513,10 +534,9 @@
     peer_neigh = swap(lower_neighbour, "feat", 1)
     grads = [embed_grad] + [swap(embed_grad, "feat", 2 * mask) for mask in range(1, chips)]
 
-    place = jnp.stack([chip, core]).astype(jnp.int32)
-    picks = build_rows(
-        place, seed_ids[None, :], first_hop.T, second_hop.transpose(1, 2, 0), table_rows
-    )
+    place = jnp.stack([chip, core, batch]).astype(jnp.int32)
+    own_ids = jnp.concatenate([seed_ids[None, :], first_hop.T], axis=0)
+    picks = build_rows(place, own_ids, second_hop.transpose(1, 2, 0), table_rows)
 
     weights = (lower_self, peer_self, lower_neighbour, peer_neigh)
     per_slot = seeds // LANES
@@ -591,13 +611,48 @@
         name="middle",
     )(place, *operands)
 
-    parts = pl.pallas_call(
-        merge_kernel,
-        out_shape=jax.ShapeDtypeStruct((batches, per_group + 16, hidden_width), BF),
+    bits = [1 << i for i in range(batches.bit_length() - 1)]
+    rounds = (bits, bits[1::-1] + bits[2:])
+
+    def order_of(masks):
+        order = [0]
+        for mask in reversed(masks):
+            order = order + [i ^ mask for i in order]
+        return order
+
+    def kept_and_sent(pieces):
+        return [
+            jax.ShapeDtypeStruct((pieces, per_group, hidden_width), F32),
+            jax.ShapeDtypeStruct((pieces * per_group + 16, hidden_width), BF),
+            jax.ShapeDtypeStruct((16, hidden_width), BF),
+        ]
+
+    def exchange(value, step):
+        pairs = [
+            (f * batches + b, f * batches + (b ^ rounds[f % 2][step]))
+            for f in range(feats)
+            for b in range(batches)
+        ]
+        return lax.ppermute(value, ("feat", "batch"), pairs)
+
+    pieces = batches // 2
+    kept, sent, tail = pl.pallas_call(
+        functools.partial(merge_kernel, [order_of(masks) for masks in rounds]),
+        in_specs=[SMEM] + [VMEM] * 4,
+        out_shape=kept_and_sent(pieces),
         compiler_params=params(16),
         name="merge",
-    )(keep, swap(send, "feat", 1), sums, swap(sums, "feat", 1))
-    parts = lax.all_to_all(parts, "batch", 0, 0)
+    )(place, keep, swap(send, "feat", 1), sums, swap(sums, "feat", 1))
+    got = exchange(sent, 0)
+    for step in range(1, len(bits)):
+        pieces //= 2
+        kept, sent, tail = pl.pallas_call(
+            halve_kernel,
+            out_shape=kept_and_sent(pieces),
+            compiler_params=params(16),
+            name="halve",
+        )(kept, got, tail)
+        got = exchange(sent, step)
 
     piece = width // batches
     column = lax.dynamic_slice(stats[2:4], (0, batch * piece), (2, piece)).reshape(1, 2 * piece)
@@ -609,7 +664,7 @@
         out_shape=[jax.ShapeDtypeStruct((out_rows, hidden_width), BF), line, line],
         compiler_params=params(16),
         name="finish",
-    )(parts, stats, gain_row, column)
+    )(kept, got, tail, stats, gain_row, column)
 
     gathered, masks = done[None], [0]
     mask = batches // 2
@@ -619,24 +674,26 @@
         mask //= 2
     grad_self, grad_neigh, upper = pl.pallas_call(
         functools.partial(place_kernel, tuple(masks)),
-        in_specs=[SMEM, VMEM],
+        in_specs=[SMEM] + [VMEM] * 3,
         out_shape=[
             jax.ShapeDtypeStruct((width, hidden_width), F32),
             jax.ShapeDtypeStruct((width, hidden_width), F32),
-            jax.ShapeDtypeStruct((hidden_width, hidden_width), F32),
+            jax.ShapeDtypeStruct((hidden_width + 8, hidden_width), F32),
         ],
         compiler_params=params(16),
         name="place",
-    )(batch.astype(jnp.int32)[None], gathered)
+    )(batch.astype(jnp.int32)[None], gathered, grad_gain, grad_shift)
     upper_other = swap(upper, "feat", 1)
+    first = jnp.where(core == 0, upper, upper_other)
+    second = jnp.where(core == 0, upper_other, upper)
     return (
         embedding,
         grad_self,
         grad_neigh,
-        jnp.where(core == 0, upper, upper_other),
-        jnp.where(core == 0, upper_other, upper),
-        grad_gain[0],
-        grad_shift[0],
+        first[:hidden_width],
+        second[:hidden_width],
+        first[hidden_width],
+        first[hidden_width + 1],
     )
 
 

time: 103 us -> 95.6 us (0.928)
  waiting for transfers between devices: 48 us -> 35.9 us
  starting transfers between devices: 20.8 us -> 26.1 us
  Pallas kernels: 29.6 us -> 28.4 us
    all_to_all x1 -> x0, waiting for transfers between devices: 18.9 us -> none  [on_device(): parts = lax.all_to_all(parts, 'batch', 0, 0)]
    ppermute x0 -> x3, waiting for transfers between devices: none -> 12.1 us  [exchange(): return lax.ppermute(value, ('feat', 'batch'), pairs)]
    ppermute x0 -> x3, starting transfers between devices: none -> 5.91 us  [exchange(): return lax.ppermute(value, ('feat', 'batch'), pairs)]
    all_to_all x1 -> x0, starting transfers between devices: 5.83 us -> none  [on_device(): parts = lax.all_to_all(parts, 'batch', 0, 0)]
    ppermute x18, waiting for transfers between devices: 29.1 us -> 23.7 us  [swap(): lax.ppermute(value, axis, [(i, i ^ mask) for i in range(lax.axis_size(axi...]
    ppermute x18, starting transfers between devices: 15 us -> 20.2 us  [swap(): lax.ppermute(value, axis, [(i, i ^ mask) for i in range(lax.axis_size(axi...]
    unnamed x22 -> x18, local copies, waits for them, and re-layouts: 2.35 us -> 0.96 us
    slice x0 -> x2, local copies, waits for them, and re-layouts: none -> 1.29 us  [the longest x1 0.72 us: on_device(): first[:hidden_width]]
  transfers between devices with their start and end apart: 19 -> 21, of which waited for: 10 -> 12; matrix products, arithmetic and copies ran while one was open for 0% -> 1% of each run, Pallas kernels for 18% -> 19%
where the time goes in v4:
time: 95.6 us; the launch traced here: 95.3 us
  waiting for transfers between devices  35.9 us (38%)
  Pallas kernels  28.4 us (30%)
  starting transfers between devices  26.1 us (27%)
  local copies, waits for them, and re-layouts  2.41 us (3%)
  other arithmetic  1.65 us (2%)
    ppermute x18, waiting for transfers between devices, swap(): lax.ppermute(value, axis, [(i, i ^ mask) for i in range(lax.axis_size(axi...  23.7 us
    ppermute x18, starting transfers between devices, swap(): lax.ppermute(value, axis, [(i, i ^ mask) for i in range(lax.axis_size(axi...  20.2 us
    pallas_call x4, Pallas kernels, pick_rows(): pl.pallas_call(functools.partial(pick_kernel, first_block, start, blocks,...  13.8 us
    ppermute x3, waiting for transfers between devices, exchange(): return lax.ppermute(value, ('feat', 'batch'), pairs)  12.1 us
    pallas_call x1, Pallas kernels, build_rows(): pl.pallas_call(build_kernel, grid=(steps,), in_specs=[SMEM, VMEM, VMEM],...  8.3 us
    ppermute x3, starting transfers between devices, exchange(): return lax.ppermute(value, ('feat', 'batch'), pairs)  5.91 us
    pallas_call x1, Pallas kernels, on_device(): pl.pallas_call(functools.partial(middle_kernel, len(CHUNKS), slots, row_t...  3.78 us
  transfers between devices with their start and end apart: 21, of which 12 were waited for; matrix products, arithmetic and copies ran while one was open for 1% of the time, Pallas kernels for 19%

profile of v4, /device:TPU:0, one launch (start us, length us, event | category | flops | bytes accessed | tf_op | source)
XLA Modules:
  0.0 95.3 jit_solution(103601257261049073)
XLA Ops:
  0.6 0.5 collective-permute-start
  1.1 0.1 collective-permute-start.1
  1.2 0.4 collective-permute-start.2
  1.7 0.1 pad_add_fusion.1.place_ref
  1.7 0.7 pad_add_fusion.own_ref
  2.5 0.9 copy-done.3
  3.4 8.3 %build_rows.1.rows_ref = bf16[2816,4096]{1,0:T(8,128)(2,1)S(1)} custom-call(s32[3]{0:T(128)S(1)} %pad_add_fusion.1.place_ref, s32[11,256]{1,0:T(8,128)S(1)} %pad_add_fusion.own_ref, s32[10,15,256]{2,1,0:T(8,128)S(1)} %bitcast.15), custom_call_target="tpu_custom_call" | custom-call | flops 2952790016 | bytes 23068672 | tf_op jit(solution)/shard_map/build_rows/pallas_call | solution.py:156
  11.7 0.0 collective-permute-done.1.self_peer_ref
  11.7 0.0 collective-permute-done.2.neigh_peer_ref
  11.7 0.0 collective-permute-done.peer_ref
  11.8 3.7 %pick_rows.7 = (bf16[1024,384]{1,0:T(8,128)(2,1)S(1)}, bf16[384,256]{1,0:T(8,128)(2,1)S(1)}, f32[8,1024]{1,0:T(8,128)S(1)}) custom-call(bf16[2816,4096]{1,0:T(8,128)(2,1)S(1)} %build_rows.1.rows_ref, bf16[4096,256]{1,0:T(8,128)(2,1)S(1)} %copy-done, bf16[4096,256]{1,0:T(8,128)(2,1)S(1)} %collective-permute-done.peer_ref, bf16[256,256]{1,0:T(8,128)(2,1)S(1)} %copy-done.1, ...), custom_call_target="tpu_custom_call" | custom-call | flops 3221225472 | bytes 7340032 | tf_op jit(solution)/shard_map/pick_rows/pallas_call | solution.py:245
  15.5 2.6 %collective-permute-start.6 = (bf16[384,256]{1,0:T(8,128)(2,1)S(1)}, bf16[384,256]{1,0:T(8,128)(2,1)S(1)}, u32[]{:S(2)}, u32[]{:S(2)}) collective-permute-start(bf16[384,256]{1,0:T(8,128)(2,1)S(1)} %get-tuple-element.43.refs_6_), channel_id=1, source_target_pairs={{0,16},{8,24},{16,0},{24,8},{1,17},{9,25},{17,1},{25,9},{2,18},{10... | collective-permute-start | bytes 589832 | tf_op jit(solution)/shard_map/ppermute | solution.py:503
  18.1 3.7 %pick_rows.6 = (bf16[1024,384]{1,0:T(8,128)(2,1)S(1)}, bf16[384,256]{1,0:T(8,128)(2,1)S(1)}, f32[8,1024]{1,0:T(8,128)S(1)}) custom-call(bf16[2816,4096]{1,0:T(8,128)(2,1)S(1)} %build_rows.1.rows_ref, bf16[4096,256]{1,0:T(8,128)(2,1)S(1)} %copy-done, bf16[4096,256]{1,0:T(8,128)(2,1)S(1)} %collective-permute-done.peer_ref, bf16[256,256]{1,0:T(8,128)(2,1)S(1)} %copy-done.1, ...), custom_call_target="tpu_custom_call" | custom-call | flops 3221225472 | bytes 7340032 | tf_op jit(solution)/shard_map/pick_rows/pallas_call | solution.py:245
  21.8 0.1 collective-permute-start.5
  21.9 3.7 %pick_rows.5 = (bf16[1024,384]{1,0:T(8,128)(2,1)S(1)}, bf16[384,256]{1,0:T(8,128)(2,1)S(1)}, f32[8,1024]{1,0:T(8,128)S(1)}) custom-call(bf16[2816,4096]{1,0:T(8,128)(2,1)S(1)} %build_rows.1.rows_ref, bf16[4096,256]{1,0:T(8,128)(2,1)S(1)} %copy-done, bf16[4096,256]{1,0:T(8,128)(2,1)S(1)} %collective-permute-done.peer_ref, bf16[256,256]{1,0:T(8,128)(2,1)S(1)} %copy-done.1, ...), custom_call_target="tpu_custom_call" | custom-call | flops 3221225472 | bytes 7340032 | tf_op jit(solution)/shard_map/pick_rows/pallas_call | solution.py:245
  25.6 0.0 copy-start.6
  25.6 0.0 copy-start.4
  25.6 0.0 copy-start.5
  25.6 0.0 copy-start.7
  25.6 0.0 copy-start.8
  25.6 2.1 %collective-permute-start.4 = (bf16[384,256]{1,0:T(8,128)(2,1)S(1)}, bf16[384,256]{1,0:T(8,128)(2,1)S(1)}, u32[]{:S(2)}, u32[]{:S(2)}) collective-permute-start(bf16[384,256]{1,0:T(8,128)(2,1)S(1)} %get-tuple-element.41.refs_2_), channel_id=1, source_target_pairs={{0,16},{8,24},{16,0},{24,8},{1,17},{9,25},{17,1},{25,9},{2,18},{10... | collective-permute-start | bytes 589832 | tf_op jit(solution)/shard_map/ppermute | solution.py:503
  27.7 2.7 %pick_rows.4 = (bf16[1024,256]{1,0:T(8,128)(2,1)S(1)}, bf16[256,256]{1,0:T(8,128)(2,1)S(1)}, f32[8,1024]{1,0:T(8,128)S(1)}) custom-call(bf16[2816,4096]{1,0:T(8,128)(2,1)S(1)} %build_rows.1.rows_ref, bf16[4096,256]{1,0:T(8,128)(2,1)S(1)} %copy-done, bf16[4096,256]{1,0:T(8,128)(2,1)S(1)} %collective-permute-done.peer_ref, bf16[256,256]{1,0:T(8,128)(2,1)S(1)} %copy-done.1, ...), custom_call_target="tpu_custom_call" | custom-call | flops 2147483648 | bytes 6291456 | tf_op jit(solution)/shard_map/pick_rows/pallas_call | solution.py:245
  30.5 0.1 collective-permute-start.3
  30.6 5.3 %collective-permute-done.3.refs_1_ = bf16[256,256]{1,0:T(8,128)(2,1)S(1)} collective-permute-done((bf16[256,256]{1,0:T(8,128)(2,1)S(1)}, bf16[256,256]{1,0:T(8,128)(2,1)S(1)}, u32[]{:S(2)}, u32[]{:S(2)}) %collective-permute-start.3) | collective-permute-done | bytes 131104 | tf_op jit(solution)/shard_map/ppermute | solution.py:503
  35.8 0.0 collective-permute-done.6.refs_7_
  35.9 0.0 collective-permute-done.5.refs_5_
  35.9 0.5 stats.1
  36.4 0.1 collective-permute-start.8
  36.5 1.4 %collective-permute-start.7 = (bf16[64,256]{1,0:T(8,128)(2,1)S(1)}, bf16[64,256]{1,0:T(8,128)(2,1)S(1)}, u32[]{:S(2)}, u32[]{:S(2)}) collective-permute-start(bf16[64,256]{1,0:T(8,128)(2,1)S(1)} %copy-done.6), channel_id=1, source_target_pairs={{0,16},{8,24},{16,0},{24,8},{1,17},{9,25},{17,1},{25,9},{2,18},{10... | collective-permute-start | bytes 98312 | tf_op jit(solution)/shard_map/ppermute | solution.py:503
  37.9 0.0 collective-permute-done.8.other_ref
  37.9 1.6 %collective-permute-start.9 = (f32[8,256]{1,0:T(8,128)S(1)}, f32[8,256]{1,0:T(8,128)S(1)}, u32[]{:S(2)}, u32[]{:S(2)}) collective-permute-start(f32[8,256]{1,0:T(8,128)S(1)} %join.4.mine_ref), channel_id=1, source_target_pairs={{0,1},{1,0},{2,3},{3,2},{4,5},{5,4},{6,7},{7,6},{8,9},{9,8},{10,11... | collective-permute-start | bytes 24584 | tf_op jit(solution)/shard_map/ppermute | solution.py:503
  39.5 2.1 %collective-permute-done.9.other_ref = f32[8,256]{1,0:T(8,128)S(1)} collective-permute-done((f32[8,256]{1,0:T(8,128)S(1)}, f32[8,256]{1,0:T(8,128)S(1)}, u32[]{:S(2)}, u32[]{:S(2)}) %collective-permute-start.9) | collective-permute-done | bytes 8224 | tf_op jit(solution)/shard_map/ppermute | solution.py:503
  41.6 1.6 %collective-permute-start.10 = (f32[8,256]{1,0:T(8,128)S(1)}, f32[8,256]{1,0:T(8,128)S(1)}, u32[]{:S(2)}, u32[]{:S(2)}) collective-permute-start(f32[8,256]{1,0:T(8,128)S(1)} %join.5.mine_ref), channel_id=1, source_target_pairs={{0,2},{1,3},{2,0},{3,1},{4,6},{5,7},{6,4},{7,5},{8,10},{9,11},{10,... | collective-permute-start | bytes 24584 | tf_op jit(solution)/shard_map/ppermute | solution.py:503
  43.2 2.1 %collective-permute-done.10.other_ref = f32[8,256]{1,0:T(8,128)S(1)} collective-permute-done((f32[8,256]{1,0:T(8,128)S(1)}, f32[8,256]{1,0:T(8,128)S(1)}, u32[]{:S(2)}, u32[]{:S(2)}) %collective-permute-start.10) | collective-permute-done | bytes 8224 | tf_op jit(solution)/shard_map/ppermute | solution.py:503
  45.3 2.6 %collective-permute-start.11 = (f32[8,256]{1,0:T(8,128)S(1)}, f32[8,256]{1,0:T(8,128)S(1)}, u32[]{:S(2)}, u32[]{:S(2)}) collective-permute-start(f32[8,256]{1,0:T(8,128)S(1)} %join.6.mine_ref), channel_id=1, source_target_pairs={{0,4},{1,5},{2,6},{3,7},{4,0},{5,1},{6,2},{7,3},{8,12},{9,13},{10,... | collective-permute-start | bytes 24584 | tf_op jit(solution)/shard_map/ppermute | solution.py:503
  47.9 2.0 %collective-permute-done.11.other_ref = f32[8,256]{1,0:T(8,128)S(1)} collective-permute-done((f32[8,256]{1,0:T(8,128)S(1)}, f32[8,256]{1,0:T(8,128)S(1)}, u32[]{:S(2)}, u32[]{:S(2)}) %collective-permute-start.11) | collective-permute-done | bytes 8224 | tf_op jit(solution)/shard_map/ppermute | solution.py:503
  49.9 0.0 collective-permute-done.7.refs_13_
  49.9 3.8 %middle.1 = (bf16[64,256]{1,0:T(8,128)(2,1)}, f32[8,160,256]{2,1,0:T(8,128)S(1)}, bf16[8,160,256]{2,1,0:T(8,128)(2,1)S(1)}, bf16[16,256]{1,0:T(8,128)(2,1)S(1)}) custom-call(s32[3]{0:T(128)S(1)} %pad_add_fusion.1.place_ref, bf16[256,256]{1,0:T(8,128)(2,1)S(1)} %get-tuple-element.40.refs_0_, bf16[256,256]{1,0:T(8,128)(2,1)S(1)} %collective-permute-done.3.refs_1_, ...), custom_call_target="tpu_custom_call" | custom-call | tf_op jit(solution)/shard_map/middle/pallas_call | solution.py:596
  53.7 0.1 collective-permute-start.12
  53.8 0.5 collective-permute-start.13
  54.3 1.6 %collective-permute-done.13.got_sums_ref = bf16[16,256]{1,0:T(8,128)(2,1)S(1)} collective-permute-done((bf16[16,256]{1,0:T(8,128)(2,1)S(1)}, bf16[16,256]{1,0:T(8,128)(2,1)S(1)}, u32[]{:S(2)}, u32[]{:S(2)}) %collective-permute-start.13) | collective-permute-done | bytes 8224 | tf_op jit(solution)/shard_map/ppermute | solution.py:503
  55.9 0.0 collective-permute-done.12.got_ref
  55.9 0.7 merge.1
  56.5 1.6 %collective-permute-start.14 = (bf16[656,256]{1,0:T(8,128)(2,1)S(1)}, bf16[656,256]{1,0:T(8,128)(2,1)S(1)}, u32[]{:S(2)}, u32[]{:S(2)}) collective-permute-start(bf16[656,256]{1,0:T(8,128)(2,1)S(1)} %get-tuple-element.59), channel_id=1, source_target_pairs={{0,1},{1,0},{2,3},{3,2},{4,5},{5,4},{6,7},{7,6},{8,10},{9,11},{10,... | collective-permute-start | bytes 1007624 | tf_op jit(solution)/shard_map/ppermute | solution.py:636
  58.1 5.6 %collective-permute-done.14.got_ref = bf16[656,256]{1,0:T(8,128)(2,1)S(1)} collective-permute-done((bf16[656,256]{1,0:T(8,128)(2,1)S(1)}, bf16[656,256]{1,0:T(8,128)(2,1)S(1)}, u32[]{:S(2)}, u32[]{:S(2)}) %collective-permute-start.14) | collective-permute-done | bytes 335904 | tf_op jit(solution)/shard_map/ppermute | solution.py:636
  63.8 0.1 halve.2
  63.9 1.7 %collective-permute-start.15 = (bf16[336,256]{1,0:T(8,128)(2,1)S(1)}, bf16[336,256]{1,0:T(8,128)(2,1)S(1)}, u32[]{:S(2)}, u32[]{:S(2)}) collective-permute-start(bf16[336,256]{1,0:T(8,128)(2,1)S(1)} %get-tuple-element.62), channel_id=1, source_target_pairs={{0,2},{1,3},{2,0},{3,1},{4,6},{5,7},{6,4},{7,5},{8,9},{9,8},{10,11... | collective-permute-start | bytes 516104 | tf_op jit(solution)/shard_map/ppermute | solution.py:636
  65.5 3.8 %collective-permute-done.15.got_ref = bf16[336,256]{1,0:T(8,128)(2,1)S(1)} collective-permute-done((bf16[336,256]{1,0:T(8,128)(2,1)S(1)}, bf16[336,256]{1,0:T(8,128)(2,1)S(1)}, u32[]{:S(2)}, u32[]{:S(2)}) %collective-permute-start.15) | collective-permute-done | bytes 172064 | tf_op jit(solution)/shard_map/ppermute | solution.py:636
  69.4 2.7 %collective-permute-start.16 = (bf16[176,256]{1,0:T(8,128)(2,1)S(1)}, bf16[176,256]{1,0:T(8,128)(2,1)S(1)}, u32[]{:S(2)}, u32[]{:S(2)}) collective-permute-start(bf16[176,256]{1,0:T(8,128)(2,1)S(1)} %get-tuple-element.65), channel_id=1, source_target_pairs={{0,4},{1,5},{2,6},{3,7},{4,0},{5,1},{6,2},{7,3},{8,12},{9,13},{10,... | collective-permute-start | bytes 270344 | tf_op jit(solution)/shard_map/ppermute | solution.py:636
  72.0 0.1 constant_dynamic-slice_fusion
  72.1 0.1 reshape.17
  72.2 2.7 %collective-permute-done.16.got_ref = bf16[176,256]{1,0:T(8,128)(2,1)S(1)} collective-permute-done((bf16[176,256]{1,0:T(8,128)(2,1)S(1)}, bf16[176,256]{1,0:T(8,128)(2,1)S(1)}, u32[]{:S(2)}, u32[]{:S(2)}) %collective-permute-start.16) | collective-permute-done | bytes 90144 | tf_op jit(solution)/shard_map/ppermute | solution.py:636
  74.9 0.3 finish.1
  75.1 2.7 %collective-permute-start.17 = (bf16[1,96,256]{2,1,0:T(8,128)(2,1)S(1)}, bf16[1,96,256]{2,1,0:T(8,128)(2,1)S(1)}, u32[]{:S(2)}, u32[]{:S(2)}) collective-permute-start(bf16[1,96,256]{2,1,0:T(8,128)(2,1)S(1)} %bitcast.11), channel_id=1, source_target_pairs={{0,4},{1,5},{2,6},{3,7},{4,0},{5,1},{6,2},{7,3},{8,12},{9,13},{10,... | collective-permute-start | bytes 147464 | tf_op jit(solution)/shard_map/ppermute | solution.py:503
  77.9 2.4 %collective-permute-done.17 = bf16[1,96,256]{2,1,0:T(8,128)(2,1)S(1)} collective-permute-done((bf16[1,96,256]{2,1,0:T(8,128)(2,1)S(1)}, bf16[1,96,256]{2,1,0:T(8,128)(2,1)S(1)}, u32[]{:S(2)}, u32[]{:S(2)}) %collective-permute-start.17) | collective-permute-done | bytes 49184 | tf_op jit(solution)/shard_map/ppermute | solution.py:503
  80.3 2.1 %collective-permute-start.18 = (bf16[2,96,256]{2,1,0:T(8,128)(2,1)S(1)}, bf16[2,96,256]{2,1,0:T(8,128)(2,1)S(1)}, u32[]{:S(2)}, u32[]{:S(2)}) collective-permute-start(bf16[2,96,256]{2,1,0:T(8,128)(2,1)S(1)} %pad_maximum_fusion.2), channel_id=1, source_target_pairs={{0,2},{1,3},{2,0},{3,1},{4,6},{5,7},{6,4},{7,5},{8,10},{9,11},{10,... | collective-permute-start | bytes 294920 | tf_op jit(solution)/shard_map/ppermute | solution.py:503
  82.5 2.6 %collective-permute-done.18 = bf16[2,96,256]{2,1,0:T(8,128)(2,1)S(1)} collective-permute-done((bf16[2,96,256]{2,1,0:T(8,128)(2,1)S(1)}, bf16[2,96,256]{2,1,0:T(8,128)(2,1)S(1)}, u32[]{:S(2)}, u32[]{:S(2)}) %collective-permute-start.18) | collective-permute-done | bytes 98336 | tf_op jit(solution)/shard_map/ppermute | solution.py:503
  85.1 1.6 %collective-permute-start.19 = (bf16[4,96,256]{2,1,0:T(8,128)(2,1)S(1)}, bf16[4,96,256]{2,1,0:T(8,128)(2,1)S(1)}, u32[]{:S(2)}, u32[]{:S(2)}) collective-permute-start(bf16[4,96,256]{2,1,0:T(8,128)(2,1)S(1)} %pad_maximum_fusion.1), channel_id=1, source_target_pairs={{0,1},{1,0},{2,3},{3,2},{4,5},{5,4},{6,7},{7,6},{8,9},{9,8},{10,11... | collective-permute-start | bytes 589832 | tf_op jit(solution)/shard_map/ppermute | solution.py:503
  86.7 4.1 %collective-permute-done.19 = bf16[4,96,256]{2,1,0:T(8,128)(2,1)S(1)} collective-permute-done((bf16[4,96,256]{2,1,0:T(8,128)(2,1)S(1)}, bf16[4,96,256]{2,1,0:T(8,128)(2,1)S(1)}, u32[]{:S(2)}, u32[]{:S(2)}) %collective-permute-start.19) | collective-permute-done | bytes 196640 | tf_op jit(solution)/shard_map/ppermute | solution.py:503
  90.9 0.8 place.1
  91.7 1.5 %collective-permute-done.20 = f32[264,256]{1,0:T(8,128)S(1)} collective-permute-done((f32[264,256]{1,0:T(8,128)S(1)}, f32[264,256]{1,0:T(8,128)S(1)}, u32[]{:S(2)}, u32[]{:S(2)}) %collective-permute-start.20) | collective-permute-done | bytes 270368 | tf_op jit(solution)/shard_map/ppermute | solution.py:503
  93.3 0.6 fusion
  93.9 0.7 slice.21
  94.6 0.7 slice_select_fusion
  (25 shorter events, 0.2 us)
Async XLA Ops:
  0.6 11.1 %collective-permute-start = (bf16[4096,256]{1,0:T(8,128)(2,1)}, bf16[4096,256]{1,0:T(8,128)(2,1)S(1)}, u32[]{:S(2)}, u32[]{:S(2)}) collective-permute-start(bf16[4096,256]{1,0:T(8,128)(2,1)} %own_ref.7), channel_id=1, source_target_pairs={{0,8},{8,0},{16,24},{24,16},{1,9},{9,1},{17,25},{25,17},{2,10},{10... | collective-permute-start | bytes 6291464 | tf_op jit(solution)/shard_map/ppermute | solution.py:503
  1.1 10.5 %collective-permute-start.1 = (bf16[256,256]{1,0:T(8,128)(2,1)}, bf16[256,256]{1,0:T(8,128)(2,1)S(1)}, u32[]{:S(2)}, u32[]{:S(2)}) collective-permute-start(bf16[256,256]{1,0:T(8,128)(2,1)} %self_own_ref.7), channel_id=1, source_target_pairs={{0,8},{8,0},{16,24},{24,16},{1,9},{9,1},{17,25},{25,17},{2,10},{10... | collective-permute-start | bytes 393224 | tf_op jit(solution)/shard_map/ppermute | solution.py:503
  1.2 10.5 %collective-permute-start.2 = (bf16[256,256]{1,0:T(8,128)(2,1)}, bf16[256,256]{1,0:T(8,128)(2,1)S(1)}, u32[]{:S(2)}, u32[]{:S(2)}) collective-permute-start(bf16[256,256]{1,0:T(8,128)(2,1)} %neigh_own_ref.7), channel_id=1, source_target_pairs={{0,8},{8,0},{16,24},{24,16},{1,9},{9,1},{17,25},{25,17},{2,10},{10... | collective-permute-start | bytes 393224 | tf_op jit(solution)/shard_map/ppermute | solution.py:503
  2.5 0.9 copy-start.3
  3.4 8.3 %copy-start = (bf16[4096,256]{1,0:T(8,128)(2,1)S(1)}, bf16[4096,256]{1,0:T(8,128)(2,1)}, u32[]{:S(2)}) copy-start(bf16[4096,256]{1,0:T(8,128)(2,1)} %own_ref.7) | copy-start | bytes 6291460
  3.4 8.4 %copy-start.1 = (bf16[256,256]{1,0:T(8,128)(2,1)S(1)}, bf16[256,256]{1,0:T(8,128)(2,1)}, u32[]{:S(2)}) copy-start(bf16[256,256]{1,0:T(8,128)(2,1)} %self_own_ref.7) | copy-start | bytes 393220
  3.4 8.4 %copy-start.2 = (bf16[256,256]{1,0:T(8,128)(2,1)S(1)}, bf16[256,256]{1,0:T(8,128)(2,1)}, u32[]{:S(2)}) copy-start(bf16[256,256]{1,0:T(8,128)(2,1)} %neigh_own_ref.7) | copy-start | bytes 393220
  15.5 20.4 %collective-permute-start.6 = (bf16[384,256]{1,0:T(8,128)(2,1)S(1)}, bf16[384,256]{1,0:T(8,128)(2,1)S(1)}, u32[]{:S(2)}, u32[]{:S(2)}) collective-permute-start(bf16[384,256]{1,0:T(8,128)(2,1)S(1)} %get-tuple-element.43.refs_6_), channel_id=1, source_target_pairs={{0,16},{8,24},{16,0},{24,8},{1,17},{9,25},{17,1},{25,9},{2,18},{10... | collective-permute-start | bytes 589832 | tf_op jit(solution)/shard_map/ppermute | solution.py:503
  21.8 14.1 %collective-permute-start.5 = (bf16[384,256]{1,0:T(8,128)(2,1)S(1)}, bf16[384,256]{1,0:T(8,128)(2,1)S(1)}, u32[]{:S(2)}, u32[]{:S(2)}) collective-permute-start(bf16[384,256]{1,0:T(8,128)(2,1)S(1)} %get-tuple-element.42.refs_4_), channel_id=1, source_target_pairs={{0,16},{8,24},{16,0},{24,8},{1,17},{9,25},{17,1},{25,9},{2,18},{10... | collective-permute-start | bytes 589832 | tf_op jit(solution)/shard_map/ppermute | solution.py:503
  25.6 10.9 %copy-start.6 = (bf16[64,256]{1,0:T(8,128)(2,1)S(1)}, bf16[64,256]{1,0:T(8,128)(2,1)}, u32[]{:S(2)}) copy-start(bf16[64,256]{1,0:T(8,128)(2,1)} %refs_12_.1) | copy-start | bytes 98308
  25.6 24.3 %copy-start.4 = (bf16[256,256]{1,0:T(8,128)(2,1)S(1)}, bf16[256,256]{1,0:T(8,128)(2,1)}, u32[]{:S(2)}) copy-start(bf16[256,256]{1,0:T(8,128)(2,1)} %refs_17_.1) | copy-start | bytes 393220
  25.6 24.3 %copy-start.5 = (bf16[256,256]{1,0:T(8,128)(2,1)S(1)}, bf16[256,256]{1,0:T(8,128)(2,1)}, u32[]{:S(2)}) copy-start(bf16[256,256]{1,0:T(8,128)(2,1)} %refs_18_.1) | copy-start | bytes 393220
  25.6 24.3 %copy-start.7 = (f32[256]{0:T(256)S(1)}, f32[256]{0:T(256)}, u32[]{:S(2)}) copy-start(f32[256]{0:T(256)} %param.17) | copy-start | bytes 3076
  25.6 24.3 %copy-start.8 = (f32[256]{0:T(256)S(1)}, f32[256]{0:T(256)}, u32[]{:S(2)}) copy-start(f32[256]{0:T(256)} %param.18) | copy-start | bytes 3076
  25.6 10.2 %collective-permute-start.4 = (bf16[384,256]{1,0:T(8,128)(2,1)S(1)}, bf16[384,256]{1,0:T(8,128)(2,1)S(1)}, u32[]{:S(2)}, u32[]{:S(2)}) collective-permute-start(bf16[384,256]{1,0:T(8,128)(2,1)S(1)} %get-tuple-element.41.refs_2_), channel_id=1, source_target_pairs={{0,16},{8,24},{16,0},{24,8},{1,17},{9,25},{17,1},{25,9},{2,18},{10... | collective-permute-start | bytes 589832 | tf_op jit(solution)/shard_map/ppermute | solution.py:503
  30.5 5.4 %collective-permute-start.3 = (bf16[256,256]{1,0:T(8,128)(2,1)S(1)}, bf16[256,256]{1,0:T(8,128)(2,1)S(1)}, u32[]{:S(2)}, u32[]{:S(2)}) collective-permute-start(bf16[256,256]{1,0:T(8,128)(2,1)S(1)} %get-tuple-element.40.refs_0_), channel_id=1, source_target_pairs={{0,16},{8,24},{16,0},{24,8},{1,17},{9,25},{17,1},{25,9},{2,18},{10... | collective-permute-start | bytes 393224 | tf_op jit(solution)/shard_map/ppermute | solution.py:503
  36.4 1.5 %collective-permute-start.8 = (f32[8,256]{1,0:T(8,128)S(1)}, f32[8,256]{1,0:T(8,128)S(1)}, u32[]{:S(2)}, u32[]{:S(2)}) collective-permute-start(f32[8,256]{1,0:T(8,128)S(1)} %get-tuple-element.53), channel_id=1, source_target_pairs={{0,8},{8,0},{16,24},{24,16},{1,9},{9,1},{17,25},{25,17},{2,10},{10... | collective-permute-start | bytes 24584 | tf_op jit(solution)/shard_map/ppermute | solution.py:503
  36.5 13.4 %collective-permute-start.7 = (bf16[64,256]{1,0:T(8,128)(2,1)S(1)}, bf16[64,256]{1,0:T(8,128)(2,1)S(1)}, u32[]{:S(2)}, u32[]{:S(2)}) collective-permute-start(bf16[64,256]{1,0:T(8,128)(2,1)S(1)} %copy-done.6), channel_id=1, source_target_pairs={{0,16},{8,24},{16,0},{24,8},{1,17},{9,25},{17,1},{25,9},{2,18},{10... | collective-permute-start | bytes 98312 | tf_op jit(solution)/shard_map/ppermute | solution.py:503
  37.9 3.7 %collective-permute-start.9 = (f32[8,256]{1,0:T(8,128)S(1)}, f32[8,256]{1,0:T(8,128)S(1)}, u32[]{:S(2)}, u32[]{:S(2)}) collective-permute-start(f32[8,256]{1,0:T(8,128)S(1)} %join.4.mine_ref), channel_id=1, source_target_pairs={{0,1},{1,0},{2,3},{3,2},{4,5},{5,4},{6,7},{7,6},{8,9},{9,8},{10,11... | collective-permute-start | bytes 24584 | tf_op jit(solution)/shard_map/ppermute | solution.py:503
  41.6 3.7 %collective-permute-start.10 = (f32[8,256]{1,0:T(8,128)S(1)}, f32[8,256]{1,0:T(8,128)S(1)}, u32[]{:S(2)}, u32[]{:S(2)}) collective-permute-start(f32[8,256]{1,0:T(8,128)S(1)} %join.5.mine_ref), channel_id=1, source_target_pairs={{0,2},{1,3},{2,0},{3,1},{4,6},{5,7},{6,4},{7,5},{8,10},{9,11},{10,... | collective-permute-start | bytes 24584 | tf_op jit(solution)/shard_map/ppermute | solution.py:503
  45.3 4.5 %collective-permute-start.11 = (f32[8,256]{1,0:T(8,128)S(1)}, f32[8,256]{1,0:T(8,128)S(1)}, u32[]{:S(2)}, u32[]{:S(2)}) collective-permute-start(f32[8,256]{1,0:T(8,128)S(1)} %join.6.mine_ref), channel_id=1, source_target_pairs={{0,4},{1,5},{2,6},{3,7},{4,0},{5,1},{6,2},{7,3},{8,12},{9,13},{10,... | collective-permute-start | bytes 24584 | tf_op jit(solution)/shard_map/ppermute | solution.py:503
  53.7 2.2 %collective-permute-start.12 = (bf16[8,160,256]{2,1,0:T(8,128)(2,1)S(1)}, bf16[8,160,256]{2,1,0:T(8,128)(2,1)S(1)}, u32[]{:S(2)}, u32[]{:S(2)}) collective-permute-start(bf16[8,160,256]{2,1,0:T(8,128)(2,1)S(1)} %get-tuple-element.56), channel_id=1, source_target_pairs={{0,8},{8,0},{16,24},{24,16},{1,9},{9,1},{17,25},{25,17},{2,10},{10... | collective-permute-start | bytes 1966088 | tf_op jit(solution)/shard_map/ppermute | solution.py:503
  53.8 2.1 %collective-permute-start.13 = (bf16[16,256]{1,0:T(8,128)(2,1)S(1)}, bf16[16,256]{1,0:T(8,128)(2,1)S(1)}, u32[]{:S(2)}, u32[]{:S(2)}) collective-permute-start(bf16[16,256]{1,0:T(8,128)(2,1)S(1)} %get-tuple-element.57.sums_ref), channel_id=1, source_target_pairs={{0,8},{8,0},{16,24},{24,16},{1,9},{9,1},{17,25},{25,17},{2,10},{10... | collective-permute-start | bytes 24584 | tf_op jit(solution)/shard_map/ppermute | solution.py:503
  56.5 7.2 %collective-permute-start.14 = (bf16[656,256]{1,0:T(8,128)(2,1)S(1)}, bf16[656,256]{1,0:T(8,128)(2,1)S(1)}, u32[]{:S(2)}, u32[]{:S(2)}) collective-permute-start(bf16[656,256]{1,0:T(8,128)(2,1)S(1)} %get-tuple-element.59), channel_id=1, source_target_pairs={{0,1},{1,0},{2,3},{3,2},{4,5},{5,4},{6,7},{7,6},{8,10},{9,11},{10,... | collective-permute-start | bytes 1007624 | tf_op jit(solution)/shard_map/ppermute | solution.py:636
  63.9 5.5 %collective-permute-start.15 = (bf16[336,256]{1,0:T(8,128)(2,1)S(1)}, bf16[336,256]{1,0:T(8,128)(2,1)S(1)}, u32[]{:S(2)}, u32[]{:S(2)}) collective-permute-start(bf16[336,256]{1,0:T(8,128)(2,1)S(1)} %get-tuple-element.62), channel_id=1, source_target_pairs={{0,2},{1,3},{2,0},{3,1},{4,6},{5,7},{6,4},{7,5},{8,9},{9,8},{10,11... | collective-permute-start | bytes 516104 | tf_op jit(solution)/shard_map/ppermute | solution.py:636
  69.4 5.5 %collective-permute-start.16 = (bf16[176,256]{1,0:T(8,128)(2,1)S(1)}, bf16[176,256]{1,0:T(8,128)(2,1)S(1)}, u32[]{:S(2)}, u32[]{:S(2)}) collective-permute-start(bf16[176,256]{1,0:T(8,128)(2,1)S(1)} %get-tuple-element.65), channel_id=1, source_target_pairs={{0,4},{1,5},{2,6},{3,7},{4,0},{5,1},{6,2},{7,3},{8,12},{9,13},{10,... | collective-permute-start | bytes 270344 | tf_op jit(solution)/shard_map/ppermute | solution.py:636
  75.1 5.2 %collective-permute-start.17 = (bf16[1,96,256]{2,1,0:T(8,128)(2,1)S(1)}, bf16[1,96,256]{2,1,0:T(8,128)(2,1)S(1)}, u32[]{:S(2)}, u32[]{:S(2)}) collective-permute-start(bf16[1,96,256]{2,1,0:T(8,128)(2,1)S(1)} %bitcast.11), channel_id=1, source_target_pairs={{0,4},{1,5},{2,6},{3,7},{4,0},{5,1},{6,2},{7,3},{8,12},{9,13},{10,... | collective-permute-start | bytes 147464 | tf_op jit(solution)/shard_map/ppermute | solution.py:503
  80.3 4.7 %collective-permute-start.18 = (bf16[2,96,256]{2,1,0:T(8,128)(2,1)S(1)}, bf16[2,96,256]{2,1,0:T(8,128)(2,1)S(1)}, u32[]{:S(2)}, u32[]{:S(2)}) collective-permute-start(bf16[2,96,256]{2,1,0:T(8,128)(2,1)S(1)} %pad_maximum_fusion.2), channel_id=1, source_target_pairs={{0,2},{1,3},{2,0},{3,1},{4,6},{5,7},{6,4},{7,5},{8,10},{9,11},{10,... | collective-permute-start | bytes 294920 | tf_op jit(solution)/shard_map/ppermute | solution.py:503
  85.1 5.7 %collective-permute-start.19 = (bf16[4,96,256]{2,1,0:T(8,128)(2,1)S(1)}, bf16[4,96,256]{2,1,0:T(8,128)(2,1)S(1)}, u32[]{:S(2)}, u32[]{:S(2)}) collective-permute-start(bf16[4,96,256]{2,1,0:T(8,128)(2,1)S(1)} %pad_maximum_fusion.1), channel_id=1, source_target_pairs={{0,1},{1,0},{2,3},{3,2},{4,5},{5,4},{6,7},{7,6},{8,9},{9,8},{10,11... | collective-permute-start | bytes 589832 | tf_op jit(solution)/shard_map/ppermute | solution.py:503
  91.7 1.5 %collective-permute-start.20 = (f32[264,256]{1,0:T(8,128)S(1)}, f32[264,256]{1,0:T(8,128)S(1)}, u32[]{:S(2)}, u32[]{:S(2)}) collective-permute-start(f32[264,256]{1,0:T(8,128)S(1)} %get-tuple-element.72), channel_id=1, source_target_pairs={{0,8},{8,0},{16,24},{24,16},{1,9},{9,1},{17,25},{25,17},{2,10},{10... | collective-permute-start | bytes 811016 | tf_op jit(solution)/shard_map/ppermute | solution.py:503

commit v5 on v4

--- a/solution.py
+++ b/solution.py
@@ -386,9 +386,12 @@
     gain_high, gain_low = halves(jnp.sum(gain_sum, axis=0, keepdims=True))
     shift_high, shift_low = halves(jnp.sum(shift_sum, axis=0, keepdims=True))
     sums = [gain_high, gain_low, shift_high, shift_low]
-    sums_ref[...] = jnp.concatenate(
+    sums = jnp.concatenate(
         [s.astype(F32) for s in sums] + [jnp.zeros((12, hidden_width), F32)], axis=0
     ).astype(BF)
+    sums_ref[...] = sums
+    per_group = keep_ref.shape[1]
+    send_ref[batches * per_group :, :] = sums
     lower = None
     first = 0
     for a in acrosses:
@@ -396,7 +399,7 @@
         lower = part if lower is None else lower + part
         first += a.shape[1]
     piece, upper_piece = width // batches, hidden_width // batches
-    for block, upper, ref in ((0, upper_keep, keep_ref), (2, upper_send, send_ref)):
+    for block, upper in ((0, upper_keep), (2, upper_send)):
         for d in range(batches):
             parts = []
             for lane in (0, hidden_width):
@@ -404,7 +407,11 @@
                     row = (block + j) * width + d * piece
                     parts.append(lower[row : row + piece, lane : lane + hidden_width])
             parts.append(upper[d * upper_piece : (d + 1) * upper_piece, :])
-            ref[d, :, :] = jnp.concatenate(parts, axis=0).astype(ref.dtype)
+            value = jnp.concatenate(parts, axis=0)
+            if block == 0:
+                keep_ref[d, :, :] = value
+            else:
+                send_ref[d * per_group : (d + 1) * per_group, :] = value.astype(BF)
 
 
 def joined_sums(mine, theirs):
@@ -416,14 +423,16 @@
 
 
 def merge_kernel(
-    orders, place_ref, keep_ref, got_ref, sums_ref, got_sums_ref, kept_ref, sent_ref, tail_ref
+    orders, place_ref, keep_ref, got_ref, sums_ref, kept_ref, sent_ref, tail_ref
 ):
     batches, rows, _ = keep_ref.shape
-    tail = joined_sums(sums_ref[...].astype(F32), got_sums_ref[...].astype(F32)).astype(BF)
+    got_sums = got_ref[batches * rows :, :].astype(F32)
+    tail = joined_sums(sums_ref[...].astype(F32), got_sums).astype(BF)
     half = batches // 2
     for i in range(batches):
         d = place_ref[2] ^ jnp.where(place_ref[1] == 0, orders[0][i], orders[1][i])
-        value = keep_ref[d, :, :] + got_ref[d, :, :].astype(F32)
+        at = pl.multiple_of(d * rows, rows)
+        value = keep_ref[d, :, :] + got_ref[pl.ds(at, rows), :].astype(F32)
         if i < half:
             kept_ref[i, :, :] = value
         else:
@@ -447,56 +456,64 @@
     new_tail_ref[...] = tail
 
 
+def both_kernel(keep_ref, got_ref, tail_ref, sent_ref, new_tail_ref):
+    pieces, rows, _ = keep_ref.shape
+    got_tail = got_ref[pieces * rows :, :].astype(F32)
+    tail = joined_sums(tail_ref[...].astype(F32), got_tail).astype(BF)
+    for i in range(pieces):
+        value = keep_ref[i, :, :] + got_ref[i * rows : (i + 1) * rows, :].astype(F32)
+        sent_ref[i * rows : (i + 1) * rows, :] = value.astype(BF)
+    sent_ref[pieces * rows :, :] = tail
+    new_tail_ref[...] = tail
+
+
 def finish_kernel(
-    row_total,
-    keep_ref,
-    got_ref,
-    tail_ref,
-    stats_ref,
-    gain_ref,
-    column_ref,
-    out_ref,
-    gain_out,
-    shift_out,
+    row_total, sent_ref, got_ref, tail_ref, stats_ref, gain_ref, column_ref, out_ref, sums_ref
 ):
-    rows = keep_ref.shape[1]
-    total = keep_ref[0, :, :] + got_ref[:rows, :].astype(F32)
-    sums = joined_sums(tail_ref[...].astype(F32), got_ref[rows:, :].astype(F32))
-    pieces = column_ref.shape[1]
+    rows = (sent_ref.shape[0] - 16) // 2
+    sums = joined_sums(tail_ref[...].astype(F32), got_ref[2 * rows :, :].astype(F32))
+    pieces = column_ref.shape[2]
     grad_gain = sums[0:1] + sums[1:2]
     grad_shift = sums[2:3] + sums[3:4]
-    inv_std = lax.rsqrt(stats_ref[1:2, :] / row_total + 1e-05)
-    outer = dot(
-        column_ref[...],
-        jnp.broadcast_to(grad_shift / row_total, (8, grad_shift.shape[1])),
-        ((0,), (0,)),
-        lax.Precision.HIGHEST,
-    )
-    lower = (gain_ref[...] * inv_std) * (
-        total[:pieces] - outer - total[pieces : 2 * pieces] * (grad_gain / row_total)
-    )
-    out_ref[...] = jnp.concatenate([lower, total[2 * pieces : rows]], axis=0).astype(BF)
-    gain_out[...] = grad_gain
-    shift_out[...] = grad_shift
-
-
-def place_kernel(
-    masks, group_ref, parts_ref, gain_ref, shift_ref, self_ref, neigh_ref, upper_ref
-):
+    scale = gain_ref[...] * lax.rsqrt(stats_ref[1:2, :] / row_total + 1e-05)
+    shift_part = jnp.broadcast_to(grad_shift / row_total, (8, grad_shift.shape[1]))
+    for i in range(2):
+        mine = sent_ref[i * rows : (i + 1) * rows, :].astype(F32)
+        total = mine + got_ref[(1 - i) * rows : (2 - i) * rows, :].astype(F32)
+        outer = dot(column_ref[i, :, :], shift_part, ((0,), (0,)), lax.Precision.HIGHEST)
+        lower = scale * (
+            total[:pieces] - outer - total[pieces : 2 * pieces] * (grad_gain / row_total)
+        )
+        out_ref[i, :, :] = jnp.concatenate([lower, total[2 * pieces : rows]], axis=0).astype(BF)
+    sums_ref[...] = sums.astype(BF)
+
+
+def upper_kernel(masks, place_ref, parts_ref, sums_ref, upper_ref):
+    rows = upper_ref.shape[0] - 16
+    piece = rows // len(masks)
+    for i, mask in enumerate(masks):
+        at = pl.multiple_of((place_ref[2] ^ mask) * piece, piece)
+        upper_ref[pl.ds(at, piece), :] = parts_ref[i, parts_ref.shape[1] - piece :, :].astype(F32)
+    upper_ref[rows:, :] = sums_ref[...].astype(F32)
+
+
+def lower_kernel(masks, place_ref, parts_ref, self_ref, neigh_ref):
     piece = self_ref.shape[0] // len(masks)
-    upper_piece = (upper_ref.shape[0] - 8) // len(masks)
-    hidden_width = upper_ref.shape[1]
-    upper_ref[upper_ref.shape[0] - 8 :, :] = jnp.concatenate(
-        [gain_ref[...], shift_ref[...], jnp.zeros((6, hidden_width), F32)], axis=0
-    )
     for i, mask in enumerate(masks):
-        d = group_ref[0] ^ mask
+        at = pl.ds(pl.multiple_of((place_ref[2] ^ mask) * piece, piece), piece)
         rows = parts_ref[i, :, :].astype(F32)
-        self_ref[pl.ds(pl.multiple_of(d * piece, piece), piece), :] = rows[:piece]
-        neigh_ref[pl.ds(pl.multiple_of(d * piece, piece), piece), :] = rows[piece : 2 * piece]
-        upper_ref[pl.ds(pl.multiple_of(d * upper_piece, upper_piece), upper_piece), :] = rows[
-            2 * piece :
-        ]
+        self_ref[at, :] = rows[:piece]
+        neigh_ref[at, :] = rows[piece : 2 * piece]
+
+
+def last_kernel(place_ref, mine_ref, other_ref, self_ref, neigh_ref, gain_ref, shift_ref):
+    rows = self_ref.shape[0]
+    first_core = place_ref[1] == 0
+    first = jnp.where(first_core, mine_ref[...], other_ref[...])
+    self_ref[...] = first[:rows]
+    neigh_ref[...] = jnp.where(first_core, other_ref[:rows, :], mine_ref[:rows, :])
+    gain_ref[...] = first[rows : rows + 1] + first[rows + 1 : rows + 2]
+    shift_ref[...] = first[rows + 2 : rows + 3] + first[rows + 3 : rows + 4]
 
 
 def swap(value, axis, mask):
@@ -599,7 +616,7 @@
         out_shape=[
             jax.ShapeDtypeStruct((own_seeds, hidden_width), BF),
             jax.ShapeDtypeStruct((batches, per_group, hidden_width), F32),
-            jax.ShapeDtypeStruct((batches, per_group, hidden_width), BF),
+            jax.ShapeDtypeStruct((batches * per_group + 16, hidden_width), BF),
             jax.ShapeDtypeStruct((16, hidden_width), BF),
         ],
         scratch_shapes=[
@@ -638,13 +655,13 @@
     pieces = batches // 2
     kept, sent, tail = pl.pallas_call(
         functools.partial(merge_kernel, [order_of(masks) for masks in rounds]),
-        in_specs=[SMEM] + [VMEM] * 4,
+        in_specs=[SMEM] + [VMEM] * 3,
         out_shape=kept_and_sent(pieces),
         compiler_params=params(16),
         name="merge",
-    )(place, keep, swap(send, "feat", 1), sums, swap(sums, "feat", 1))
+    )(place, keep, swap(send, "feat", 1), sums)
     got = exchange(sent, 0)
-    for step in range(1, len(bits)):
+    for step in range(1, len(bits) - 1):
         pieces //= 2
         kept, sent, tail = pl.pallas_call(
             halve_kernel,
@@ -653,47 +670,73 @@
             name="halve",
         )(kept, got, tail)
         got = exchange(sent, step)
+    sent, tail = pl.pallas_call(
+        both_kernel,
+        out_shape=kept_and_sent(pieces)[1:],
+        compiler_params=params(16),
+        name="both",
+    )(kept, got, tail)
+    got = exchange(sent, len(bits) - 1)
 
     piece = width // batches
-    column = lax.dynamic_slice(stats[2:4], (0, batch * piece), (2, piece)).reshape(1, 2 * piece)
-    column = jnp.pad(column, ((0, 7), (0, 0)))
+    columns = []
+    for mask in (0, batches // 2):
+        at = (0, (batch ^ mask) * piece)
+        columns.append(lax.dynamic_slice(stats[2:4], at, (2, piece)).reshape(1, 1, 2 * piece))
+    column = jnp.pad(jnp.concatenate(columns, axis=0), ((0, 0), (0, 7), (0, 0)))
     out_rows = 2 * piece + hidden_width // batches
-    line = jax.ShapeDtypeStruct((1, hidden_width), F32)
-    done, grad_gain, grad_shift = pl.pallas_call(
+    done, sums = pl.pallas_call(
         functools.partial(finish_kernel, row_total),
-        out_shape=[jax.ShapeDtypeStruct((out_rows, hidden_width), BF), line, line],
+        out_shape=[
+            jax.ShapeDtypeStruct((2, out_rows, hidden_width), BF),
+            jax.ShapeDtypeStruct((16, hidden_width), BF),
+        ],
         compiler_params=params(16),
         name="finish",
-    )(kept, got, tail, stats, gain_row, column)
-
-    gathered, masks = done[None], [0]
-    mask = batches // 2
+    )(sent, got, tail, stats, gain_row, column)
+
+    gathered, masks = done, [0, batches // 2]
+    mask = batches // 4
     while mask:
         gathered = jnp.concatenate([gathered, swap(gathered, "batch", mask)], axis=0)
         masks += [m ^ mask for m in masks]
         mask //= 2
-    grad_self, grad_neigh, upper = pl.pallas_call(
-        functools.partial(place_kernel, tuple(masks)),
-        in_specs=[SMEM] + [VMEM] * 3,
-        out_shape=[
-            jax.ShapeDtypeStruct((width, hidden_width), F32),
-            jax.ShapeDtypeStruct((width, hidden_width), F32),
-            jax.ShapeDtypeStruct((hidden_width + 8, hidden_width), F32),
-        ],
-        compiler_params=params(16),
-        name="place",
-    )(batch.astype(jnp.int32)[None], gathered, grad_gain, grad_shift)
+    square = jax.ShapeDtypeStruct((hidden_width, hidden_width), F32)
+    tall = jax.ShapeDtypeStruct((width, hidden_width), F32)
+    line = jax.ShapeDtypeStruct((1, hidden_width), F32)
+    upper = pl.pallas_call(
+        functools.partial(upper_kernel, tuple(masks)),
+        in_specs=[SMEM, VMEM, VMEM],
+        out_shape=jax.ShapeDtypeStruct((hidden_width + 16, hidden_width), F32),
+        compiler_params=params(4),
+        name="upper",
+    )(place, gathered, sums)
     upper_other = swap(upper, "feat", 1)
-    first = jnp.where(core == 0, upper, upper_other)
-    second = jnp.where(core == 0, upper_other, upper)
+    grad_self, grad_neigh = pl.pallas_call(
+        functools.partial(lower_kernel, tuple(masks)),
+        in_specs=[SMEM, VMEM],
+        out_shape=[tall, tall],
+        compiler_params=params(4),
+        cost_estimate=pl.CostEstimate(
+            flops=0, bytes_accessed=12 * width * hidden_width, transcendentals=0
+        ),
+        name="lower",
+    )(place, gathered)
+    grad_upper_self, grad_upper_neigh, grad_gain, grad_shift = pl.pallas_call(
+        last_kernel,
+        in_specs=[SMEM, VMEM, VMEM],
+        out_shape=[square, square, line, line],
+        compiler_params=params(4),
+        name="last",
+    )(place, upper, upper_other)
     return (
         embedding,
         grad_self,
         grad_neigh,
-        first[:hidden_width],
-        second[:hidden_width],
-        first[hidden_width],
-        first[hidden_width + 1],
+        grad_upper_self,
+        grad_upper_neigh,
+        grad_gain[0],
+        grad_shift[0],
     )
 
 

time: 95.6 us -> 93.3 us (0.976)
  starting transfers between devices: 26.1 us -> 21.6 us
  Pallas kernels: 28.4 us -> 30.9 us
  waiting for transfers between devices: 35.9 us -> 37.7 us
  local copies, waits for them, and re-layouts: 2.41 us -> 1.23 us
    ppermute x18 -> x16, starting transfers between devices: 20.2 us -> 15.7 us  [swap(): lax.ppermute(value, axis, [(i, i ^ mask) for i in range(lax.axis_size(axi...]
    ppermute x3, waiting for transfers between devices: 12.1 us -> 15.9 us  [exchange(): return lax.ppermute(value, ('feat', 'batch'), pairs)]
    pallas_call x1 -> x4, Pallas kernels: 0.84 us -> 3.35 us  [the longest x1 1.37 us: on_device(): pl.pallas_call(last_kernel, in_specs=[SMEM, VMEM, VMEM], out_shape=[squar...]
    ppermute x18 -> x16, waiting for transfers between devices: 23.7 us -> 21.8 us  [swap(): lax.ppermute(value, axis, [(i, i ^ mask) for i in range(lax.axis_size(axi...]
    slice x2 -> x0, local copies, waits for them, and re-layouts: 1.29 us -> none  [the longest x1 0.72 us: on_device(): first[:hidden_width]]
  transfers between devices with their start and end apart: 21 -> 19, of which waited for: 12 -> 11; matrix products, arithmetic and copies ran while one was open for 1% -> 1% of each run, Pallas kernels for 19% -> 21%
where the time goes in v5:
time: 93.3 us; the launch traced here: 93 us
  waiting for transfers between devices  37.7 us (40%)
  Pallas kernels  30.9 us (33%)
  starting transfers between devices  21.6 us (23%)
  local copies, waits for them, and re-layouts  1.23 us (1%)
    ppermute x16, waiting for transfers between devices, swap(): lax.ppermute(value, axis, [(i, i ^ mask) for i in range(lax.axis_size(axi...  21.8 us
    ppermute x3, waiting for transfers between devices, exchange(): return lax.ppermute(value, ('feat', 'batch'), pairs)  15.9 us
    ppermute x16, starting transfers between devices, swap(): lax.ppermute(value, axis, [(i, i ^ mask) for i in range(lax.axis_size(axi...  15.7 us
    pallas_call x4, Pallas kernels, pick_rows(): pl.pallas_call(functools.partial(pick_kernel, first_block, start, blocks,...  13.8 us
    pallas_call x1, Pallas kernels, build_rows(): pl.pallas_call(build_kernel, grid=(steps,), in_specs=[SMEM, VMEM, VMEM],...  8.3 us
    ppermute x3, starting transfers between devices, exchange(): return lax.ppermute(value, ('feat', 'batch'), pairs)  5.91 us
    pallas_call x1, Pallas kernels, on_device(): pl.pallas_call(functools.partial(middle_kernel, len(CHUNKS), slots, row_t...  3.78 us
  transfers between devices with their start and end apart: 19, of which 11 were waited for; matrix products, arithmetic and copies ran while one was open for 1% of the time, Pallas kernels for 21%

profile of v5, /device:TPU:0, one launch (start us, length us, event | category | flops | bytes accessed | tf_op | source)
XLA Modules:
  0.0 93.0 jit_solution(8795738929531645041)
XLA Ops:
  0.6 0.5 collective-permute-start
  1.1 0.1 collective-permute-start.1
  1.2 0.4 collective-permute-start.2
  1.7 0.1 pad_add_fusion.1.place_ref
  1.7 0.7 pad_add_fusion.own_ref
  2.5 0.9 copy-done.3
  3.4 8.3 %build_rows.1.rows_ref = bf16[2816,4096]{1,0:T(8,128)(2,1)S(1)} custom-call(s32[3]{0:T(128)S(1)} %pad_add_fusion.1.place_ref, s32[11,256]{1,0:T(8,128)S(1)} %pad_add_fusion.own_ref, s32[10,15,256]{2,1,0:T(8,128)S(1)} %bitcast.10), custom_call_target="tpu_custom_call" | custom-call | flops 2952790016 | bytes 23068672 | tf_op jit(solution)/shard_map/build_rows/pallas_call | solution.py:156
  11.7 0.0 collective-permute-done.1.self_peer_ref
  11.7 0.0 collective-permute-done.2.neigh_peer_ref
  11.7 0.0 collective-permute-done.peer_ref
  11.8 3.7 %pick_rows.7 = (bf16[1024,384]{1,0:T(8,128)(2,1)S(1)}, bf16[384,256]{1,0:T(8,128)(2,1)S(1)}, f32[8,1024]{1,0:T(8,128)S(1)}) custom-call(bf16[2816,4096]{1,0:T(8,128)(2,1)S(1)} %build_rows.1.rows_ref, bf16[4096,256]{1,0:T(8,128)(2,1)S(1)} %copy-done, bf16[4096,256]{1,0:T(8,128)(2,1)S(1)} %collective-permute-done.peer_ref, bf16[256,256]{1,0:T(8,128)(2,1)S(1)} %copy-done.1, ...), custom_call_target="tpu_custom_call" | custom-call | flops 3221225472 | bytes 7340032 | tf_op jit(solution)/shard_map/pick_rows/pallas_call | solution.py:245
  15.5 2.6 %collective-permute-start.6 = (bf16[384,256]{1,0:T(8,128)(2,1)S(1)}, bf16[384,256]{1,0:T(8,128)(2,1)S(1)}, u32[]{:S(2)}, u32[]{:S(2)}) collective-permute-start(bf16[384,256]{1,0:T(8,128)(2,1)S(1)} %get-tuple-element.44.refs_6_), channel_id=1, source_target_pairs={{0,16},{8,24},{16,0},{24,8},{1,17},{9,25},{17,1},{25,9},{2,18},{10... | collective-permute-start | bytes 589832 | tf_op jit(solution)/shard_map/ppermute | solution.py:520
  18.1 3.7 %pick_rows.6 = (bf16[1024,384]{1,0:T(8,128)(2,1)S(1)}, bf16[384,256]{1,0:T(8,128)(2,1)S(1)}, f32[8,1024]{1,0:T(8,128)S(1)}) custom-call(bf16[2816,4096]{1,0:T(8,128)(2,1)S(1)} %build_rows.1.rows_ref, bf16[4096,256]{1,0:T(8,128)(2,1)S(1)} %copy-done, bf16[4096,256]{1,0:T(8,128)(2,1)S(1)} %collective-permute-done.peer_ref, bf16[256,256]{1,0:T(8,128)(2,1)S(1)} %copy-done.1, ...), custom_call_target="tpu_custom_call" | custom-call | flops 3221225472 | bytes 7340032 | tf_op jit(solution)/shard_map/pick_rows/pallas_call | solution.py:245
  21.8 0.1 collective-permute-start.5
  21.9 3.7 %pick_rows.5 = (bf16[1024,384]{1,0:T(8,128)(2,1)S(1)}, bf16[384,256]{1,0:T(8,128)(2,1)S(1)}, f32[8,1024]{1,0:T(8,128)S(1)}) custom-call(bf16[2816,4096]{1,0:T(8,128)(2,1)S(1)} %build_rows.1.rows_ref, bf16[4096,256]{1,0:T(8,128)(2,1)S(1)} %copy-done, bf16[4096,256]{1,0:T(8,128)(2,1)S(1)} %collective-permute-done.peer_ref, bf16[256,256]{1,0:T(8,128)(2,1)S(1)} %copy-done.1, ...), custom_call_target="tpu_custom_call" | custom-call | flops 3221225472 | bytes 7340032 | tf_op jit(solution)/shard_map/pick_rows/pallas_call | solution.py:245
  25.6 0.0 copy-start.6
  25.6 0.0 copy-start.4
  25.6 0.0 copy-start.5
  25.6 0.0 copy-start.7
  25.6 0.0 copy-start.8
  25.6 2.1 %collective-permute-start.4 = (bf16[384,256]{1,0:T(8,128)(2,1)S(1)}, bf16[384,256]{1,0:T(8,128)(2,1)S(1)}, u32[]{:S(2)}, u32[]{:S(2)}) collective-permute-start(bf16[384,256]{1,0:T(8,128)(2,1)S(1)} %get-tuple-element.42.refs_2_), channel_id=1, source_target_pairs={{0,16},{8,24},{16,0},{24,8},{1,17},{9,25},{17,1},{25,9},{2,18},{10... | collective-permute-start | bytes 589832 | tf_op jit(solution)/shard_map/ppermute | solution.py:520
  27.7 2.7 %pick_rows.4 = (bf16[1024,256]{1,0:T(8,128)(2,1)S(1)}, bf16[256,256]{1,0:T(8,128)(2,1)S(1)}, f32[8,1024]{1,0:T(8,128)S(1)}) custom-call(bf16[2816,4096]{1,0:T(8,128)(2,1)S(1)} %build_rows.1.rows_ref, bf16[4096,256]{1,0:T(8,128)(2,1)S(1)} %copy-done, bf16[4096,256]{1,0:T(8,128)(2,1)S(1)} %collective-permute-done.peer_ref, bf16[256,256]{1,0:T(8,128)(2,1)S(1)} %copy-done.1, ...), custom_call_target="tpu_custom_call" | custom-call | flops 2147483648 | bytes 6291456 | tf_op jit(solution)/shard_map/pick_rows/pallas_call | solution.py:245
  30.5 0.1 collective-permute-start.3
  30.6 5.3 %collective-permute-done.3.refs_1_ = bf16[256,256]{1,0:T(8,128)(2,1)S(1)} collective-permute-done((bf16[256,256]{1,0:T(8,128)(2,1)S(1)}, bf16[256,256]{1,0:T(8,128)(2,1)S(1)}, u32[]{:S(2)}, u32[]{:S(2)}) %collective-permute-start.3) | collective-permute-done | bytes 131104 | tf_op jit(solution)/shard_map/ppermute | solution.py:520
  35.8 0.0 collective-permute-done.6.refs_7_
  35.9 0.0 collective-permute-done.5.refs_5_
  35.9 0.0 collective-permute-done.4.refs_3_
  35.9 0.5 stats.1
  36.4 0.1 collective-permute-start.8
  36.5 1.4 %collective-permute-start.7 = (bf16[64,256]{1,0:T(8,128)(2,1)S(1)}, bf16[64,256]{1,0:T(8,128)(2,1)S(1)}, u32[]{:S(2)}, u32[]{:S(2)}) collective-permute-start(bf16[64,256]{1,0:T(8,128)(2,1)S(1)} %copy-done.6), channel_id=1, source_target_pairs={{0,16},{8,24},{16,0},{24,8},{1,17},{9,25},{17,1},{25,9},{2,18},{10... | collective-permute-start | bytes 98312 | tf_op jit(solution)/shard_map/ppermute | solution.py:520
  37.9 0.0 collective-permute-done.8.other_ref
  37.9 1.6 %collective-permute-start.9 = (f32[8,256]{1,0:T(8,128)S(1)}, f32[8,256]{1,0:T(8,128)S(1)}, u32[]{:S(2)}, u32[]{:S(2)}) collective-permute-start(f32[8,256]{1,0:T(8,128)S(1)} %join.4.mine_ref), channel_id=1, source_target_pairs={{0,1},{1,0},{2,3},{3,2},{4,5},{5,4},{6,7},{7,6},{8,9},{9,8},{10,11... | collective-permute-start | bytes 24584 | tf_op jit(solution)/shard_map/ppermute | solution.py:520
  39.5 2.1 %collective-permute-done.9.other_ref = f32[8,256]{1,0:T(8,128)S(1)} collective-permute-done((f32[8,256]{1,0:T(8,128)S(1)}, f32[8,256]{1,0:T(8,128)S(1)}, u32[]{:S(2)}, u32[]{:S(2)}) %collective-permute-start.9) | collective-permute-done | bytes 8224 | tf_op jit(solution)/shard_map/ppermute | solution.py:520
  41.6 1.6 %collective-permute-start.10 = (f32[8,256]{1,0:T(8,128)S(1)}, f32[8,256]{1,0:T(8,128)S(1)}, u32[]{:S(2)}, u32[]{:S(2)}) collective-permute-start(f32[8,256]{1,0:T(8,128)S(1)} %join.5.mine_ref), channel_id=1, source_target_pairs={{0,2},{1,3},{2,0},{3,1},{4,6},{5,7},{6,4},{7,5},{8,10},{9,11},{10,... | collective-permute-start | bytes 24584 | tf_op jit(solution)/shard_map/ppermute | solution.py:520
  43.2 2.1 %collective-permute-done.10.other_ref = f32[8,256]{1,0:T(8,128)S(1)} collective-permute-done((f32[8,256]{1,0:T(8,128)S(1)}, f32[8,256]{1,0:T(8,128)S(1)}, u32[]{:S(2)}, u32[]{:S(2)}) %collective-permute-start.10) | collective-permute-done | bytes 8224 | tf_op jit(solution)/shard_map/ppermute | solution.py:520
  45.3 2.6 %collective-permute-start.11 = (f32[8,256]{1,0:T(8,128)S(1)}, f32[8,256]{1,0:T(8,128)S(1)}, u32[]{:S(2)}, u32[]{:S(2)}) collective-permute-start(f32[8,256]{1,0:T(8,128)S(1)} %join.6.mine_ref), channel_id=1, source_target_pairs={{0,4},{1,5},{2,6},{3,7},{4,0},{5,1},{6,2},{7,3},{8,12},{9,13},{10,... | collective-permute-start | bytes 24584 | tf_op jit(solution)/shard_map/ppermute | solution.py:520
  47.9 2.0 %collective-permute-done.11.other_ref = f32[8,256]{1,0:T(8,128)S(1)} collective-permute-done((f32[8,256]{1,0:T(8,128)S(1)}, f32[8,256]{1,0:T(8,128)S(1)}, u32[]{:S(2)}, u32[]{:S(2)}) %collective-permute-start.11) | collective-permute-done | bytes 8224 | tf_op jit(solution)/shard_map/ppermute | solution.py:520
  49.8 0.0 collective-permute-done.7.refs_13_
  49.8 0.0 copy-done.4
  49.9 0.0 copy-done.5
  49.9 3.8 %middle.1 = (bf16[64,256]{1,0:T(8,128)(2,1)}, f32[8,160,256]{2,1,0:T(8,128)S(1)}, bf16[1296,256]{1,0:T(8,128)(2,1)S(1)}, bf16[16,256]{1,0:T(8,128)(2,1)S(1)}) custom-call(s32[3]{0:T(128)S(1)} %pad_add_fusion.1.place_ref, bf16[256,256]{1,0:T(8,128)(2,1)S(1)} %get-tuple-element.41.refs_0_, bf16[256,256]{1,0:T(8,128)(2,1)S(1)} %collective-permute-done.3.refs_1_, ...), custom_call_target="tpu_custom_call" | custom-call | tf_op jit(solution)/shard_map/middle/pallas_call | solution.py:613
  53.7 0.1 collective-permute-start.12
  53.8 2.1 %collective-permute-done.12.got_ref = bf16[1296,256]{1,0:T(8,128)(2,1)S(1)} collective-permute-done((bf16[1296,256]{1,0:T(8,128)(2,1)S(1)}, bf16[1296,256]{1,0:T(8,128)(2,1)S(1)}, u32[]{:S(2)}, u32[]{:S(2)}) %collective-permute-start.12) | collective-permute-done | bytes 663584 | tf_op jit(solution)/shard_map/ppermute | solution.py:520
  55.8 0.7 merge.1
  56.5 1.6 %collective-permute-start.13 = (bf16[656,256]{1,0:T(8,128)(2,1)S(1)}, bf16[656,256]{1,0:T(8,128)(2,1)S(1)}, u32[]{:S(2)}, u32[]{:S(2)}) collective-permute-start(bf16[656,256]{1,0:T(8,128)(2,1)S(1)} %get-tuple-element.60), channel_id=1, source_target_pairs={{0,1},{1,0},{2,3},{3,2},{4,5},{5,4},{6,7},{7,6},{8,10},{9,11},{10,... | collective-permute-start | bytes 1007624 | tf_op jit(solution)/shard_map/ppermute | solution.py:653
  58.1 5.6 %collective-permute-done.13.got_ref = bf16[656,256]{1,0:T(8,128)(2,1)S(1)} collective-permute-done((bf16[656,256]{1,0:T(8,128)(2,1)S(1)}, bf16[656,256]{1,0:T(8,128)(2,1)S(1)}, u32[]{:S(2)}, u32[]{:S(2)}) %collective-permute-start.13) | collective-permute-done | bytes 335904 | tf_op jit(solution)/shard_map/ppermute | solution.py:653
  63.7 0.1 halve.1
  63.8 1.7 %collective-permute-start.14 = (bf16[336,256]{1,0:T(8,128)(2,1)S(1)}, bf16[336,256]{1,0:T(8,128)(2,1)S(1)}, u32[]{:S(2)}, u32[]{:S(2)}) collective-permute-start(bf16[336,256]{1,0:T(8,128)(2,1)S(1)} %get-tuple-element.63), channel_id=1, source_target_pairs={{0,2},{1,3},{2,0},{3,1},{4,6},{5,7},{6,4},{7,5},{8,9},{9,8},{10,11... | collective-permute-start | bytes 516104 | tf_op jit(solution)/shard_map/ppermute | solution.py:653
  65.5 3.8 %collective-permute-done.14.got_ref = bf16[336,256]{1,0:T(8,128)(2,1)S(1)} collective-permute-done((bf16[336,256]{1,0:T(8,128)(2,1)S(1)}, bf16[336,256]{1,0:T(8,128)(2,1)S(1)}, u32[]{:S(2)}, u32[]{:S(2)}) %collective-permute-start.14) | collective-permute-done | bytes 172064 | tf_op jit(solution)/shard_map/ppermute | solution.py:653
  69.3 2.7 %collective-permute-start.15 = (bf16[336,256]{1,0:T(8,128)(2,1)S(1)}, bf16[336,256]{1,0:T(8,128)(2,1)S(1)}, u32[]{:S(2)}, u32[]{:S(2)}) collective-permute-start(bf16[336,256]{1,0:T(8,128)(2,1)S(1)} %get-tuple-element.65.sent_ref), channel_id=1, source_target_pairs={{0,4},{1,5},{2,6},{3,7},{4,0},{5,1},{6,2},{7,3},{8,12},{9,13},{10,... | collective-permute-start | bytes 516104 | tf_op jit(solution)/shard_map/ppermute | solution.py:653
  72.0 0.1 constant_dynamic-slice_fusion.1
  72.1 0.1 reshape.20
  72.1 0.1 reshape.21
  72.2 6.5 %collective-permute-done.15.got_ref = bf16[336,256]{1,0:T(8,128)(2,1)S(1)} collective-permute-done((bf16[336,256]{1,0:T(8,128)(2,1)S(1)}, bf16[336,256]{1,0:T(8,128)(2,1)S(1)}, u32[]{:S(2)}, u32[]{:S(2)}) %collective-permute-start.15) | collective-permute-done | bytes 172064 | tf_op jit(solution)/shard_map/ppermute | solution.py:653
  78.7 0.3 finish.1
  79.0 0.7 collective-permute-start.16
  79.8 3.9 %collective-permute-done.16 = bf16[2,96,256]{2,1,0:T(8,128)(2,1)S(1)} collective-permute-done((bf16[2,96,256]{2,1,0:T(8,128)(2,1)S(1)}, bf16[2,96,256]{2,1,0:T(8,128)(2,1)S(1)}, u32[]{:S(2)}, u32[]{:S(2)}) %collective-permute-start.16) | collective-permute-done | bytes 98336 | tf_op jit(solution)/shard_map/ppermute | solution.py:520
  83.7 1.6 %collective-permute-start.17 = (bf16[4,96,256]{2,1,0:T(8,128)(2,1)S(1)}, bf16[4,96,256]{2,1,0:T(8,128)(2,1)S(1)}, u32[]{:S(2)}, u32[]{:S(2)}) collective-permute-start(bf16[4,96,256]{2,1,0:T(8,128)(2,1)S(1)} %pad_maximum_fusion), channel_id=1, source_target_pairs={{0,1},{1,0},{2,3},{3,2},{4,5},{5,4},{6,7},{7,6},{8,9},{9,8},{10,11... | collective-permute-start | bytes 589832 | tf_op jit(solution)/shard_map/ppermute | solution.py:520
  85.3 4.1 %collective-permute-done.17 = bf16[4,96,256]{2,1,0:T(8,128)(2,1)S(1)} collective-permute-done((bf16[4,96,256]{2,1,0:T(8,128)(2,1)S(1)}, bf16[4,96,256]{2,1,0:T(8,128)(2,1)S(1)}, u32[]{:S(2)}, u32[]{:S(2)}) %collective-permute-start.17) | collective-permute-done | bytes 196640 | tf_op jit(solution)/shard_map/ppermute | solution.py:520
  89.5 0.6 upper.1.mine_ref
  90.0 0.1 collective-permute-start.18
  90.1 1.4 %lower.1 = (f32[256,256]{1,0:T(8,128)}, f32[256,256]{1,0:T(8,128)}) custom-call(s32[3]{0:T(128)S(1)} %pad_add_fusion.1.place_ref, bf16[8,96,256]{2,1,0:T(8,128)(2,1)S(1)} %constant_dynamic-update-slice_fusion.parts_ref), custom_call_target="tpu_custom_call" | custom-call | bytes 786432 | tf_op jit(solution)/shard_map/lower/pallas_call | solution.py:715
  91.5 0.2 collective-permute-done.18.other_ref
  91.7 1.4 %last.1 = (f32[256,256]{1,0:T(8,128)}, f32[256,256]{1,0:T(8,128)}, f32[1,256]{1,0:T(1,128)}, f32[1,256]{1,0:T(1,128)}) custom-call(s32[3]{0:T(128)S(1)} %pad_add_fusion.1.place_ref, f32[272,256]{1,0:T(8,128)S(1)} %upper.1.mine_ref, f32[272,256]{1,0:T(8,128)S(1)} %collective-permute-done.18.other_ref), custom_call_target="tpu_custom_call" | custom-call | tf_op jit(solution)/shard_map/last/pallas_call | solution.py:725
  (21 shorter events, 0.2 us)
Async XLA Ops:
  0.6 11.1 %collective-permute-start = (bf16[4096,256]{1,0:T(8,128)(2,1)}, bf16[4096,256]{1,0:T(8,128)(2,1)S(1)}, u32[]{:S(2)}, u32[]{:S(2)}) collective-permute-start(bf16[4096,256]{1,0:T(8,128)(2,1)} %own_ref.7), channel_id=1, source_target_pairs={{0,8},{8,0},{16,24},{24,16},{1,9},{9,1},{17,25},{25,17},{2,10},{10... | collective-permute-start | bytes 6291464 | tf_op jit(solution)/shard_map/ppermute | solution.py:520
  1.1 10.5 %collective-permute-start.1 = (bf16[256,256]{1,0:T(8,128)(2,1)}, bf16[256,256]{1,0:T(8,128)(2,1)S(1)}, u32[]{:S(2)}, u32[]{:S(2)}) collective-permute-start(bf16[256,256]{1,0:T(8,128)(2,1)} %self_own_ref.7), channel_id=1, source_target_pairs={{0,8},{8,0},{16,24},{24,16},{1,9},{9,1},{17,25},{25,17},{2,10},{10... | collective-permute-start | bytes 393224 | tf_op jit(solution)/shard_map/ppermute | solution.py:520
  1.2 10.5 %collective-permute-start.2 = (bf16[256,256]{1,0:T(8,128)(2,1)}, bf16[256,256]{1,0:T(8,128)(2,1)S(1)}, u32[]{:S(2)}, u32[]{:S(2)}) collective-permute-start(bf16[256,256]{1,0:T(8,128)(2,1)} %neigh_own_ref.7), channel_id=1, source_target_pairs={{0,8},{8,0},{16,24},{24,16},{1,9},{9,1},{17,25},{25,17},{2,10},{10... | collective-permute-start | bytes 393224 | tf_op jit(solution)/shard_map/ppermute | solution.py:520
  2.5 0.9 copy-start.3
  3.4 8.3 %copy-start = (bf16[4096,256]{1,0:T(8,128)(2,1)S(1)}, bf16[4096,256]{1,0:T(8,128)(2,1)}, u32[]{:S(2)}) copy-start(bf16[4096,256]{1,0:T(8,128)(2,1)} %own_ref.7) | copy-start | bytes 6291460
  3.4 8.4 %copy-start.1 = (bf16[256,256]{1,0:T(8,128)(2,1)S(1)}, bf16[256,256]{1,0:T(8,128)(2,1)}, u32[]{:S(2)}) copy-start(bf16[256,256]{1,0:T(8,128)(2,1)} %self_own_ref.7) | copy-start | bytes 393220
  3.4 8.4 %copy-start.2 = (bf16[256,256]{1,0:T(8,128)(2,1)S(1)}, bf16[256,256]{1,0:T(8,128)(2,1)}, u32[]{:S(2)}) copy-start(bf16[256,256]{1,0:T(8,128)(2,1)} %neigh_own_ref.7) | copy-start | bytes 393220
  15.5 20.4 %collective-permute-start.6 = (bf16[384,256]{1,0:T(8,128)(2,1)S(1)}, bf16[384,256]{1,0:T(8,128)(2,1)S(1)}, u32[]{:S(2)}, u32[]{:S(2)}) collective-permute-start(bf16[384,256]{1,0:T(8,128)(2,1)S(1)} %get-tuple-element.44.refs_6_), channel_id=1, source_target_pairs={{0,16},{8,24},{16,0},{24,8},{1,17},{9,25},{17,1},{25,9},{2,18},{10... | collective-permute-start | bytes 589832 | tf_op jit(solution)/shard_map/ppermute | solution.py:520
  21.8 14.1 %collective-permute-start.5 = (bf16[384,256]{1,0:T(8,128)(2,1)S(1)}, bf16[384,256]{1,0:T(8,128)(2,1)S(1)}, u32[]{:S(2)}, u32[]{:S(2)}) collective-permute-start(bf16[384,256]{1,0:T(8,128)(2,1)S(1)} %get-tuple-element.43.refs_4_), channel_id=1, source_target_pairs={{0,16},{8,24},{16,0},{24,8},{1,17},{9,25},{17,1},{25,9},{2,18},{10... | collective-permute-start | bytes 589832 | tf_op jit(solution)/shard_map/ppermute | solution.py:520
  25.6 10.9 %copy-start.6 = (bf16[64,256]{1,0:T(8,128)(2,1)S(1)}, bf16[64,256]{1,0:T(8,128)(2,1)}, u32[]{:S(2)}) copy-start(bf16[64,256]{1,0:T(8,128)(2,1)} %refs_12_.1) | copy-start | bytes 98308
  25.6 24.2 %copy-start.4 = (bf16[256,256]{1,0:T(8,128)(2,1)S(1)}, bf16[256,256]{1,0:T(8,128)(2,1)}, u32[]{:S(2)}) copy-start(bf16[256,256]{1,0:T(8,128)(2,1)} %refs_17_.1) | copy-start | bytes 393220
  25.6 24.2 %copy-start.5 = (bf16[256,256]{1,0:T(8,128)(2,1)S(1)}, bf16[256,256]{1,0:T(8,128)(2,1)}, u32[]{:S(2)}) copy-start(bf16[256,256]{1,0:T(8,128)(2,1)} %refs_18_.1) | copy-start | bytes 393220
  25.6 24.2 %copy-start.7 = (f32[256]{0:T(256)S(1)}, f32[256]{0:T(256)}, u32[]{:S(2)}) copy-start(f32[256]{0:T(256)} %param.17) | copy-start | bytes 3076
  25.6 24.2 %copy-start.8 = (f32[256]{0:T(256)S(1)}, f32[256]{0:T(256)}, u32[]{:S(2)}) copy-start(f32[256]{0:T(256)} %param.18) | copy-start | bytes 3076
  25.6 10.2 %collective-permute-start.4 = (bf16[384,256]{1,0:T(8,128)(2,1)S(1)}, bf16[384,256]{1,0:T(8,128)(2,1)S(1)}, u32[]{:S(2)}, u32[]{:S(2)}) collective-permute-start(bf16[384,256]{1,0:T(8,128)(2,1)S(1)} %get-tuple-element.42.refs_2_), channel_id=1, source_target_pairs={{0,16},{8,24},{16,0},{24,8},{1,17},{9,25},{17,1},{25,9},{2,18},{10... | collective-permute-start | bytes 589832 | tf_op jit(solution)/shard_map/ppermute | solution.py:520
  30.5 5.4 %collective-permute-start.3 = (bf16[256,256]{1,0:T(8,128)(2,1)S(1)}, bf16[256,256]{1,0:T(8,128)(2,1)S(1)}, u32[]{:S(2)}, u32[]{:S(2)}) collective-permute-start(bf16[256,256]{1,0:T(8,128)(2,1)S(1)} %get-tuple-element.41.refs_0_), channel_id=1, source_target_pairs={{0,16},{8,24},{16,0},{24,8},{1,17},{9,25},{17,1},{25,9},{2,18},{10... | collective-permute-start | bytes 393224 | tf_op jit(solution)/shard_map/ppermute | solution.py:520
  36.4 1.5 %collective-permute-start.8 = (f32[8,256]{1,0:T(8,128)S(1)}, f32[8,256]{1,0:T(8,128)S(1)}, u32[]{:S(2)}, u32[]{:S(2)}) collective-permute-start(f32[8,256]{1,0:T(8,128)S(1)} %get-tuple-element.54), channel_id=1, source_target_pairs={{0,8},{8,0},{16,24},{24,16},{1,9},{9,1},{17,25},{25,17},{2,10},{10... | collective-permute-start | bytes 24584 | tf_op jit(solution)/shard_map/ppermute | solution.py:520
  36.5 13.4 %collective-permute-start.7 = (bf16[64,256]{1,0:T(8,128)(2,1)S(1)}, bf16[64,256]{1,0:T(8,128)(2,1)S(1)}, u32[]{:S(2)}, u32[]{:S(2)}) collective-permute-start(bf16[64,256]{1,0:T(8,128)(2,1)S(1)} %copy-done.6), channel_id=1, source_target_pairs={{0,16},{8,24},{16,0},{24,8},{1,17},{9,25},{17,1},{25,9},{2,18},{10... | collective-permute-start | bytes 98312 | tf_op jit(solution)/shard_map/ppermute | solution.py:520
  37.9 3.7 %collective-permute-start.9 = (f32[8,256]{1,0:T(8,128)S(1)}, f32[8,256]{1,0:T(8,128)S(1)}, u32[]{:S(2)}, u32[]{:S(2)}) collective-permute-start(f32[8,256]{1,0:T(8,128)S(1)} %join.4.mine_ref), channel_id=1, source_target_pairs={{0,1},{1,0},{2,3},{3,2},{4,5},{5,4},{6,7},{7,6},{8,9},{9,8},{10,11... | collective-permute-start | bytes 24584 | tf_op jit(solution)/shard_map/ppermute | solution.py:520
  41.6 3.7 %collective-permute-start.10 = (f32[8,256]{1,0:T(8,128)S(1)}, f32[8,256]{1,0:T(8,128)S(1)}, u32[]{:S(2)}, u32[]{:S(2)}) collective-permute-start(f32[8,256]{1,0:T(8,128)S(1)} %join.5.mine_ref), channel_id=1, source_target_pairs={{0,2},{1,3},{2,0},{3,1},{4,6},{5,7},{6,4},{7,5},{8,10},{9,11},{10,... | collective-permute-start | bytes 24584 | tf_op jit(solution)/shard_map/ppermute | solution.py:520
  45.3 4.5 %collective-permute-start.11 = (f32[8,256]{1,0:T(8,128)S(1)}, f32[8,256]{1,0:T(8,128)S(1)}, u32[]{:S(2)}, u32[]{:S(2)}) collective-permute-start(f32[8,256]{1,0:T(8,128)S(1)} %join.6.mine_ref), channel_id=1, source_target_pairs={{0,4},{1,5},{2,6},{3,7},{4,0},{5,1},{6,2},{7,3},{8,12},{9,13},{10,... | collective-permute-start | bytes 24584 | tf_op jit(solution)/shard_map/ppermute | solution.py:520
  53.7 2.2 %collective-permute-start.12 = (bf16[1296,256]{1,0:T(8,128)(2,1)S(1)}, bf16[1296,256]{1,0:T(8,128)(2,1)S(1)}, u32[]{:S(2)}, u32[]{:S(2)}) collective-permute-start(bf16[1296,256]{1,0:T(8,128)(2,1)S(1)} %get-tuple-element.57), channel_id=1, source_target_pairs={{0,8},{8,0},{16,24},{24,16},{1,9},{9,1},{17,25},{25,17},{2,10},{10... | collective-permute-start | bytes 1990664 | tf_op jit(solution)/shard_map/ppermute | solution.py:520
  56.5 7.2 %collective-permute-start.13 = (bf16[656,256]{1,0:T(8,128)(2,1)S(1)}, bf16[656,256]{1,0:T(8,128)(2,1)S(1)}, u32[]{:S(2)}, u32[]{:S(2)}) collective-permute-start(bf16[656,256]{1,0:T(8,128)(2,1)S(1)} %get-tuple-element.60), channel_id=1, source_target_pairs={{0,1},{1,0},{2,3},{3,2},{4,5},{5,4},{6,7},{7,6},{8,10},{9,11},{10,... | collective-permute-start | bytes 1007624 | tf_op jit(solution)/shard_map/ppermute | solution.py:653
  63.8 5.5 %collective-permute-start.14 = (bf16[336,256]{1,0:T(8,128)(2,1)S(1)}, bf16[336,256]{1,0:T(8,128)(2,1)S(1)}, u32[]{:S(2)}, u32[]{:S(2)}) collective-permute-start(bf16[336,256]{1,0:T(8,128)(2,1)S(1)} %get-tuple-element.63), channel_id=1, source_target_pairs={{0,2},{1,3},{2,0},{3,1},{4,6},{5,7},{6,4},{7,5},{8,9},{9,8},{10,11... | collective-permute-start | bytes 516104 | tf_op jit(solution)/shard_map/ppermute | solution.py:653
  69.3 9.4 %collective-permute-start.15 = (bf16[336,256]{1,0:T(8,128)(2,1)S(1)}, bf16[336,256]{1,0:T(8,128)(2,1)S(1)}, u32[]{:S(2)}, u32[]{:S(2)}) collective-permute-start(bf16[336,256]{1,0:T(8,128)(2,1)S(1)} %get-tuple-element.65.sent_ref), channel_id=1, source_target_pairs={{0,4},{1,5},{2,6},{3,7},{4,0},{5,1},{6,2},{7,3},{8,12},{9,13},{10,... | collective-permute-start | bytes 516104 | tf_op jit(solution)/shard_map/ppermute | solution.py:653
  79.0 4.7 %collective-permute-start.16 = (bf16[2,96,256]{2,1,0:T(8,128)(2,1)S(1)}, bf16[2,96,256]{2,1,0:T(8,128)(2,1)S(1)}, u32[]{:S(2)}, u32[]{:S(2)}) collective-permute-start(bf16[2,96,256]{2,1,0:T(8,128)(2,1)S(1)} %get-tuple-element.67), channel_id=1, source_target_pairs={{0,2},{1,3},{2,0},{3,1},{4,6},{5,7},{6,4},{7,5},{8,10},{9,11},{10,... | collective-permute-start | bytes 294920 | tf_op jit(solution)/shard_map/ppermute | solution.py:520
  83.7 5.7 %collective-permute-start.17 = (bf16[4,96,256]{2,1,0:T(8,128)(2,1)S(1)}, bf16[4,96,256]{2,1,0:T(8,128)(2,1)S(1)}, u32[]{:S(2)}, u32[]{:S(2)}) collective-permute-start(bf16[4,96,256]{2,1,0:T(8,128)(2,1)S(1)} %pad_maximum_fusion), channel_id=1, source_target_pairs={{0,1},{1,0},{2,3},{3,2},{4,5},{5,4},{6,7},{7,6},{8,9},{9,8},{10,11... | collective-permute-start | bytes 589832 | tf_op jit(solution)/shard_map/ppermute | solution.py:520
  90.0 1.6 %collective-permute-start.18 = (f32[272,256]{1,0:T(8,128)S(1)}, f32[272,256]{1,0:T(8,128)S(1)}, u32[]{:S(2)}, u32[]{:S(2)}) collective-permute-start(f32[272,256]{1,0:T(8,128)S(1)} %upper.1.mine_ref), channel_id=1, source_target_pairs={{0,8},{8,0},{16,24},{24,16},{1,9},{9,1},{17,25},{25,17},{2,10},{10... | collective-permute-start | bytes 835592 | tf_op jit(solution)/shard_map/ppermute | solution.py:520

commit v6 on v5

--- a/solution.py
+++ b/solution.py
@@ -27,7 +27,11 @@
 
 
 VMEM = pl.BlockSpec(memory_space=pltpu.VMEM)
-SMEM = pl.BlockSpec(memory_space=pltpu.SMEM)
+
+
+def here():
+    feat = lax.axis_index("feat")
+    return lax.shift_right_logical(feat, 1), jnp.bitwise_and(feat, 1), lax.axis_index("batch")
 
 
 def halves(value):
@@ -36,7 +40,6 @@
 
 
 def build_kernel(
-    place_ref,
     own_ref,
     far_ref,
     out_ref,
@@ -45,10 +48,11 @@
     spread,
     own_slot,
 ):
+    place = here()
     groups = LANES // GROUP
     per_slot = own_ref.shape[1] // (2 * LANES)
     step, steps = pl.program_id(0), pl.num_programs(0)
-    first_core = place_ref[1] == 0
+    first_core = place[1] == 0
 
     def mine(ids, p):
         parts = []
@@ -150,13 +154,13 @@
     keep(later_keys, 1 - now)
 
 
-def build_rows(place, own, far, table_rows):
+def build_rows(own, far, table_rows):
     steps = own.shape[0] * own.shape[1] // (2 * LANES)
     groups = LANES // GROUP
     return pl.pallas_call(
         build_kernel,
         grid=(steps,),
-        in_specs=[SMEM, VMEM, VMEM],
+        in_specs=[VMEM, VMEM],
         out_specs=pl.BlockSpec((2 * LANES, table_rows), lambda i: (i, 0)),
         out_shape=jax.ShapeDtypeStruct((steps * 2 * LANES, table_rows), BF),
         scratch_shapes=[
@@ -172,7 +176,7 @@
             transcendentals=0,
         ),
         name="build_rows",
-    )(place, own, far)
+    )(own, far)
 
 
 def pick_kernel(
@@ -320,9 +324,9 @@
     slots,
     row_total,
     batches,
-    place_ref,
     *refs,
 ):
+    place = here()
     pairs, acrosses = refs[: 2 * chunks], refs[2 * chunks : 3 * chunks]
     chips = len(refs) - 3 * chunks - 12
     grad_parts = refs[3 * chunks : 3 * chunks + chips]
@@ -344,7 +348,7 @@
     seeds = own_seeds * chips
     width = acrosses[0].shape[0] // 4
     for mask, part in enumerate(grad_parts):
-        at = pl.multiple_of((place_ref[0] ^ mask) * own_seeds, own_seeds)
+        at = pl.multiple_of((place[0] ^ mask) * own_seeds, own_seeds)
         grad_all[pl.ds(at, own_seeds), :] = part[...].astype(F32)
     fan_one = slots - 1
     mean = stats_ref[0:1, :]
@@ -376,11 +380,11 @@
         both[span, hidden_width:] = normed.astype(BF)
     hidden_mean = (hidden_sum / fan_one).astype(BF)
     embed_all[...] = dot(own_rows, upper_self_ref[...]) + dot(hidden_mean, upper_neigh_ref[...])
-    start = pl.multiple_of(place_ref[0] * own_seeds, own_seeds)
+    start = pl.multiple_of(place[0] * own_seeds, own_seeds)
     embed_ref[...] = embed_all[pl.ds(start, own_seeds), :].astype(BF)
     upper_self_part = dot(own_rows, grad, ((0,), (0,)))
     upper_neigh_part = dot(hidden_mean, grad, ((0,), (0,)))
-    first_core = place_ref[1] == 0
+    first_core = place[1] == 0
     upper_keep = jnp.where(first_core, upper_self_part, upper_neigh_part)
     upper_send = jnp.where(first_core, upper_neigh_part, upper_self_part)
     gain_high, gain_low = halves(jnp.sum(gain_sum, axis=0, keepdims=True))
@@ -423,14 +427,15 @@
 
 
 def merge_kernel(
-    orders, place_ref, keep_ref, got_ref, sums_ref, kept_ref, sent_ref, tail_ref
+    orders, keep_ref, got_ref, sums_ref, kept_ref, sent_ref, tail_ref
 ):
+    place = here()
     batches, rows, _ = keep_ref.shape
     got_sums = got_ref[batches * rows :, :].astype(F32)
     tail = joined_sums(sums_ref[...].astype(F32), got_sums).astype(BF)
     half = batches // 2
     for i in range(batches):
-        d = place_ref[2] ^ jnp.where(place_ref[1] == 0, orders[0][i], orders[1][i])
+        d = place[2] ^ jnp.where(place[1] == 0, orders[0][i], orders[1][i])
         at = pl.multiple_of(d * rows, rows)
         value = keep_ref[d, :, :] + got_ref[pl.ds(at, rows), :].astype(F32)
         if i < half:
@@ -488,27 +493,30 @@
     sums_ref[...] = sums.astype(BF)
 
 
-def upper_kernel(masks, place_ref, parts_ref, sums_ref, upper_ref):
+def upper_kernel(masks, parts_ref, sums_ref, upper_ref):
+    place = here()
     rows = upper_ref.shape[0] - 16
     piece = rows // len(masks)
     for i, mask in enumerate(masks):
-        at = pl.multiple_of((place_ref[2] ^ mask) * piece, piece)
+        at = pl.multiple_of((place[2] ^ mask) * piece, piece)
         upper_ref[pl.ds(at, piece), :] = parts_ref[i, parts_ref.shape[1] - piece :, :].astype(F32)
     upper_ref[rows:, :] = sums_ref[...].astype(F32)
 
 
-def lower_kernel(masks, place_ref, parts_ref, self_ref, neigh_ref):
+def lower_kernel(masks, parts_ref, self_ref, neigh_ref):
+    place = here()
     piece = self_ref.shape[0] // len(masks)
     for i, mask in enumerate(masks):
-        at = pl.ds(pl.multiple_of((place_ref[2] ^ mask) * piece, piece), piece)
+        at = pl.ds(pl.multiple_of((place[2] ^ mask) * piece, piece), piece)
         rows = parts_ref[i, :, :].astype(F32)
         self_ref[at, :] = rows[:piece]
         neigh_ref[at, :] = rows[piece : 2 * piece]
 
 
-def last_kernel(place_ref, mine_ref, other_ref, self_ref, neigh_ref, gain_ref, shift_ref):
+def last_kernel(mine_ref, other_ref, self_ref, neigh_ref, gain_ref, shift_ref):
+    place = here()
     rows = self_ref.shape[0]
-    first_core = place_ref[1] == 0
+    first_core = place[1] == 0
     first = jnp.where(first_core, mine_ref[...], other_ref[...])
     self_ref[...] = first[:rows]
     neigh_ref[...] = jnp.where(first_core, other_ref[:rows, :], mine_ref[:rows, :])
@@ -551,9 +559,8 @@
     peer_neigh = swap(lower_neighbour, "feat", 1)
     grads = [embed_grad] + [swap(embed_grad, "feat", 2 * mask) for mask in range(1, chips)]
 
-    place = jnp.stack([chip, core, batch]).astype(jnp.int32)
     own_ids = jnp.concatenate([seed_ids[None, :], first_hop.T], axis=0)
-    picks = build_rows(place, own_ids, second_hop.transpose(1, 2, 0), table_rows)
+    picks = build_rows(own_ids, second_hop.transpose(1, 2, 0), table_rows)
 
     weights = (lower_self, peer_self, lower_neighbour, peer_neigh)
     per_slot = seeds // LANES
@@ -612,7 +619,7 @@
     ]
     embedding, keep, send, sums = pl.pallas_call(
         functools.partial(middle_kernel, len(CHUNKS), slots, row_total, batches),
-        in_specs=[SMEM] + [VMEM] * len(operands),
+        in_specs=[VMEM] * len(operands),
         out_shape=[
             jax.ShapeDtypeStruct((own_seeds, hidden_width), BF),
             jax.ShapeDtypeStruct((batches, per_group, hidden_width), F32),
@@ -626,7 +633,7 @@
         ],
         compiler_params=params(24),
         name="middle",
-    )(place, *operands)
+    )(*operands)
 
     bits = [1 << i for i in range(batches.bit_length() - 1)]
     rounds = (bits, bits[1::-1] + bits[2:])
@@ -655,11 +662,11 @@
     pieces = batches // 2
     kept, sent, tail = pl.pallas_call(
         functools.partial(merge_kernel, [order_of(masks) for masks in rounds]),
-        in_specs=[SMEM] + [VMEM] * 3,
+        in_specs=[VMEM] * 3,
         out_shape=kept_and_sent(pieces),
         compiler_params=params(16),
         name="merge",
-    )(place, keep, swap(send, "feat", 1), sums)
+    )(keep, swap(send, "feat", 1), sums)
     got = exchange(sent, 0)
     for step in range(1, len(bits) - 1):
         pieces //= 2
@@ -706,29 +713,29 @@
     line = jax.ShapeDtypeStruct((1, hidden_width), F32)
     upper = pl.pallas_call(
         functools.partial(upper_kernel, tuple(masks)),
-        in_specs=[SMEM, VMEM, VMEM],
+        in_specs=[VMEM, VMEM],
         out_shape=jax.ShapeDtypeStruct((hidden_width + 16, hidden_width), F32),
         compiler_params=params(4),
         name="upper",
-    )(place, gathered, sums)
+    )(gathered, sums)
     upper_other = swap(upper, "feat", 1)
     grad_self, grad_neigh = pl.pallas_call(
         functools.partial(lower_kernel, tuple(masks)),
-        in_specs=[SMEM, VMEM],
+        in_specs=[VMEM],
         out_shape=[tall, tall],
         compiler_params=params(4),
         cost_estimate=pl.CostEstimate(
             flops=0, bytes_accessed=12 * width * hidden_width, transcendentals=0
         ),
         name="lower",
-    )(place, gathered)
+    )(gathered)
     grad_upper_self, grad_upper_neigh, grad_gain, grad_shift = pl.pallas_call(
         last_kernel,
-        in_specs=[SMEM, VMEM, VMEM],
+        in_specs=[VMEM, VMEM],
         out_shape=[square, square, line, line],
         compiler_params=params(4),
         name="last",
-    )(place, upper, upper_other)
+    )(upper, upper_other)
     return (
         embedding,
         grad_self,

time: 93.3 us -> 90.6 us (0.971)
  Pallas kernels: 30.9 us -> 27.7 us
    pallas_call x4, Pallas kernels: 11.6 us -> 9.46 us  [the longest x1 7.76 us: build_rows(): pl.pallas_call(build_kernel, grid=(steps,), in_specs=[VMEM, VMEM], out_sp...]
where the time goes in v6:
time: 90.6 us; the launch traced here: 90.4 us
  waiting for transfers between devices  38.5 us (42%)
  Pallas kernels  27.7 us (31%)
  starting transfers between devices  21.3 us (24%)
  local copies, waits for them, and re-layouts  1.23 us (1%)
    ppermute x16, waiting for transfers between devices, swap(): lax.ppermute(value, axis, [(i, i ^ mask) for i in range(lax.axis_size(axi...  22.6 us
    ppermute x3, waiting for transfers between devices, exchange(): return lax.ppermute(value, ('feat', 'batch'), pairs)  15.9 us
    ppermute x16, starting transfers between devices, swap(): lax.ppermute(value, axis, [(i, i ^ mask) for i in range(lax.axis_size(axi...  15.5 us
    pallas_call x4, Pallas kernels, pick_rows(): pl.pallas_call(functools.partial(pick_kernel, first_block, start, blocks,...  13.5 us
    pallas_call x1, Pallas kernels, build_rows(): pl.pallas_call(build_kernel, grid=(steps,), in_specs=[VMEM, VMEM], out_sp...  7.76 us
    ppermute x3, starting transfers between devices, exchange(): return lax.ppermute(value, ('feat', 'batch'), pairs)  5.87 us
    pallas_call x1, Pallas kernels, on_device(): pl.pallas_call(functools.partial(middle_kernel, len(CHUNKS), slots, row_t...  3.67 us
  transfers between devices with their start and end apart: 19, of which 11 were waited for; matrix products, arithmetic and copies ran while one was open for 1% of the time, Pallas kernels for 21%

profile of v6, /device:TPU:0, one launch (start us, length us, event | category | flops | bytes accessed | tf_op | source)
XLA Modules:
  0.0 90.4 jit_solution(10085177833256501938)
XLA Ops:
  0.6 0.5 collective-permute-start
  1.2 0.1 collective-permute-start.1
  1.2 0.4 collective-permute-start.2
  1.7 0.7 pad_add_fusion.own_ref
  2.4 0.9 %copy-done.3 = s32[256,10,15]{0,2,1:T(8,128)S(1)} copy-done((s32[256,10,15]{0,2,1:T(8,128)S(1)}, s32[256,10,15]{0,2,1:T(8,128)}, u32[]{:S(2)}) %copy-start.3) | copy-done | bytes 153624
  3.3 7.8 %build_rows.1.rows_ref = bf16[2816,4096]{1,0:T(8,128)(2,1)S(1)} custom-call(s32[11,256]{1,0:T(8,128)S(1)} %pad_add_fusion.own_ref, s32[10,15,256]{2,1,0:T(8,128)S(1)} %bitcast.7), custom_call_target="tpu_custom_call" | custom-call | flops 2952790016 | bytes 23068672 | tf_op jit(solution)/shard_map/build_rows/pallas_call | solution.py:160
  11.1 0.0 collective-permute-done.1.self_peer_ref
  11.1 0.0 collective-permute-done.2.neigh_peer_ref
  11.1 0.0 collective-permute-done.peer_ref
  11.1 0.0 copy-done
  11.1 0.0 copy-done.1
  11.1 0.0 copy-done.2
  11.1 3.6 %pick_rows.7 = (bf16[1024,384]{1,0:T(8,128)(2,1)S(1)}, bf16[384,256]{1,0:T(8,128)(2,1)S(1)}, f32[8,1024]{1,0:T(8,128)S(1)}) custom-call(bf16[2816,4096]{1,0:T(8,128)(2,1)S(1)} %build_rows.1.rows_ref, bf16[4096,256]{1,0:T(8,128)(2,1)S(1)} %copy-done, bf16[4096,256]{1,0:T(8,128)(2,1)S(1)} %collective-permute-done.peer_ref, bf16[256,256]{1,0:T(8,128)(2,1)S(1)} %copy-done.1, ...), custom_call_target="tpu_custom_call" | custom-call | flops 3221225472 | bytes 7340032 | tf_op jit(solution)/shard_map/pick_rows/pallas_call | solution.py:249
  14.8 2.6 %collective-permute-start.6 = (bf16[384,256]{1,0:T(8,128)(2,1)S(1)}, bf16[384,256]{1,0:T(8,128)(2,1)S(1)}, u32[]{:S(2)}, u32[]{:S(2)}) collective-permute-start(bf16[384,256]{1,0:T(8,128)(2,1)S(1)} %get-tuple-element.44.refs_6_), channel_id=1, source_target_pairs={{0,16},{8,24},{16,0},{24,8},{1,17},{9,25},{17,1},{25,9},{2,18},{10... | collective-permute-start | bytes 589832 | tf_op jit(solution)/shard_map/ppermute | solution.py:528
  17.4 3.6 %pick_rows.6 = (bf16[1024,384]{1,0:T(8,128)(2,1)S(1)}, bf16[384,256]{1,0:T(8,128)(2,1)S(1)}, f32[8,1024]{1,0:T(8,128)S(1)}) custom-call(bf16[2816,4096]{1,0:T(8,128)(2,1)S(1)} %build_rows.1.rows_ref, bf16[4096,256]{1,0:T(8,128)(2,1)S(1)} %copy-done, bf16[4096,256]{1,0:T(8,128)(2,1)S(1)} %collective-permute-done.peer_ref, bf16[256,256]{1,0:T(8,128)(2,1)S(1)} %copy-done.1, ...), custom_call_target="tpu_custom_call" | custom-call | flops 3221225472 | bytes 7340032 | tf_op jit(solution)/shard_map/pick_rows/pallas_call | solution.py:249
  21.0 0.1 collective-permute-start.5
  21.1 3.6 %pick_rows.5 = (bf16[1024,384]{1,0:T(8,128)(2,1)S(1)}, bf16[384,256]{1,0:T(8,128)(2,1)S(1)}, f32[8,1024]{1,0:T(8,128)S(1)}) custom-call(bf16[2816,4096]{1,0:T(8,128)(2,1)S(1)} %build_rows.1.rows_ref, bf16[4096,256]{1,0:T(8,128)(2,1)S(1)} %copy-done, bf16[4096,256]{1,0:T(8,128)(2,1)S(1)} %collective-permute-done.peer_ref, bf16[256,256]{1,0:T(8,128)(2,1)S(1)} %copy-done.1, ...), custom_call_target="tpu_custom_call" | custom-call | flops 3221225472 | bytes 7340032 | tf_op jit(solution)/shard_map/pick_rows/pallas_call | solution.py:249
  24.8 0.0 copy-start.6
  24.8 0.0 copy-start.4
  24.8 0.0 copy-start.5
  24.8 0.0 copy-start.7
  24.8 0.0 copy-start.8
  24.8 2.1 %collective-permute-start.4 = (bf16[384,256]{1,0:T(8,128)(2,1)S(1)}, bf16[384,256]{1,0:T(8,128)(2,1)S(1)}, u32[]{:S(2)}, u32[]{:S(2)}) collective-permute-start(bf16[384,256]{1,0:T(8,128)(2,1)S(1)} %get-tuple-element.42.refs_2_), channel_id=1, source_target_pairs={{0,16},{8,24},{16,0},{24,8},{1,17},{9,25},{17,1},{25,9},{2,18},{10... | collective-permute-start | bytes 589832 | tf_op jit(solution)/shard_map/ppermute | solution.py:528
  26.9 2.7 %pick_rows.4 = (bf16[1024,256]{1,0:T(8,128)(2,1)S(1)}, bf16[256,256]{1,0:T(8,128)(2,1)S(1)}, f32[8,1024]{1,0:T(8,128)S(1)}) custom-call(bf16[2816,4096]{1,0:T(8,128)(2,1)S(1)} %build_rows.1.rows_ref, bf16[4096,256]{1,0:T(8,128)(2,1)S(1)} %copy-done, bf16[4096,256]{1,0:T(8,128)(2,1)S(1)} %collective-permute-done.peer_ref, bf16[256,256]{1,0:T(8,128)(2,1)S(1)} %copy-done.1, ...), custom_call_target="tpu_custom_call" | custom-call | flops 2147483648 | bytes 6291456 | tf_op jit(solution)/shard_map/pick_rows/pallas_call | solution.py:249
  29.5 0.1 collective-permute-start.3
  29.6 5.5 %collective-permute-done.3.refs_1_ = bf16[256,256]{1,0:T(8,128)(2,1)S(1)} collective-permute-done((bf16[256,256]{1,0:T(8,128)(2,1)S(1)}, bf16[256,256]{1,0:T(8,128)(2,1)S(1)}, u32[]{:S(2)}, u32[]{:S(2)}) %collective-permute-start.3) | collective-permute-done | bytes 131104 | tf_op jit(solution)/shard_map/ppermute | solution.py:528
  35.1 0.0 collective-permute-done.6.refs_7_
  35.1 0.0 collective-permute-done.5.refs_5_
  35.1 0.0 collective-permute-done.4.refs_3_
  35.1 0.5 stats.1
  35.6 0.1 collective-permute-start.8
  35.7 0.0 copy-done.6
  35.7 1.4 %collective-permute-start.7 = (bf16[64,256]{1,0:T(8,128)(2,1)S(1)}, bf16[64,256]{1,0:T(8,128)(2,1)S(1)}, u32[]{:S(2)}, u32[]{:S(2)}) collective-permute-start(bf16[64,256]{1,0:T(8,128)(2,1)S(1)} %copy-done.6), channel_id=1, source_target_pairs={{0,16},{8,24},{16,0},{24,8},{1,17},{9,25},{17,1},{25,9},{2,18},{10... | collective-permute-start | bytes 98312 | tf_op jit(solution)/shard_map/ppermute | solution.py:528
  37.0 0.0 collective-permute-done.8.other_ref
  37.0 1.6 %collective-permute-start.9 = (f32[8,256]{1,0:T(8,128)S(1)}, f32[8,256]{1,0:T(8,128)S(1)}, u32[]{:S(2)}, u32[]{:S(2)}) collective-permute-start(f32[8,256]{1,0:T(8,128)S(1)} %join.4.mine_ref), channel_id=1, source_target_pairs={{0,1},{1,0},{2,3},{3,2},{4,5},{5,4},{6,7},{7,6},{8,9},{9,8},{10,11... | collective-permute-start | bytes 24584 | tf_op jit(solution)/shard_map/ppermute | solution.py:528
  38.6 2.1 %collective-permute-done.9.other_ref = f32[8,256]{1,0:T(8,128)S(1)} collective-permute-done((f32[8,256]{1,0:T(8,128)S(1)}, f32[8,256]{1,0:T(8,128)S(1)}, u32[]{:S(2)}, u32[]{:S(2)}) %collective-permute-start.9) | collective-permute-done | bytes 8224 | tf_op jit(solution)/shard_map/ppermute | solution.py:528
  40.8 1.6 %collective-permute-start.10 = (f32[8,256]{1,0:T(8,128)S(1)}, f32[8,256]{1,0:T(8,128)S(1)}, u32[]{:S(2)}, u32[]{:S(2)}) collective-permute-start(f32[8,256]{1,0:T(8,128)S(1)} %join.5.mine_ref), channel_id=1, source_target_pairs={{0,2},{1,3},{2,0},{3,1},{4,6},{5,7},{6,4},{7,5},{8,10},{9,11},{10,... | collective-permute-start | bytes 24584 | tf_op jit(solution)/shard_map/ppermute | solution.py:528
  42.4 2.1 %collective-permute-done.10.other_ref = f32[8,256]{1,0:T(8,128)S(1)} collective-permute-done((f32[8,256]{1,0:T(8,128)S(1)}, f32[8,256]{1,0:T(8,128)S(1)}, u32[]{:S(2)}, u32[]{:S(2)}) %collective-permute-start.10) | collective-permute-done | bytes 8224 | tf_op jit(solution)/shard_map/ppermute | solution.py:528
  44.4 2.6 %collective-permute-start.11 = (f32[8,256]{1,0:T(8,128)S(1)}, f32[8,256]{1,0:T(8,128)S(1)}, u32[]{:S(2)}, u32[]{:S(2)}) collective-permute-start(f32[8,256]{1,0:T(8,128)S(1)} %join.6.mine_ref), channel_id=1, source_target_pairs={{0,4},{1,5},{2,6},{3,7},{4,0},{5,1},{6,2},{7,3},{8,12},{9,13},{10,... | collective-permute-start | bytes 24584 | tf_op jit(solution)/shard_map/ppermute | solution.py:528
  47.0 2.0 %collective-permute-done.11.other_ref = f32[8,256]{1,0:T(8,128)S(1)} collective-permute-done((f32[8,256]{1,0:T(8,128)S(1)}, f32[8,256]{1,0:T(8,128)S(1)}, u32[]{:S(2)}, u32[]{:S(2)}) %collective-permute-start.11) | collective-permute-done | bytes 8224 | tf_op jit(solution)/shard_map/ppermute | solution.py:528
  49.0 0.0 collective-permute-done.7.refs_13_
  49.0 3.7 %middle.1 = (bf16[64,256]{1,0:T(8,128)(2,1)}, f32[8,160,256]{2,1,0:T(8,128)S(1)}, bf16[1296,256]{1,0:T(8,128)(2,1)S(1)}, bf16[16,256]{1,0:T(8,128)(2,1)S(1)}) custom-call(bf16[256,256]{1,0:T(8,128)(2,1)S(1)} %get-tuple-element.41.refs_0_, bf16[256,256]{1,0:T(8,128)(2,1)S(1)} %collective-permute-done.3.refs_1_, ...), custom_call_target="tpu_custom_call" | custom-call | tf_op jit(solution)/shard_map/middle/pallas_call | solution.py:620
  52.7 0.0 collective-permute-start.12
  52.7 2.1 %collective-permute-done.12.got_ref = bf16[1296,256]{1,0:T(8,128)(2,1)S(1)} collective-permute-done((bf16[1296,256]{1,0:T(8,128)(2,1)S(1)}, bf16[1296,256]{1,0:T(8,128)(2,1)S(1)}, u32[]{:S(2)}, u32[]{:S(2)}) %collective-permute-start.12) | collective-permute-done | bytes 663584 | tf_op jit(solution)/shard_map/ppermute | solution.py:528
  54.8 0.1 merge.1
  54.9 1.6 %collective-permute-start.13 = (bf16[656,256]{1,0:T(8,128)(2,1)S(1)}, bf16[656,256]{1,0:T(8,128)(2,1)S(1)}, u32[]{:S(2)}, u32[]{:S(2)}) collective-permute-start(bf16[656,256]{1,0:T(8,128)(2,1)S(1)} %get-tuple-element.60), channel_id=1, source_target_pairs={{0,1},{1,0},{2,3},{3,2},{4,5},{5,4},{6,7},{7,6},{8,10},{9,11},{10,... | collective-permute-start | bytes 1007624 | tf_op jit(solution)/shard_map/ppermute | solution.py:660
  56.5 5.7 %collective-permute-done.13.got_ref = bf16[656,256]{1,0:T(8,128)(2,1)S(1)} collective-permute-done((bf16[656,256]{1,0:T(8,128)(2,1)S(1)}, bf16[656,256]{1,0:T(8,128)(2,1)S(1)}, u32[]{:S(2)}, u32[]{:S(2)}) %collective-permute-start.13) | collective-permute-done | bytes 335904 | tf_op jit(solution)/shard_map/ppermute | solution.py:660
  62.2 0.1 halve.1
  62.2 1.6 %collective-permute-start.14 = (bf16[336,256]{1,0:T(8,128)(2,1)S(1)}, bf16[336,256]{1,0:T(8,128)(2,1)S(1)}, u32[]{:S(2)}, u32[]{:S(2)}) collective-permute-start(bf16[336,256]{1,0:T(8,128)(2,1)S(1)} %get-tuple-element.63), channel_id=1, source_target_pairs={{0,2},{1,3},{2,0},{3,1},{4,6},{5,7},{6,4},{7,5},{8,9},{9,8},{10,11... | collective-permute-start | bytes 516104 | tf_op jit(solution)/shard_map/ppermute | solution.py:660
  63.9 3.8 %collective-permute-done.14.got_ref = bf16[336,256]{1,0:T(8,128)(2,1)S(1)} collective-permute-done((bf16[336,256]{1,0:T(8,128)(2,1)S(1)}, bf16[336,256]{1,0:T(8,128)(2,1)S(1)}, u32[]{:S(2)}, u32[]{:S(2)}) %collective-permute-start.14) | collective-permute-done | bytes 172064 | tf_op jit(solution)/shard_map/ppermute | solution.py:660
  67.8 2.7 %collective-permute-start.15 = (bf16[336,256]{1,0:T(8,128)(2,1)S(1)}, bf16[336,256]{1,0:T(8,128)(2,1)S(1)}, u32[]{:S(2)}, u32[]{:S(2)}) collective-permute-start(bf16[336,256]{1,0:T(8,128)(2,1)S(1)} %get-tuple-element.65.sent_ref), channel_id=1, source_target_pairs={{0,4},{1,5},{2,6},{3,7},{4,0},{5,1},{6,2},{7,3},{8,12},{9,13},{10,... | collective-permute-start | bytes 516104 | tf_op jit(solution)/shard_map/ppermute | solution.py:660
  70.4 0.1 constant_dynamic-slice_fusion.1
  70.5 0.1 reshape.20
  70.6 0.1 reshape.21
  70.7 6.5 %collective-permute-done.15.got_ref = bf16[336,256]{1,0:T(8,128)(2,1)S(1)} collective-permute-done((bf16[336,256]{1,0:T(8,128)(2,1)S(1)}, bf16[336,256]{1,0:T(8,128)(2,1)S(1)}, u32[]{:S(2)}, u32[]{:S(2)}) %collective-permute-start.15) | collective-permute-done | bytes 172064 | tf_op jit(solution)/shard_map/ppermute | solution.py:660
  77.1 0.3 finish.1
  77.4 0.7 collective-permute-start.16
  78.2 3.9 %collective-permute-done.16 = bf16[2,96,256]{2,1,0:T(8,128)(2,1)S(1)} collective-permute-done((bf16[2,96,256]{2,1,0:T(8,128)(2,1)S(1)}, bf16[2,96,256]{2,1,0:T(8,128)(2,1)S(1)}, u32[]{:S(2)}, u32[]{:S(2)}) %collective-permute-start.16) | collective-permute-done | bytes 98336 | tf_op jit(solution)/shard_map/ppermute | solution.py:528
  82.1 1.6 %collective-permute-start.17 = (bf16[4,96,256]{2,1,0:T(8,128)(2,1)S(1)}, bf16[4,96,256]{2,1,0:T(8,128)(2,1)S(1)}, u32[]{:S(2)}, u32[]{:S(2)}) collective-permute-start(bf16[4,96,256]{2,1,0:T(8,128)(2,1)S(1)} %pad_maximum_fusion), channel_id=1, source_target_pairs={{0,1},{1,0},{2,3},{3,2},{4,5},{5,4},{6,7},{7,6},{8,9},{9,8},{10,11... | collective-permute-start | bytes 589832 | tf_op jit(solution)/shard_map/ppermute | solution.py:528
  83.7 4.1 %collective-permute-done.17 = bf16[4,96,256]{2,1,0:T(8,128)(2,1)S(1)} collective-permute-done((bf16[4,96,256]{2,1,0:T(8,128)(2,1)S(1)}, bf16[4,96,256]{2,1,0:T(8,128)(2,1)S(1)}, u32[]{:S(2)}, u32[]{:S(2)}) %collective-permute-start.17) | collective-permute-done | bytes 196640 | tf_op jit(solution)/shard_map/ppermute | solution.py:528
  87.9 0.1 collective-permute-start.18
  88.0 0.8 lower.1
  88.9 0.7 collective-permute-done.18.other_ref
  89.6 0.8 last.1
  (20 shorter events, 0.2 us)
Async XLA Ops:
  0.6 10.5 %collective-permute-start = (bf16[4096,256]{1,0:T(8,128)(2,1)}, bf16[4096,256]{1,0:T(8,128)(2,1)S(1)}, u32[]{:S(2)}, u32[]{:S(2)}) collective-permute-start(bf16[4096,256]{1,0:T(8,128)(2,1)} %own_ref.7), channel_id=1, source_target_pairs={{0,8},{8,0},{16,24},{24,16},{1,9},{9,1},{17,25},{25,17},{2,10},{10... | collective-permute-start | bytes 6291464 | tf_op jit(solution)/shard_map/ppermute | solution.py:528
  1.2 9.9 %collective-permute-start.1 = (bf16[256,256]{1,0:T(8,128)(2,1)}, bf16[256,256]{1,0:T(8,128)(2,1)S(1)}, u32[]{:S(2)}, u32[]{:S(2)}) collective-permute-start(bf16[256,256]{1,0:T(8,128)(2,1)} %self_own_ref.7), channel_id=1, source_target_pairs={{0,8},{8,0},{16,24},{24,16},{1,9},{9,1},{17,25},{25,17},{2,10},{10... | collective-permute-start | bytes 393224 | tf_op jit(solution)/shard_map/ppermute | solution.py:528
  1.2 9.9 %collective-permute-start.2 = (bf16[256,256]{1,0:T(8,128)(2,1)}, bf16[256,256]{1,0:T(8,128)(2,1)S(1)}, u32[]{:S(2)}, u32[]{:S(2)}) collective-permute-start(bf16[256,256]{1,0:T(8,128)(2,1)} %neigh_own_ref.7), channel_id=1, source_target_pairs={{0,8},{8,0},{16,24},{24,16},{1,9},{9,1},{17,25},{25,17},{2,10},{10... | collective-permute-start | bytes 393224 | tf_op jit(solution)/shard_map/ppermute | solution.py:528
  2.4 0.9 %copy-start.3 = (s32[256,10,15]{0,2,1:T(8,128)S(1)}, s32[256,10,15]{0,2,1:T(8,128)}, u32[]{:S(2)}) copy-start(s32[256,10,15]{0,2,1:T(8,128)} %param.14) | copy-start | bytes 460804
  3.3 7.8 %copy-start = (bf16[4096,256]{1,0:T(8,128)(2,1)S(1)}, bf16[4096,256]{1,0:T(8,128)(2,1)}, u32[]{:S(2)}) copy-start(bf16[4096,256]{1,0:T(8,128)(2,1)} %own_ref.7) | copy-start | bytes 6291460
  3.3 7.8 %copy-start.1 = (bf16[256,256]{1,0:T(8,128)(2,1)S(1)}, bf16[256,256]{1,0:T(8,128)(2,1)}, u32[]{:S(2)}) copy-start(bf16[256,256]{1,0:T(8,128)(2,1)} %self_own_ref.7) | copy-start | bytes 393220
  3.3 7.8 %copy-start.2 = (bf16[256,256]{1,0:T(8,128)(2,1)S(1)}, bf16[256,256]{1,0:T(8,128)(2,1)}, u32[]{:S(2)}) copy-start(bf16[256,256]{1,0:T(8,128)(2,1)} %neigh_own_ref.7) | copy-start | bytes 393220
  14.8 20.3 %collective-permute-start.6 = (bf16[384,256]{1,0:T(8,128)(2,1)S(1)}, bf16[384,256]{1,0:T(8,128)(2,1)S(1)}, u32[]{:S(2)}, u32[]{:S(2)}) collective-permute-start(bf16[384,256]{1,0:T(8,128)(2,1)S(1)} %get-tuple-element.44.refs_6_), channel_id=1, source_target_pairs={{0,16},{8,24},{16,0},{24,8},{1,17},{9,25},{17,1},{25,9},{2,18},{10... | collective-permute-start | bytes 589832 | tf_op jit(solution)/shard_map/ppermute | solution.py:528
  21.0 14.1 %collective-permute-start.5 = (bf16[384,256]{1,0:T(8,128)(2,1)S(1)}, bf16[384,256]{1,0:T(8,128)(2,1)S(1)}, u32[]{:S(2)}, u32[]{:S(2)}) collective-permute-start(bf16[384,256]{1,0:T(8,128)(2,1)S(1)} %get-tuple-element.43.refs_4_), channel_id=1, source_target_pairs={{0,16},{8,24},{16,0},{24,8},{1,17},{9,25},{17,1},{25,9},{2,18},{10... | collective-permute-start | bytes 589832 | tf_op jit(solution)/shard_map/ppermute | solution.py:528
  24.8 10.9 %copy-start.6 = (bf16[64,256]{1,0:T(8,128)(2,1)S(1)}, bf16[64,256]{1,0:T(8,128)(2,1)}, u32[]{:S(2)}) copy-start(bf16[64,256]{1,0:T(8,128)(2,1)} %refs_12_.1) | copy-start | bytes 98308
  24.8 24.2 %copy-start.4 = (bf16[256,256]{1,0:T(8,128)(2,1)S(1)}, bf16[256,256]{1,0:T(8,128)(2,1)}, u32[]{:S(2)}) copy-start(bf16[256,256]{1,0:T(8,128)(2,1)} %refs_17_.1) | copy-start | bytes 393220
  24.8 24.2 %copy-start.5 = (bf16[256,256]{1,0:T(8,128)(2,1)S(1)}, bf16[256,256]{1,0:T(8,128)(2,1)}, u32[]{:S(2)}) copy-start(bf16[256,256]{1,0:T(8,128)(2,1)} %refs_18_.1) | copy-start | bytes 393220
  24.8 24.2 %copy-start.7 = (f32[256]{0:T(256)S(1)}, f32[256]{0:T(256)}, u32[]{:S(2)}) copy-start(f32[256]{0:T(256)} %param.17) | copy-start | bytes 3076
  24.8 24.2 %copy-start.8 = (f32[256]{0:T(256)S(1)}, f32[256]{0:T(256)}, u32[]{:S(2)}) copy-start(f32[256]{0:T(256)} %param.18) | copy-start | bytes 3076
  24.8 10.3 %collective-permute-start.4 = (bf16[384,256]{1,0:T(8,128)(2,1)S(1)}, bf16[384,256]{1,0:T(8,128)(2,1)S(1)}, u32[]{:S(2)}, u32[]{:S(2)}) collective-permute-start(bf16[384,256]{1,0:T(8,128)(2,1)S(1)} %get-tuple-element.42.refs_2_), channel_id=1, source_target_pairs={{0,16},{8,24},{16,0},{24,8},{1,17},{9,25},{17,1},{25,9},{2,18},{10... | collective-permute-start | bytes 589832 | tf_op jit(solution)/shard_map/ppermute | solution.py:528
  29.5 5.6 %collective-permute-start.3 = (bf16[256,256]{1,0:T(8,128)(2,1)S(1)}, bf16[256,256]{1,0:T(8,128)(2,1)S(1)}, u32[]{:S(2)}, u32[]{:S(2)}) collective-permute-start(bf16[256,256]{1,0:T(8,128)(2,1)S(1)} %get-tuple-element.41.refs_0_), channel_id=1, source_target_pairs={{0,16},{8,24},{16,0},{24,8},{1,17},{9,25},{17,1},{25,9},{2,18},{10... | collective-permute-start | bytes 393224 | tf_op jit(solution)/shard_map/ppermute | solution.py:528
  35.6 1.4 %collective-permute-start.8 = (f32[8,256]{1,0:T(8,128)S(1)}, f32[8,256]{1,0:T(8,128)S(1)}, u32[]{:S(2)}, u32[]{:S(2)}) collective-permute-start(f32[8,256]{1,0:T(8,128)S(1)} %get-tuple-element.54), channel_id=1, source_target_pairs={{0,8},{8,0},{16,24},{24,16},{1,9},{9,1},{17,25},{25,17},{2,10},{10... | collective-permute-start | bytes 24584 | tf_op jit(solution)/shard_map/ppermute | solution.py:528
  35.7 13.3 %collective-permute-start.7 = (bf16[64,256]{1,0:T(8,128)(2,1)S(1)}, bf16[64,256]{1,0:T(8,128)(2,1)S(1)}, u32[]{:S(2)}, u32[]{:S(2)}) collective-permute-start(bf16[64,256]{1,0:T(8,128)(2,1)S(1)} %copy-done.6), channel_id=1, source_target_pairs={{0,16},{8,24},{16,0},{24,8},{1,17},{9,25},{17,1},{25,9},{2,18},{10... | collective-permute-start | bytes 98312 | tf_op jit(solution)/shard_map/ppermute | solution.py:528
  37.0 3.7 %collective-permute-start.9 = (f32[8,256]{1,0:T(8,128)S(1)}, f32[8,256]{1,0:T(8,128)S(1)}, u32[]{:S(2)}, u32[]{:S(2)}) collective-permute-start(f32[8,256]{1,0:T(8,128)S(1)} %join.4.mine_ref), channel_id=1, source_target_pairs={{0,1},{1,0},{2,3},{3,2},{4,5},{5,4},{6,7},{7,6},{8,9},{9,8},{10,11... | collective-permute-start | bytes 24584 | tf_op jit(solution)/shard_map/ppermute | solution.py:528
  40.8 3.7 %collective-permute-start.10 = (f32[8,256]{1,0:T(8,128)S(1)}, f32[8,256]{1,0:T(8,128)S(1)}, u32[]{:S(2)}, u32[]{:S(2)}) collective-permute-start(f32[8,256]{1,0:T(8,128)S(1)} %join.5.mine_ref), channel_id=1, source_target_pairs={{0,2},{1,3},{2,0},{3,1},{4,6},{5,7},{6,4},{7,5},{8,10},{9,11},{10,... | collective-permute-start | bytes 24584 | tf_op jit(solution)/shard_map/ppermute | solution.py:528
  44.4 4.5 %collective-permute-start.11 = (f32[8,256]{1,0:T(8,128)S(1)}, f32[8,256]{1,0:T(8,128)S(1)}, u32[]{:S(2)}, u32[]{:S(2)}) collective-permute-start(f32[8,256]{1,0:T(8,128)S(1)} %join.6.mine_ref), channel_id=1, source_target_pairs={{0,4},{1,5},{2,6},{3,7},{4,0},{5,1},{6,2},{7,3},{8,12},{9,13},{10,... | collective-permute-start | bytes 24584 | tf_op jit(solution)/shard_map/ppermute | solution.py:528
  52.7 2.1 %collective-permute-start.12 = (bf16[1296,256]{1,0:T(8,128)(2,1)S(1)}, bf16[1296,256]{1,0:T(8,128)(2,1)S(1)}, u32[]{:S(2)}, u32[]{:S(2)}) collective-permute-start(bf16[1296,256]{1,0:T(8,128)(2,1)S(1)} %get-tuple-element.57), channel_id=1, source_target_pairs={{0,8},{8,0},{16,24},{24,16},{1,9},{9,1},{17,25},{25,17},{2,10},{10... | collective-permute-start | bytes 1990664 | tf_op jit(solution)/shard_map/ppermute | solution.py:528
  54.9 7.2 %collective-permute-start.13 = (bf16[656,256]{1,0:T(8,128)(2,1)S(1)}, bf16[656,256]{1,0:T(8,128)(2,1)S(1)}, u32[]{:S(2)}, u32[]{:S(2)}) collective-permute-start(bf16[656,256]{1,0:T(8,128)(2,1)S(1)} %get-tuple-element.60), channel_id=1, source_target_pairs={{0,1},{1,0},{2,3},{3,2},{4,5},{5,4},{6,7},{7,6},{8,10},{9,11},{10,... | collective-permute-start | bytes 1007624 | tf_op jit(solution)/shard_map/ppermute | solution.py:660
  62.2 5.5 %collective-permute-start.14 = (bf16[336,256]{1,0:T(8,128)(2,1)S(1)}, bf16[336,256]{1,0:T(8,128)(2,1)S(1)}, u32[]{:S(2)}, u32[]{:S(2)}) collective-permute-start(bf16[336,256]{1,0:T(8,128)(2,1)S(1)} %get-tuple-element.63), channel_id=1, source_target_pairs={{0,2},{1,3},{2,0},{3,1},{4,6},{5,7},{6,4},{7,5},{8,9},{9,8},{10,11... | collective-permute-start | bytes 516104 | tf_op jit(solution)/shard_map/ppermute | solution.py:660
  67.8 9.4 %collective-permute-start.15 = (bf16[336,256]{1,0:T(8,128)(2,1)S(1)}, bf16[336,256]{1,0:T(8,128)(2,1)S(1)}, u32[]{:S(2)}, u32[]{:S(2)}) collective-permute-start(bf16[336,256]{1,0:T(8,128)(2,1)S(1)} %get-tuple-element.65.sent_ref), channel_id=1, source_target_pairs={{0,4},{1,5},{2,6},{3,7},{4,0},{5,1},{6,2},{7,3},{8,12},{9,13},{10,... | collective-permute-start | bytes 516104 | tf_op jit(solution)/shard_map/ppermute | solution.py:660
  77.4 4.7 %collective-permute-start.16 = (bf16[2,96,256]{2,1,0:T(8,128)(2,1)S(1)}, bf16[2,96,256]{2,1,0:T(8,128)(2,1)S(1)}, u32[]{:S(2)}, u32[]{:S(2)}) collective-permute-start(bf16[2,96,256]{2,1,0:T(8,128)(2,1)S(1)} %get-tuple-element.67), channel_id=1, source_target_pairs={{0,2},{1,3},{2,0},{3,1},{4,6},{5,7},{6,4},{7,5},{8,10},{9,11},{10,... | collective-permute-start | bytes 294920 | tf_op jit(solution)/shard_map/ppermute | solution.py:528
  82.1 5.7 %collective-permute-start.17 = (bf16[4,96,256]{2,1,0:T(8,128)(2,1)S(1)}, bf16[4,96,256]{2,1,0:T(8,128)(2,1)S(1)}, u32[]{:S(2)}, u32[]{:S(2)}) collective-permute-start(bf16[4,96,256]{2,1,0:T(8,128)(2,1)S(1)} %pad_maximum_fusion), channel_id=1, source_target_pairs={{0,1},{1,0},{2,3},{3,2},{4,5},{5,4},{6,7},{7,6},{8,9},{9,8},{10,11... | collective-permute-start | bytes 589832 | tf_op jit(solution)/shard_map/ppermute | solution.py:528
  87.9 1.6 %collective-permute-start.18 = (f32[272,256]{1,0:T(8,128)S(1)}, f32[272,256]{1,0:T(8,128)S(1)}, u32[]{:S(2)}, u32[]{:S(2)}) collective-permute-start(f32[272,256]{1,0:T(8,128)S(1)} %upper.1.mine_ref), channel_id=1, source_target_pairs={{0,8},{8,0},{16,24},{24,16},{1,9},{9,1},{17,25},{25,17},{2,10},{10... | collective-permute-start | bytes 835592 | tf_op jit(solution)/shard_map/ppermute | solution.py:528

commit v7 on v6

--- a/solution.py
+++ b/solution.py
@@ -496,17 +496,19 @@
 def upper_kernel(masks, parts_ref, sums_ref, upper_ref):
     place = here()
     rows = upper_ref.shape[0] - 16
-    piece = rows // len(masks)
-    for i, mask in enumerate(masks):
+    piece = rows // len(masks[0])
+    for i in range(len(masks[0])):
+        mask = jnp.where(place[1] == 0, masks[0][i], masks[1][i])
         at = pl.multiple_of((place[2] ^ mask) * piece, piece)
-        upper_ref[pl.ds(at, piece), :] = parts_ref[i, parts_ref.shape[1] - piece :, :].astype(F32)
-    upper_ref[rows:, :] = sums_ref[...].astype(F32)
+        upper_ref[pl.ds(at, piece), :] = parts_ref[i, parts_ref.shape[1] - piece :, :]
+    upper_ref[rows:, :] = sums_ref[...]
 
 
 def lower_kernel(masks, parts_ref, self_ref, neigh_ref):
     place = here()
-    piece = self_ref.shape[0] // len(masks)
-    for i, mask in enumerate(masks):
+    piece = self_ref.shape[0] // len(masks[0])
+    for i in range(len(masks[0])):
+        mask = jnp.where(place[1] == 0, masks[0][i], masks[1][i])
         at = pl.ds(pl.multiple_of((place[2] ^ mask) * piece, piece), piece)
         rows = parts_ref[i, :, :].astype(F32)
         self_ref[at, :] = rows[:piece]
@@ -517,9 +519,10 @@
     place = here()
     rows = self_ref.shape[0]
     first_core = place[1] == 0
-    first = jnp.where(first_core, mine_ref[...], other_ref[...])
+    mine, other = mine_ref[...].astype(F32), other_ref[...].astype(F32)
+    first = jnp.where(first_core, mine, other)
     self_ref[...] = first[:rows]
-    neigh_ref[...] = jnp.where(first_core, other_ref[:rows, :], mine_ref[:rows, :])
+    neigh_ref[...] = jnp.where(first_core, other[:rows], mine[:rows])
     gain_ref[...] = first[rows : rows + 1] + first[rows + 1 : rows + 2]
     shift_ref[...] = first[rows + 2 : rows + 3] + first[rows + 3 : rows + 4]
 
@@ -702,25 +705,24 @@
         name="finish",
     )(sent, got, tail, stats, gain_row, column)
 
-    gathered, masks = done, [0, batches // 2]
-    mask = batches // 4
-    while mask:
-        gathered = jnp.concatenate([gathered, swap(gathered, "batch", mask)], axis=0)
-        masks += [m ^ mask for m in masks]
-        mask //= 2
+    gathered, masks = done, [[0, batches // 2], [0, batches // 2]]
+    for step in range(len(bits) - 2, -1, -1):
+        other = exchange(gathered, step)
+        gathered = jnp.concatenate([gathered, other], axis=0)
+        masks = [m + [k ^ rounds[c][step] for k in m] for c, m in enumerate(masks)]
     square = jax.ShapeDtypeStruct((hidden_width, hidden_width), F32)
     tall = jax.ShapeDtypeStruct((width, hidden_width), F32)
     line = jax.ShapeDtypeStruct((1, hidden_width), F32)
     upper = pl.pallas_call(
-        functools.partial(upper_kernel, tuple(masks)),
+        functools.partial(upper_kernel, masks),
         in_specs=[VMEM, VMEM],
-        out_shape=jax.ShapeDtypeStruct((hidden_width + 16, hidden_width), F32),
+        out_shape=jax.ShapeDtypeStruct((hidden_width + 16, hidden_width), BF),
         compiler_params=params(4),
         name="upper",
     )(gathered, sums)
     upper_other = swap(upper, "feat", 1)
     grad_self, grad_neigh = pl.pallas_call(
-        functools.partial(lower_kernel, tuple(masks)),
+        functools.partial(lower_kernel, masks),
         in_specs=[VMEM],
         out_shape=[tall, tall],
         compiler_params=params(4),
@@ -747,7 +749,7 @@
     )
 
 
-CHUNKS = (2, 3, 3, 3)
+CHUNKS = (4, 4, 3)
 
 
 def solution(mesh):

time: 90.6 us -> 90.5 us (level)
  waiting for transfers between devices: 38.5 us -> 39.7 us
  Pallas kernels: 27.7 us -> 26.6 us
    ppermute x3 -> x5, waiting for transfers between devices: 15.9 us -> 24 us  [exchange(): return lax.ppermute(value, ('feat', 'batch'), pairs)]
    ppermute x16 -> x13, waiting for transfers between devices: 22.6 us -> 15.7 us  [swap(): lax.ppermute(value, axis, [(i, i ^ mask) for i in range(lax.axis_size(axi...]
    ppermute x16 -> x13, starting transfers between devices: 15.5 us -> 12.8 us  [swap(): lax.ppermute(value, axis, [(i, i ^ mask) for i in range(lax.axis_size(axi...]
    ppermute x3 -> x5, starting transfers between devices: 5.87 us -> 8.18 us  [exchange(): return lax.ppermute(value, ('feat', 'batch'), pairs)]
    pallas_call x4 -> x3, Pallas kernels: 13.5 us -> 13.1 us  [pick_rows(): pl.pallas_call(functools.partial(pick_kernel, first_block, start, blocks,...]
  transfers between devices with their start and end apart: 19 -> 18, of which waited for: 11 -> 12; matrix products, arithmetic and copies ran while one was open for 1% -> 1% of each run, Pallas kernels for 21% -> 19%
where the time goes in v7:
time: 90.5 us; the launch traced here: 90.2 us
  waiting for transfers between devices  39.7 us (44%)
  Pallas kernels  26.6 us (29%)
  starting transfers between devices  21 us (23%)
  local copies, waits for them, and re-layouts  1.23 us (1%)
    ppermute x5, waiting for transfers between devices, exchange(): return lax.ppermute(value, ('feat', 'batch'), pairs)  24 us
    ppermute x13, waiting for transfers between devices, swap(): lax.ppermute(value, axis, [(i, i ^ mask) for i in range(lax.axis_size(axi...  15.7 us
    pallas_call x3, Pallas kernels, pick_rows(): pl.pallas_call(functools.partial(pick_kernel, first_block, start, blocks,...  13.1 us
    ppermute x13, starting transfers between devices, swap(): lax.ppermute(value, axis, [(i, i ^ mask) for i in range(lax.axis_size(axi...  12.8 us
    ppermute x5, starting transfers between devices, exchange(): return lax.ppermute(value, ('feat', 'batch'), pairs)  8.18 us
    pallas_call x1, Pallas kernels, build_rows(): pl.pallas_call(build_kernel, grid=(steps,), in_specs=[VMEM, VMEM], out_sp...  7.76 us
    pallas_call x1, Pallas kernels, on_device(): pl.pallas_call(functools.partial(middle_kernel, len(CHUNKS), slots, row_t...  2.93 us
  transfers between devices with their start and end apart: 18, of which 12 were waited for; matrix products, arithmetic and copies ran while one was open for 1% of the time, Pallas kernels for 19%

profile of v7, /device:TPU:0, one launch (start us, length us, event | category | flops | bytes accessed | tf_op | source)
XLA Modules:
  0.0 90.2 jit_solution(3488708462067791695)
XLA Ops:
  0.6 0.5 collective-permute-start
  1.2 0.1 collective-permute-start.1
  1.2 0.4 collective-permute-start.2
  1.7 0.7 pad_add_fusion.own_ref
  2.4 0.9 %copy-done.3 = s32[256,10,15]{0,2,1:T(8,128)S(1)} copy-done((s32[256,10,15]{0,2,1:T(8,128)S(1)}, s32[256,10,15]{0,2,1:T(8,128)}, u32[]{:S(2)}) %copy-start.3) | copy-done | bytes 153624
  3.3 7.8 %build_rows.1.rows_ref = bf16[2816,4096]{1,0:T(8,128)(2,1)S(1)} custom-call(s32[11,256]{1,0:T(8,128)S(1)} %pad_add_fusion.own_ref, s32[10,15,256]{2,1,0:T(8,128)S(1)} %bitcast.7), custom_call_target="tpu_custom_call" | custom-call | flops 2952790016 | bytes 23068672 | tf_op jit(solution)/shard_map/build_rows/pallas_call | solution.py:160
  11.1 0.0 collective-permute-done.1.self_peer_ref
  11.1 0.0 collective-permute-done.2.neigh_peer_ref
  11.1 0.0 collective-permute-done.peer_ref
  11.1 0.0 copy-done
  11.1 0.0 copy-done.1
  11.1 0.0 copy-done.2
  11.1 4.8 %pick_rows.4 = (bf16[1024,512]{1,0:T(8,128)(2,1)S(1)}, bf16[512,256]{1,0:T(8,128)(2,1)S(1)}, f32[8,1024]{1,0:T(8,128)S(1)}) custom-call(bf16[2816,4096]{1,0:T(8,128)(2,1)S(1)} %build_rows.1.rows_ref, bf16[4096,256]{1,0:T(8,128)(2,1)S(1)} %copy-done, bf16[4096,256]{1,0:T(8,128)(2,1)S(1)} %collective-permute-done.peer_ref, bf16[256,256]{1,0:T(8,128)(2,1)S(1)} %copy-done.1, ...), custom_call_target="tpu_custom_call" | custom-call | flops 4294967296 | bytes 8388608 | tf_op jit(solution)/shard_map/pick_rows/pallas_call | solution.py:249
  15.9 2.6 %collective-permute-start.4 = (bf16[512,256]{1,0:T(8,128)(2,1)S(1)}, bf16[512,256]{1,0:T(8,128)(2,1)S(1)}, u32[]{:S(2)}, u32[]{:S(2)}) collective-permute-start(bf16[512,256]{1,0:T(8,128)(2,1)S(1)} %get-tuple-element.39.refs_2_), channel_id=1, source_target_pairs={{0,16},{8,24},{16,0},{24,8},{1,17},{9,25},{17,1},{25,9},{2,18},{10... | collective-permute-start | bytes 786440 | tf_op jit(solution)/shard_map/ppermute | solution.py:531
  18.5 4.8 %pick_rows.3 = (bf16[1024,512]{1,0:T(8,128)(2,1)S(1)}, bf16[512,256]{1,0:T(8,128)(2,1)S(1)}, f32[8,1024]{1,0:T(8,128)S(1)}) custom-call(bf16[2816,4096]{1,0:T(8,128)(2,1)S(1)} %build_rows.1.rows_ref, bf16[4096,256]{1,0:T(8,128)(2,1)S(1)} %copy-done, bf16[4096,256]{1,0:T(8,128)(2,1)S(1)} %collective-permute-done.peer_ref, bf16[256,256]{1,0:T(8,128)(2,1)S(1)} %copy-done.1, ...), custom_call_target="tpu_custom_call" | custom-call | flops 4294967296 | bytes 8388608 | tf_op jit(solution)/shard_map/pick_rows/pallas_call | solution.py:249
  23.3 0.0 copy-start.6
  23.3 0.0 copy-start.4
  23.3 0.0 copy-start.5
  23.3 0.0 copy-start.7
  23.4 0.0 copy-start.8
  23.4 0.1 collective-permute-start.3
  23.4 3.6 %pick_rows.5 = (bf16[1024,384]{1,0:T(8,128)(2,1)S(1)}, bf16[384,256]{1,0:T(8,128)(2,1)S(1)}, f32[8,1024]{1,0:T(8,128)S(1)}) custom-call(bf16[2816,4096]{1,0:T(8,128)(2,1)S(1)} %build_rows.1.rows_ref, bf16[4096,256]{1,0:T(8,128)(2,1)S(1)} %copy-done, bf16[4096,256]{1,0:T(8,128)(2,1)S(1)} %collective-permute-done.peer_ref, bf16[256,256]{1,0:T(8,128)(2,1)S(1)} %copy-done.1, ...), custom_call_target="tpu_custom_call" | custom-call | flops 3221225472 | bytes 7340032 | tf_op jit(solution)/shard_map/pick_rows/pallas_call | solution.py:249
  27.1 2.1 %collective-permute-start.5 = (bf16[384,256]{1,0:T(8,128)(2,1)S(1)}, bf16[384,256]{1,0:T(8,128)(2,1)S(1)}, u32[]{:S(2)}, u32[]{:S(2)}) collective-permute-start(bf16[384,256]{1,0:T(8,128)(2,1)S(1)} %get-tuple-element.40.refs_4_), channel_id=1, source_target_pairs={{0,16},{8,24},{16,0},{24,8},{1,17},{9,25},{17,1},{25,9},{2,18},{10... | collective-permute-start | bytes 589832 | tf_op jit(solution)/shard_map/ppermute | solution.py:531
  29.2 6.9 %collective-permute-done.5.refs_5_ = bf16[384,256]{1,0:T(8,128)(2,1)S(1)} collective-permute-done((bf16[384,256]{1,0:T(8,128)(2,1)S(1)}, bf16[384,256]{1,0:T(8,128)(2,1)S(1)}, u32[]{:S(2)}, u32[]{:S(2)}) %collective-permute-start.5) | collective-permute-done | bytes 196640 | tf_op jit(solution)/shard_map/ppermute | solution.py:531
  36.0 0.0 collective-permute-done.4.refs_3_
  36.0 0.0 collective-permute-done.3.refs_1_
  36.0 0.5 stats.1
  36.5 0.1 collective-permute-start.7
  36.6 1.1 %collective-permute-start.6 = (bf16[64,256]{1,0:T(8,128)(2,1)S(1)}, bf16[64,256]{1,0:T(8,128)(2,1)S(1)}, u32[]{:S(2)}, u32[]{:S(2)}) collective-permute-start(bf16[64,256]{1,0:T(8,128)(2,1)S(1)} %copy-done.6), channel_id=1, source_target_pairs={{0,16},{8,24},{16,0},{24,8},{1,17},{9,25},{17,1},{25,9},{2,18},{10... | collective-permute-start | bytes 98312 | tf_op jit(solution)/shard_map/ppermute | solution.py:531
  37.7 0.1 collective-permute-done.7.other_ref
  37.8 1.5 %collective-permute-start.8 = (f32[8,256]{1,0:T(8,128)S(1)}, f32[8,256]{1,0:T(8,128)S(1)}, u32[]{:S(2)}, u32[]{:S(2)}) collective-permute-start(f32[8,256]{1,0:T(8,128)S(1)} %join.4.mine_ref), channel_id=1, source_target_pairs={{0,1},{1,0},{2,3},{3,2},{4,5},{5,4},{6,7},{7,6},{8,9},{9,8},{10,11... | collective-permute-start | bytes 24584 | tf_op jit(solution)/shard_map/ppermute | solution.py:531
  39.3 2.1 %collective-permute-done.8.other_ref = f32[8,256]{1,0:T(8,128)S(1)} collective-permute-done((f32[8,256]{1,0:T(8,128)S(1)}, f32[8,256]{1,0:T(8,128)S(1)}, u32[]{:S(2)}, u32[]{:S(2)}) %collective-permute-start.8) | collective-permute-done | bytes 8224 | tf_op jit(solution)/shard_map/ppermute | solution.py:531
  41.5 1.6 %collective-permute-start.9 = (f32[8,256]{1,0:T(8,128)S(1)}, f32[8,256]{1,0:T(8,128)S(1)}, u32[]{:S(2)}, u32[]{:S(2)}) collective-permute-start(f32[8,256]{1,0:T(8,128)S(1)} %join.5.mine_ref), channel_id=1, source_target_pairs={{0,2},{1,3},{2,0},{3,1},{4,6},{5,7},{6,4},{7,5},{8,10},{9,11},{10,... | collective-permute-start | bytes 24584 | tf_op jit(solution)/shard_map/ppermute | solution.py:531
  43.0 2.1 %collective-permute-done.9.other_ref = f32[8,256]{1,0:T(8,128)S(1)} collective-permute-done((f32[8,256]{1,0:T(8,128)S(1)}, f32[8,256]{1,0:T(8,128)S(1)}, u32[]{:S(2)}, u32[]{:S(2)}) %collective-permute-start.9) | collective-permute-done | bytes 8224 | tf_op jit(solution)/shard_map/ppermute | solution.py:531
  45.1 2.6 %collective-permute-start.10 = (f32[8,256]{1,0:T(8,128)S(1)}, f32[8,256]{1,0:T(8,128)S(1)}, u32[]{:S(2)}, u32[]{:S(2)}) collective-permute-start(f32[8,256]{1,0:T(8,128)S(1)} %join.6.mine_ref), channel_id=1, source_target_pairs={{0,4},{1,5},{2,6},{3,7},{4,0},{5,1},{6,2},{7,3},{8,12},{9,13},{10,... | collective-permute-start | bytes 24584 | tf_op jit(solution)/shard_map/ppermute | solution.py:531
  47.7 2.0 %collective-permute-done.10.other_ref = f32[8,256]{1,0:T(8,128)S(1)} collective-permute-done((f32[8,256]{1,0:T(8,128)S(1)}, f32[8,256]{1,0:T(8,128)S(1)}, u32[]{:S(2)}, u32[]{:S(2)}) %collective-permute-start.10) | collective-permute-done | bytes 8224 | tf_op jit(solution)/shard_map/ppermute | solution.py:531
  49.7 0.0 collective-permute-done.6.refs_10_
  49.7 0.0 copy-done.4
  49.7 0.0 copy-done.5
  49.7 0.0 copy-done.7
  49.7 0.0 copy-done.8
  49.7 2.9 %middle.1 = (bf16[64,256]{1,0:T(8,128)(2,1)}, f32[8,160,256]{2,1,0:T(8,128)S(1)}, bf16[1296,256]{1,0:T(8,128)(2,1)S(1)}, bf16[16,256]{1,0:T(8,128)(2,1)S(1)}) custom-call(bf16[512,256]{1,0:T(8,128)(2,1)S(1)} %get-tuple-element.38.refs_0_, bf16[512,256]{1,0:T(8,128)(2,1)S(1)} %collective-permute-done.3.refs_1_, ...), custom_call_target="tpu_custom_call" | custom-call | tf_op jit(solution)/shard_map/middle/pallas_call | solution.py:623
  52.7 0.1 collective-permute-start.11
  52.7 2.1 %collective-permute-done.11.got_ref = bf16[1296,256]{1,0:T(8,128)(2,1)S(1)} collective-permute-done((bf16[1296,256]{1,0:T(8,128)(2,1)S(1)}, bf16[1296,256]{1,0:T(8,128)(2,1)S(1)}, u32[]{:S(2)}, u32[]{:S(2)}) %collective-permute-start.11) | collective-permute-done | bytes 663584 | tf_op jit(solution)/shard_map/ppermute | solution.py:531
  54.8 0.1 merge.1
  55.0 1.6 %collective-permute-start.12 = (bf16[656,256]{1,0:T(8,128)(2,1)S(1)}, bf16[656,256]{1,0:T(8,128)(2,1)S(1)}, u32[]{:S(2)}, u32[]{:S(2)}) collective-permute-start(bf16[656,256]{1,0:T(8,128)(2,1)S(1)} %get-tuple-element.54), channel_id=1, source_target_pairs={{0,1},{1,0},{2,3},{3,2},{4,5},{5,4},{6,7},{7,6},{8,10},{9,11},{10,... | collective-permute-start | bytes 1007624 | tf_op jit(solution)/shard_map/ppermute | solution.py:663
  56.5 5.7 %collective-permute-done.12.got_ref = bf16[656,256]{1,0:T(8,128)(2,1)S(1)} collective-permute-done((bf16[656,256]{1,0:T(8,128)(2,1)S(1)}, bf16[656,256]{1,0:T(8,128)(2,1)S(1)}, u32[]{:S(2)}, u32[]{:S(2)}) %collective-permute-start.12) | collective-permute-done | bytes 335904 | tf_op jit(solution)/shard_map/ppermute | solution.py:663
  62.2 0.1 halve.1
  62.3 1.6 %collective-permute-start.13 = (bf16[336,256]{1,0:T(8,128)(2,1)S(1)}, bf16[336,256]{1,0:T(8,128)(2,1)S(1)}, u32[]{:S(2)}, u32[]{:S(2)}) collective-permute-start(bf16[336,256]{1,0:T(8,128)(2,1)S(1)} %get-tuple-element.57), channel_id=1, source_target_pairs={{0,2},{1,3},{2,0},{3,1},{4,6},{5,7},{6,4},{7,5},{8,9},{9,8},{10,11... | collective-permute-start | bytes 516104 | tf_op jit(solution)/shard_map/ppermute | solution.py:663
  63.9 3.8 %collective-permute-done.13.got_ref = bf16[336,256]{1,0:T(8,128)(2,1)S(1)} collective-permute-done((bf16[336,256]{1,0:T(8,128)(2,1)S(1)}, bf16[336,256]{1,0:T(8,128)(2,1)S(1)}, u32[]{:S(2)}, u32[]{:S(2)}) %collective-permute-start.13) | collective-permute-done | bytes 172064 | tf_op jit(solution)/shard_map/ppermute | solution.py:663
  67.8 2.7 %collective-permute-start.14 = (bf16[336,256]{1,0:T(8,128)(2,1)S(1)}, bf16[336,256]{1,0:T(8,128)(2,1)S(1)}, u32[]{:S(2)}, u32[]{:S(2)}) collective-permute-start(bf16[336,256]{1,0:T(8,128)(2,1)S(1)} %get-tuple-element.59.sent_ref), channel_id=1, source_target_pairs={{0,4},{1,5},{2,6},{3,7},{4,0},{5,1},{6,2},{7,3},{8,12},{9,13},{10,... | collective-permute-start | bytes 516104 | tf_op jit(solution)/shard_map/ppermute | solution.py:663
  70.4 0.1 constant_dynamic-slice_fusion.1
  70.5 0.1 reshape.20
  70.6 0.1 reshape.21
  70.7 6.5 %collective-permute-done.14.got_ref = bf16[336,256]{1,0:T(8,128)(2,1)S(1)} collective-permute-done((bf16[336,256]{1,0:T(8,128)(2,1)S(1)}, bf16[336,256]{1,0:T(8,128)(2,1)S(1)}, u32[]{:S(2)}, u32[]{:S(2)}) %collective-permute-start.14) | collective-permute-done | bytes 172064 | tf_op jit(solution)/shard_map/ppermute | solution.py:663
  77.1 0.3 finish.1
  77.5 0.7 collective-permute-start.15
  78.2 3.9 %collective-permute-done.15 = bf16[2,96,256]{2,1,0:T(8,128)(2,1)S(1)} collective-permute-done((bf16[2,96,256]{2,1,0:T(8,128)(2,1)S(1)}, bf16[2,96,256]{2,1,0:T(8,128)(2,1)S(1)}, u32[]{:S(2)}, u32[]{:S(2)}) %collective-permute-start.15) | collective-permute-done | bytes 98336 | tf_op jit(solution)/shard_map/ppermute | solution.py:663
  82.2 1.6 %collective-permute-start.16 = (bf16[4,96,256]{2,1,0:T(8,128)(2,1)S(1)}, bf16[4,96,256]{2,1,0:T(8,128)(2,1)S(1)}, u32[]{:S(2)}, u32[]{:S(2)}) collective-permute-start(bf16[4,96,256]{2,1,0:T(8,128)(2,1)S(1)} %pad_maximum_fusion), channel_id=1, source_target_pairs={{0,1},{1,0},{2,3},{3,2},{4,5},{5,4},{6,7},{7,6},{8,10},{9,11},{10,... | collective-permute-start | bytes 589832 | tf_op jit(solution)/shard_map/ppermute | solution.py:663
  83.8 4.1 %collective-permute-done.16 = bf16[4,96,256]{2,1,0:T(8,128)(2,1)S(1)} collective-permute-done((bf16[4,96,256]{2,1,0:T(8,128)(2,1)S(1)}, bf16[4,96,256]{2,1,0:T(8,128)(2,1)S(1)}, u32[]{:S(2)}, u32[]{:S(2)}) %collective-permute-start.16) | collective-permute-done | bytes 196640 | tf_op jit(solution)/shard_map/ppermute | solution.py:663
  87.9 0.1 collective-permute-start.17
  88.0 0.8 lower.1
  88.9 0.5 collective-permute-done.17.other_ref
  89.4 0.8 last.1
  (17 shorter events, 0.2 us)
Async XLA Ops:
  0.6 10.5 %collective-permute-start = (bf16[4096,256]{1,0:T(8,128)(2,1)}, bf16[4096,256]{1,0:T(8,128)(2,1)S(1)}, u32[]{:S(2)}, u32[]{:S(2)}) collective-permute-start(bf16[4096,256]{1,0:T(8,128)(2,1)} %own_ref.5), channel_id=1, source_target_pairs={{0,8},{8,0},{16,24},{24,16},{1,9},{9,1},{17,25},{25,17},{2,10},{10... | collective-permute-start | bytes 6291464 | tf_op jit(solution)/shard_map/ppermute | solution.py:531
  1.2 9.9 %collective-permute-start.1 = (bf16[256,256]{1,0:T(8,128)(2,1)}, bf16[256,256]{1,0:T(8,128)(2,1)S(1)}, u32[]{:S(2)}, u32[]{:S(2)}) collective-permute-start(bf16[256,256]{1,0:T(8,128)(2,1)} %self_own_ref.5), channel_id=1, source_target_pairs={{0,8},{8,0},{16,24},{24,16},{1,9},{9,1},{17,25},{25,17},{2,10},{10... | collective-permute-start | bytes 393224 | tf_op jit(solution)/shard_map/ppermute | solution.py:531
  1.2 9.9 %collective-permute-start.2 = (bf16[256,256]{1,0:T(8,128)(2,1)}, bf16[256,256]{1,0:T(8,128)(2,1)S(1)}, u32[]{:S(2)}, u32[]{:S(2)}) collective-permute-start(bf16[256,256]{1,0:T(8,128)(2,1)} %neigh_own_ref.5), channel_id=1, source_target_pairs={{0,8},{8,0},{16,24},{24,16},{1,9},{9,1},{17,25},{25,17},{2,10},{10... | collective-permute-start | bytes 393224 | tf_op jit(solution)/shard_map/ppermute | solution.py:531
  2.4 0.9 %copy-start.3 = (s32[256,10,15]{0,2,1:T(8,128)S(1)}, s32[256,10,15]{0,2,1:T(8,128)}, u32[]{:S(2)}) copy-start(s32[256,10,15]{0,2,1:T(8,128)} %param.14) | copy-start | bytes 460804
  3.3 7.8 %copy-start = (bf16[4096,256]{1,0:T(8,128)(2,1)S(1)}, bf16[4096,256]{1,0:T(8,128)(2,1)}, u32[]{:S(2)}) copy-start(bf16[4096,256]{1,0:T(8,128)(2,1)} %own_ref.5) | copy-start | bytes 6291460
  3.3 7.8 %copy-start.1 = (bf16[256,256]{1,0:T(8,128)(2,1)S(1)}, bf16[256,256]{1,0:T(8,128)(2,1)}, u32[]{:S(2)}) copy-start(bf16[256,256]{1,0:T(8,128)(2,1)} %self_own_ref.5) | copy-start | bytes 393220
  3.3 7.8 %copy-start.2 = (bf16[256,256]{1,0:T(8,128)(2,1)S(1)}, bf16[256,256]{1,0:T(8,128)(2,1)}, u32[]{:S(2)}) copy-start(bf16[256,256]{1,0:T(8,128)(2,1)} %neigh_own_ref.5) | copy-start | bytes 393220
  15.9 20.1 %collective-permute-start.4 = (bf16[512,256]{1,0:T(8,128)(2,1)S(1)}, bf16[512,256]{1,0:T(8,128)(2,1)S(1)}, u32[]{:S(2)}, u32[]{:S(2)}) collective-permute-start(bf16[512,256]{1,0:T(8,128)(2,1)S(1)} %get-tuple-element.39.refs_2_), channel_id=1, source_target_pairs={{0,16},{8,24},{16,0},{24,8},{1,17},{9,25},{17,1},{25,9},{2,18},{10... | collective-permute-start | bytes 786440 | tf_op jit(solution)/shard_map/ppermute | solution.py:531
  23.3 13.3 %copy-start.6 = (bf16[64,256]{1,0:T(8,128)(2,1)S(1)}, bf16[64,256]{1,0:T(8,128)(2,1)}, u32[]{:S(2)}) copy-start(bf16[64,256]{1,0:T(8,128)(2,1)} %refs_9_.1) | copy-start | bytes 98308
  23.3 26.4 %copy-start.4 = (bf16[256,256]{1,0:T(8,128)(2,1)S(1)}, bf16[256,256]{1,0:T(8,128)(2,1)}, u32[]{:S(2)}) copy-start(bf16[256,256]{1,0:T(8,128)(2,1)} %refs_14_.1) | copy-start | bytes 393220
  23.3 26.4 %copy-start.5 = (bf16[256,256]{1,0:T(8,128)(2,1)S(1)}, bf16[256,256]{1,0:T(8,128)(2,1)}, u32[]{:S(2)}) copy-start(bf16[256,256]{1,0:T(8,128)(2,1)} %refs_15_.1) | copy-start | bytes 393220
  23.3 26.4 %copy-start.7 = (f32[256]{0:T(256)S(1)}, f32[256]{0:T(256)}, u32[]{:S(2)}) copy-start(f32[256]{0:T(256)} %param.17) | copy-start | bytes 3076
  23.4 26.4 %copy-start.8 = (f32[256]{0:T(256)S(1)}, f32[256]{0:T(256)}, u32[]{:S(2)}) copy-start(f32[256]{0:T(256)} %param.18) | copy-start | bytes 3076
  23.4 12.7 %collective-permute-start.3 = (bf16[512,256]{1,0:T(8,128)(2,1)S(1)}, bf16[512,256]{1,0:T(8,128)(2,1)S(1)}, u32[]{:S(2)}, u32[]{:S(2)}) collective-permute-start(bf16[512,256]{1,0:T(8,128)(2,1)S(1)} %get-tuple-element.38.refs_0_), channel_id=1, source_target_pairs={{0,16},{8,24},{16,0},{24,8},{1,17},{9,25},{17,1},{25,9},{2,18},{10... | collective-permute-start | bytes 786440 | tf_op jit(solution)/shard_map/ppermute | solution.py:531
  27.1 8.9 %collective-permute-start.5 = (bf16[384,256]{1,0:T(8,128)(2,1)S(1)}, bf16[384,256]{1,0:T(8,128)(2,1)S(1)}, u32[]{:S(2)}, u32[]{:S(2)}) collective-permute-start(bf16[384,256]{1,0:T(8,128)(2,1)S(1)} %get-tuple-element.40.refs_4_), channel_id=1, source_target_pairs={{0,16},{8,24},{16,0},{24,8},{1,17},{9,25},{17,1},{25,9},{2,18},{10... | collective-permute-start | bytes 589832 | tf_op jit(solution)/shard_map/ppermute | solution.py:531
  36.5 1.2 %collective-permute-start.7 = (f32[8,256]{1,0:T(8,128)S(1)}, f32[8,256]{1,0:T(8,128)S(1)}, u32[]{:S(2)}, u32[]{:S(2)}) collective-permute-start(f32[8,256]{1,0:T(8,128)S(1)} %get-tuple-element.48), channel_id=1, source_target_pairs={{0,8},{8,0},{16,24},{24,16},{1,9},{9,1},{17,25},{25,17},{2,10},{10... | collective-permute-start | bytes 24584 | tf_op jit(solution)/shard_map/ppermute | solution.py:531
  36.6 13.1 %collective-permute-start.6 = (bf16[64,256]{1,0:T(8,128)(2,1)S(1)}, bf16[64,256]{1,0:T(8,128)(2,1)S(1)}, u32[]{:S(2)}, u32[]{:S(2)}) collective-permute-start(bf16[64,256]{1,0:T(8,128)(2,1)S(1)} %copy-done.6), channel_id=1, source_target_pairs={{0,16},{8,24},{16,0},{24,8},{1,17},{9,25},{17,1},{25,9},{2,18},{10... | collective-permute-start | bytes 98312 | tf_op jit(solution)/shard_map/ppermute | solution.py:531
  37.8 3.7 %collective-permute-start.8 = (f32[8,256]{1,0:T(8,128)S(1)}, f32[8,256]{1,0:T(8,128)S(1)}, u32[]{:S(2)}, u32[]{:S(2)}) collective-permute-start(f32[8,256]{1,0:T(8,128)S(1)} %join.4.mine_ref), channel_id=1, source_target_pairs={{0,1},{1,0},{2,3},{3,2},{4,5},{5,4},{6,7},{7,6},{8,9},{9,8},{10,11... | collective-permute-start | bytes 24584 | tf_op jit(solution)/shard_map/ppermute | solution.py:531
  41.5 3.7 %collective-permute-start.9 = (f32[8,256]{1,0:T(8,128)S(1)}, f32[8,256]{1,0:T(8,128)S(1)}, u32[]{:S(2)}, u32[]{:S(2)}) collective-permute-start(f32[8,256]{1,0:T(8,128)S(1)} %join.5.mine_ref), channel_id=1, source_target_pairs={{0,2},{1,3},{2,0},{3,1},{4,6},{5,7},{6,4},{7,5},{8,10},{9,11},{10,... | collective-permute-start | bytes 24584 | tf_op jit(solution)/shard_map/ppermute | solution.py:531
  45.1 4.5 %collective-permute-start.10 = (f32[8,256]{1,0:T(8,128)S(1)}, f32[8,256]{1,0:T(8,128)S(1)}, u32[]{:S(2)}, u32[]{:S(2)}) collective-permute-start(f32[8,256]{1,0:T(8,128)S(1)} %join.6.mine_ref), channel_id=1, source_target_pairs={{0,4},{1,5},{2,6},{3,7},{4,0},{5,1},{6,2},{7,3},{8,12},{9,13},{10,... | collective-permute-start | bytes 24584 | tf_op jit(solution)/shard_map/ppermute | solution.py:531
  52.7 2.2 %collective-permute-start.11 = (bf16[1296,256]{1,0:T(8,128)(2,1)S(1)}, bf16[1296,256]{1,0:T(8,128)(2,1)S(1)}, u32[]{:S(2)}, u32[]{:S(2)}) collective-permute-start(bf16[1296,256]{1,0:T(8,128)(2,1)S(1)} %get-tuple-element.51), channel_id=1, source_target_pairs={{0,8},{8,0},{16,24},{24,16},{1,9},{9,1},{17,25},{25,17},{2,10},{10... | collective-permute-start | bytes 1990664 | tf_op jit(solution)/shard_map/ppermute | solution.py:531
  55.0 7.2 %collective-permute-start.12 = (bf16[656,256]{1,0:T(8,128)(2,1)S(1)}, bf16[656,256]{1,0:T(8,128)(2,1)S(1)}, u32[]{:S(2)}, u32[]{:S(2)}) collective-permute-start(bf16[656,256]{1,0:T(8,128)(2,1)S(1)} %get-tuple-element.54), channel_id=1, source_target_pairs={{0,1},{1,0},{2,3},{3,2},{4,5},{5,4},{6,7},{7,6},{8,10},{9,11},{10,... | collective-permute-start | bytes 1007624 | tf_op jit(solution)/shard_map/ppermute | solution.py:663
  62.3 5.5 %collective-permute-start.13 = (bf16[336,256]{1,0:T(8,128)(2,1)S(1)}, bf16[336,256]{1,0:T(8,128)(2,1)S(1)}, u32[]{:S(2)}, u32[]{:S(2)}) collective-permute-start(bf16[336,256]{1,0:T(8,128)(2,1)S(1)} %get-tuple-element.57), channel_id=1, source_target_pairs={{0,2},{1,3},{2,0},{3,1},{4,6},{5,7},{6,4},{7,5},{8,9},{9,8},{10,11... | collective-permute-start | bytes 516104 | tf_op jit(solution)/shard_map/ppermute | solution.py:663
  67.8 9.4 %collective-permute-start.14 = (bf16[336,256]{1,0:T(8,128)(2,1)S(1)}, bf16[336,256]{1,0:T(8,128)(2,1)S(1)}, u32[]{:S(2)}, u32[]{:S(2)}) collective-permute-start(bf16[336,256]{1,0:T(8,128)(2,1)S(1)} %get-tuple-element.59.sent_ref), channel_id=1, source_target_pairs={{0,4},{1,5},{2,6},{3,7},{4,0},{5,1},{6,2},{7,3},{8,12},{9,13},{10,... | collective-permute-start | bytes 516104 | tf_op jit(solution)/shard_map/ppermute | solution.py:663
  77.5 4.7 %collective-permute-start.15 = (bf16[2,96,256]{2,1,0:T(8,128)(2,1)S(1)}, bf16[2,96,256]{2,1,0:T(8,128)(2,1)S(1)}, u32[]{:S(2)}, u32[]{:S(2)}) collective-permute-start(bf16[2,96,256]{2,1,0:T(8,128)(2,1)S(1)} %get-tuple-element.61), channel_id=1, source_target_pairs={{0,2},{1,3},{2,0},{3,1},{4,6},{5,7},{6,4},{7,5},{8,9},{9,8},{10,11... | collective-permute-start | bytes 294920 | tf_op jit(solution)/shard_map/ppermute | solution.py:663
  82.2 5.7 %collective-permute-start.16 = (bf16[4,96,256]{2,1,0:T(8,128)(2,1)S(1)}, bf16[4,96,256]{2,1,0:T(8,128)(2,1)S(1)}, u32[]{:S(2)}, u32[]{:S(2)}) collective-permute-start(bf16[4,96,256]{2,1,0:T(8,128)(2,1)S(1)} %pad_maximum_fusion), channel_id=1, source_target_pairs={{0,1},{1,0},{2,3},{3,2},{4,5},{5,4},{6,7},{7,6},{8,10},{9,11},{10,... | collective-permute-start | bytes 589832 | tf_op jit(solution)/shard_map/ppermute | solution.py:663
  87.9 1.4 %collective-permute-start.17 = (bf16[272,256]{1,0:T(8,128)(2,1)S(1)}, bf16[272,256]{1,0:T(8,128)(2,1)S(1)}, u32[]{:S(2)}, u32[]{:S(2)}) collective-permute-start(bf16[272,256]{1,0:T(8,128)(2,1)S(1)} %upper.1.mine_ref), channel_id=1, source_target_pairs={{0,8},{8,0},{16,24},{24,16},{1,9},{9,1},{17,25},{25,17},{2,10},{10... | collective-permute-start | bytes 417800 | tf_op jit(solution)/shard_map/ppermute | solution.py:531
